TPU v7x, 128 devices: a whole 4x4x4 slice. The times are simulated.
128 devices in a mesh: ctx: 32 (over x, z_lo, y), head: 4 (over z_hi, core).
Axes of the slice: x: 4, y: 4, z: 4 (z_hi: 2, z_lo: 2; z = z_hi * 2 + z_lo), core: 2. Of those that a mesh axis runs over, the one named last changes fastest.
Arguments:
- block_order: int32 [64], replicated, may hold values from 0 to 63, as said below
- query_latent: bfloat16 [4096, 128, 576], P('ctx', 'head'), may hold values from -12 to 12
- key_latent: bfloat16 [4096, 576], P('ctx'), may hold values from -6 to 6
- normalizer: float32 [4096, 128], P('ctx', 'head'), may hold values from 6 to 9
- indexer_query: bfloat16 [4096, 64, 128], P('ctx', 'head'), may hold values from -8 to 8
- indexer_key: bfloat16 [4096, 128], P('ctx'), may hold values from -4 to 4
- indexer_weight: bfloat16 [4096, 64], P('ctx', 'head'), may hold values from -4 to 4
Outputs:
- query_grad: float32 [4096, 64, 128], P('ctx', 'head')
- key_grad: float32 [4096, 128], P(('ctx', 'head'))
Inputs may be any that keep to these rules, and one draw needn't show every extreme that they name: `block_order`: entries 2 i and 2 i + 1 are the blocks stored on ctx index i; all entries together are each of 0 to 63 once, and the two entries of one index sum to 63.
All inputs are finite; a program needn't handle non-finite values.
Results may differ from a plain program's by a relative error of at most 0.0037.
Values may be sent and summed in bfloat16 or wider, within the bound.
No kernel may reach another device: no remote copies, remote signals or barrier semaphores. Data moves between devices by JAX's collectives and lax.ppermute only.
A program may use at most 128 MiB of HBM per device.

v0:
```python
import math

import jax
import jax.numpy as jnp
from jax import lax
from jax.sharding import PartitionSpec as P

mla_scale = 192.0 ** (-0.5)
loss_scale = 64.0


def gradient(tile_sums, query_pos, key_pos):
    visible = key_pos[None, :] <= query_pos[:, None]
    target_sum = jnp.where(visible, tile_sums[0], 0.0)
    row_total = jnp.sum(target_sum, axis=1, keepdims=True)
    logits = tile_sums[1]
    row_top = jnp.max(jnp.where(visible, logits, -jnp.inf), axis=1, keepdims=True)
    exp_logit = jnp.where(visible, jnp.exp(logits - row_top), 0.0)
    norm_sum = jnp.sum(exp_logit, axis=1, keepdims=True)
    return jnp.where(
        visible, loss_scale * (exp_logit / norm_sum - target_sum / row_total), 0.0
    ).astype(jnp.bfloat16)


def per_device(
    block_order, query_latent, key_latent, normalizer, indexer_query, indexer_key, indexer_weight
):
    query_rows = query_latent.shape[0]
    block_rows = query_rows // 2
    cycle_count = lax.axis_size("ctx")
    group_count = lax.axis_size("head")
    tokens = query_rows * cycle_count
    local_heads = indexer_query.shape[1]
    idx_scale = (local_heads * group_count * indexer_query.shape[2]) ** (-0.5)
    key_pos = (
        block_order[:, None] * block_rows + jnp.arange(block_rows, dtype=jnp.int32)[None, :]
    ).reshape(-1)
    query_pos = lax.dynamic_slice_in_dim(key_pos, lax.axis_index("ctx") * query_rows, query_rows, 0)
    all_latent, all_index = (
        lax.all_gather(key_latent, "ctx", axis=0, tiled=True),
        lax.all_gather(indexer_key, "ctx", axis=0, tiled=True),
    )
    key_block = math.gcd(tokens, 512)
    block_count = tokens // key_block
    weight_float = indexer_weight.astype(jnp.float32)

    def forward(step_index, state):
        tile_sums, positive = state
        offset = step_index * key_block
        latent_block = lax.dynamic_slice_in_dim(all_latent, offset, key_block, 0)
        index_block = lax.dynamic_slice_in_dim(all_index, offset, key_block, 0)
        scores = (
            jnp.einsum(
                "thl,sl->ths", query_latent, latent_block, preferred_element_type=jnp.float32
            )
            * mla_scale
        )
        target_part = jnp.sum(jnp.exp(scores - normalizer[:, :, None]), axis=1)
        idx_dot = jnp.einsum(
            "tjd,sd->tjs", indexer_query, index_block, preferred_element_type=jnp.float32
        )
        logit_part = idx_scale * jnp.sum(
            weight_float[:, :, None] * jnp.maximum(idx_dot, 0.0), axis=1
        )
        tile_sums = lax.dynamic_update_slice_in_dim(
            tile_sums, jnp.stack((target_part, logit_part)), offset, 2
        )
        positive = lax.dynamic_update_slice_in_dim(positive, idx_dot > 0, offset, 2)
        return (tile_sums, positive)

    start_state = (
        jnp.zeros((2, query_rows, tokens), jnp.float32),
        jnp.zeros((query_rows, local_heads, tokens), jnp.bool_),
    )
    tile_sums, positive = lax.fori_loop(0, block_count, forward, start_state)
    whole_sums = lax.psum(tile_sums, "head")
    grad_logit = gradient(whole_sums, query_pos, key_pos)
    weight_scaled = weight_float * idx_scale

    def backward(step_index, state):
        coeff_buffer, query_accum = state
        offset = step_index * key_block
        positive_block = lax.dynamic_slice_in_dim(positive, offset, key_block, 2)
        grad_block = lax.dynamic_slice_in_dim(grad_logit, offset, key_block, 1)
        coeff_block = jnp.where(
            positive_block,
            grad_block.astype(jnp.float32)[:, None, :] * weight_scaled[:, :, None],
            0.0,
        ).astype(jnp.bfloat16)
        index_block = lax.dynamic_slice_in_dim(all_index, offset, key_block, 0)
        query_accum = query_accum + jnp.einsum(
            "tjs,sd->tjd", coeff_block, index_block, preferred_element_type=jnp.float32
        )
        coeff_buffer = lax.dynamic_update_slice_in_dim(coeff_buffer, coeff_block, offset, 2)
        return (coeff_buffer, query_accum)

    back_state = (
        jnp.zeros((query_rows, local_heads, tokens), jnp.bfloat16),
        jnp.zeros(indexer_query.shape, jnp.float32),
    )
    coefficient, query_grad = lax.fori_loop(0, block_count, backward, back_state)
    key_grad = lax.psum_scatter(
        jnp.einsum("tjs,tjd->sd", coefficient, indexer_query, preferred_element_type=jnp.float32),
        ("ctx", "head"),
        scatter_dimension=0,
        tiled=True,
    )
    return (query_grad, key_grad)


def solution(mesh):
    return jax.shard_map(
        per_device,
        mesh=mesh,
        in_specs=(
            P(),
            P("ctx", "head", None),
            P("ctx", None),
            P("ctx", "head"),
            P("ctx", "head", None),
            P("ctx", None),
            P("ctx", "head"),
        ),
        out_specs=(P("ctx", "head", None), P(("ctx", "head"), None)),
        check_vma=False,
    )
```

profile of v0, /device:TPU:0, one launch (start us, length us, event | category | flops | bytes accessed | tf_op | source)
XLA Modules:
  0.0 1250.0 jit_solution(11668386351569774965)
XLA Ops:
  10.6 152.5 %all-gather.5.cloned.1.call-done = bf16[4096,128]{1,0:T(8,128)(2,1)} async-done(((bf16[128,128]{1,0:T(8,128)(2,1)}), bf16[4096,128]{1,0:T(8,128)(2,1)}) %all-gather.5.cloned.1.call-update) | async-done | bytes 1048592 | tf_op jit(solution)/shard_map/all_gather | solution.py:41
  163.1 142.4 %all-gather.3.cloned.1.call-done = bf16[4096,576]{0,1:T(8,128)(2,1)} async-done(((bf16[128,576]{0,1:T(8,128)(2,1)}), bf16[4096,576]{0,1:T(8,128)(2,1)}) %all-gather.3.cloned.1.call-update) | async-done | bytes 4718608 | tf_op jit(solution)/shard_map/all_gather | solution.py:40
  308.0 6.5 broadcast_in_dim.50
  314.4 121.9 %while.31 = (s32[]{:T(128)}, f32[2,128,4096]{2,1,0:T(8,128)}, pred[128,16,4096]{0,2,1:T(32,128)(4,1)}, bf16[4096,576]{0,1:T(8,128)(2,1)}, bf16[128,32,576]{0,2,1...) while((s32[]{:T(128)}, f32[2,128,4096]{2,1,0:T(8,128)}, ...), condition=%wide.region_3.0_spmd, body=%wide.region_0.0_spmd.sunk | while | flops 2694905856 | bytes 19620028 | solution.py:75
  314.4 6.6 exponential_reduce_fusion.2
  325.9 3.8 bitcast_dynamic-update-slice_fusion.2
  329.7 6.6 exponential_reduce_fusion.2
  341.1 3.8 bitcast_dynamic-update-slice_fusion.2
  344.9 6.6 exponential_reduce_fusion.2
  360.1 6.6 exponential_reduce_fusion.2
  371.6 3.8 bitcast_dynamic-update-slice_fusion.2
  375.4 6.6 exponential_reduce_fusion.2
  386.9 3.8 bitcast_dynamic-update-slice_fusion.2
  390.7 6.6 exponential_reduce_fusion.2
  402.1 3.8 bitcast_dynamic-update-slice_fusion.2
  405.9 6.6 exponential_reduce_fusion.2
  417.3 3.8 bitcast_dynamic-update-slice_fusion.2
  421.1 6.6 exponential_reduce_fusion.2
  432.6 3.8 bitcast_dynamic-update-slice_fusion.2
  437.3 92.7 %all-reduce.2.cloned.1.call-done = f32[2,128,4096]{2,1,0:T(8,128)} async-done(((f32[2,128,4096]{2,1,0:T(8,128)}), f32[2,128,4096]{2,1,0:T(8,128)}) %all-reduce.2.cloned.1.call-update) | async-done | bytes 4194320 | tf_op jit(solution)/shard_map/psum | solution.py:76
  536.0 6.0 broadcast_in_dim.47
  542.0 52.6 %while.32 = (s32[]{:T(128)}, bf16[128,16,4096]{2,0,1:T(8,128)(2,1)}, f32[128,16,128]{2,0,1:T(8,128)S(1)}, pred[128,16,4096]{0,2,1:T(32,128)(4,1)}, bf16[128,4096...) while((s32[]{:T(128)}, ...), condition=%wide.region_9.10_spmd.clone, body=%wide.region_8.9_spmd.clone.sunk | while | flops 275316736 | bytes 11550909 | solution.py:101
  594.6 9.6 convolution_bitcast_fusion
  605.8 637.7 %reduce-scatter.2.cloned.1.call-done = f32[32,128]{1,0:T(8,128)} async-done(((f32[4096,128]{1,0:T(8,128)}), f32[32,128]{1,0:T(8,128)}) %reduce-scatter.2.cloned.1.call-update) | async-done | bytes 16400 | tf_op jit(solution)/shard_map/reduce_scatter | solution.py:102
  (112 shorter events, 109.0 us)
Async XLA Ops:
  7.2 155.9 %all-gather.5.cloned.1.call-start = ((), (), s32[]{:S(2)}) async-start(), calls=%async_computation.2 | async-start | bytes 1081344 | tf_op jit(solution)/shard_map/all_gather | solution.py:41
  7.9 297.6 %all-gather.3.cloned.1.call-start = ((), (), s32[]{:S(2)}) async-start(), calls=%async_computation.1 | async-start | bytes 4866048 | tf_op jit(solution)/shard_map/all_gather | solution.py:40
  8.6 521.3 %all-reduce.2.cloned.1.call-start = ((), (), s32[]{:S(2)}) async-start(), calls=%async_computation.3 | async-start | bytes 8388608 | tf_op jit(solution)/shard_map/psum | solution.py:76
  308.0 6.5 copy-start.3
  436.4 0.7 copy-start.4
  436.4 0.9 copy-start.2
  436.4 807.1 %reduce-scatter.2.cloned.1.call-start = ((), (), s32[]{:S(2)}) async-start(), calls=%async_computation.4 | async-start | bytes 2113536 | tf_op jit(solution)/shard_map/reduce_scatter | solution.py:102
  530.0 5.1 copy-start
  542.0 52.6 %copy-start.1 = (bf16[128,16,128]{2,1,0:T(8,128)(2,1)S(1)}, bf16[128,16,128]{2,1,0:T(8,128)(2,1)}, u32[]{:S(2)}) copy-start(bf16[128,16,128]{2,1,0:T(8,128)(2,1)} %param.15) | copy-start | bytes 1572868
Sparse Core Ops, SparseCore 0:
  9.6 153.3 all-gather.4
  164.6 140.8 all-gather.2
  436.5 93.3 all-reduce.1
  604.3 639.1 reduce-scatter.1
where the time goes:
time: 1250 us
  waiting for transfers between devices  1030 us (82%)
  matrix products  107 us (9%)
  other arithmetic  54.6 us (4%)
  local copies, waits for them, and re-layouts  47.1 us (4%)
  between operations  13.8 us (1%)
    reduce_scatter x1, waiting for transfers between devices, per_device(): lax.psum_scatter(jnp.einsum('tjs,tjd->sd', coefficient, indexer_query, pr...  638 us
    all_gather x1, waiting for transfers between devices, per_device(): lax.all_gather(indexer_key, 'ctx', axis=0, tiled=True)  152 us
    all_gather x1, waiting for transfers between devices, per_device(): lax.all_gather(key_latent, 'ctx', axis=0, tiled=True)  142 us
    psum x1, waiting for transfers between devices, per_device(): whole_sums = lax.psum(tile_sums, 'head')  92.7 us
    dot_general x8, matrix products, forward(): jnp.einsum('thl,sl->ths', query_latent, latent_block, preferred_element_t...  53.1 us
    dynamic_update_slice x8, other arithmetic, forward(): positive = lax.dynamic_update_slice_in_dim(positive, idx_dot > 0, offset, 2)  30.2 us
    dot_general x8, matrix products, forward(): jnp.einsum('tjd,sd->tjs', indexer_query, index_block, preferred_element_t...  29.2 us
  transfers between devices with their start and end apart: 4, of which 4 were waited for; matrix products, arithmetic and copies ran while one was open for 0% of the time, Pallas kernels for 0%

commit v1 on v0

v1 whole, which is shorter than its diff:
```python
import functools
import math

import jax
import jax.numpy as jnp
from jax import lax
from jax.experimental import pallas as pl
from jax.experimental.pallas import tpu as pltpu
from jax.sharding import PartitionSpec as P

ALL = ("ctx", "head")
HALF = 64
TILE = 256
PER_TILE = TILE // HALF
TILES = 17
MLA_SCALE = 192.0**-0.5
LOSS_SCALE = 64.0
NT = (((1,), (1,)), ((), ()))
NN = (((1,), (0,)), ((), ()))


def permutation(move):
    pairs = []
    for x in range(4):
        for zl in range(2):
            for y in range(4):
                for zh in range(2):
                    for k in range(2):
                        tx, tz, ty, tk = move(x, 2 * zh + zl, y, k)
                        tx, tz, ty, tk = tx % 4, tz % 4, ty % 4, tk % 2
                        source = (x * 8 + zl * 4 + y) * 4 + zh * 2 + k
                        target = (tx * 8 + (tz % 2) * 4 + ty) * 4 + (tz // 2) * 2 + tk
                        pairs.append((source, target))
    return pairs


def send(value, move):
    return lax.ppermute(value, ALL, permutation(move))


def swap_core(value):
    return send(value, lambda x, z, y, k: (x, z, y, k + 1))


def swap_high(value):
    return send(value, lambda x, z, y, k: (x, z + 2, y, k))


def along(first, shift):
    def move(x, z, y, k):
        if (k == 0) == first:
            return (x, z, y + shift, k)
        return (x + shift, z, y, k)

    return move


def vmem():
    return pl.BlockSpec(memory_space=pltpu.VMEM)


def smem():
    return pl.BlockSpec(memory_space=pltpu.SMEM)


def anywhere():
    return pl.BlockSpec(memory_space=pl.ANY)


def params(mib):
    return pltpu.CompilerParams(vmem_limit_bytes=mib * 1024 * 1024)


def place(meta, step):
    half = (step >= meta[0]).astype(jnp.int32)
    return half, step - half * meta[0]


def target_kernel(meta, loc, q_ref, m0, m1, m2, m3, s0, s1, s2, s3, keep, other, sorted_ref, keys, sems):
    core = meta[1]
    copies = []
    for side, group in enumerate(((m0, m1, m2, m3), (s0, s1, s2, s3))):
        owner = core if side == 0 else 1 - core
        for j, ref in enumerate(group):
            copies.append(
                pltpu.make_async_copy(ref, keys.at[pl.ds(owner * 32 + j * 8, 8)], sems.at[side * 4 + j])
            )
    for copy in copies:
        copy.start()
    for copy in copies:
        copy.wait()

    def sort(p, _):
        sorted_ref[pl.ds(pl.multiple_of(p * HALF, HALF), HALF), :] = keys[loc[p], :, 640:768]
        return 0

    lax.fori_loop(0, 64, sort, 0, unroll=4)
    scale = MLA_SCALE * math.log2(math.e)

    def body(step, _):
        half, ktile = place(meta, step)
        tile = jnp.concatenate(
            [keys[loc[ktile * PER_TILE + u], :, 0:640] for u in range(PER_TILE)], axis=0
        )
        total = jnp.zeros((HALF, TILE), jnp.float32)
        for g in range(8):
            rows = q_ref[pl.ds(pl.multiple_of(half * 2048 + g * 256, 256), 256), :]
            s = lax.dot_general(rows, tile, NT, preferred_element_type=jnp.float32)
            e = jnp.exp2(s * scale)
            total = total + ((e[0:64] + e[64:128]) + (e[128:192] + e[192:256]))
        top, low = total[0:32], total[32:64]
        keep[step] = jnp.where(core == 0, top, low)
        other[step] = jnp.where(core == 0, low, top)
        return 0

    lax.fori_loop(0, TILES, body, 0)


def visible_of(meta, half, ktile):
    rows = lax.broadcasted_iota(jnp.int32, (32, TILE), 0) + meta[1] * 32 + meta[2 + half] * HALF
    cols = lax.broadcasted_iota(jnp.int32, (32, TILE), 1) + ktile * TILE
    return cols <= rows


def logit_kernel(idx_scale, meta, a_ref, b_ref, key_ref, out, wide, top, norm):
    for side, ref in enumerate((a_ref, b_ref)):
        for c in range(2):
            for half in range(2):
                w = ref[c, half, 16].astype(jnp.float32)
                for j in range(16):
                    wide[side, c, half, pl.ds(j * 32, 32)] = jnp.broadcast_to(w[:, j : j + 1], (32, 128))
    top[...] = jnp.full(top.shape, -jnp.inf, jnp.float32)
    norm[...] = jnp.zeros(norm.shape, jnp.float32)

    def first(step, _):
        half, ktile = place(meta, step)
        tile = key_ref[pl.ds(pl.multiple_of(ktile * TILE, TILE), TILE), :]
        total = jnp.zeros((32, TILE), jnp.float32)
        for side, ref in enumerate((a_ref, b_ref)):
            for c in range(2):
                rows = ref[c, half, 0:16].reshape(512, 128)
                d = jnp.maximum(lax.dot_general(rows, tile, NT, preferred_element_type=jnp.float32), 0.0)
                w = wide[side, c, half]
                d = d * jnp.concatenate((w, w), axis=1)
                for j in range(16):
                    total = total + d[j * 32 : (j + 1) * 32]
        logits = jnp.where(visible_of(meta, half, ktile), total * idx_scale, -jnp.inf)
        out[step] = logits
        top[half] = jnp.maximum(top[half], logits)
        return 0

    lax.fori_loop(0, TILES, first, 0)
    for half in range(2):
        top[half] = jnp.broadcast_to(jnp.max(top[half], axis=1, keepdims=True), (32, TILE))

    def second(step, _):
        half, _ktile = place(meta, step)
        e = jnp.exp(out[step] - top[half])
        out[step] = e
        norm[half] = norm[half] + e
        return 0

    lax.fori_loop(0, TILES, second, 0)
    for half in range(2):
        norm[half] = jnp.broadcast_to(1.0 / jnp.sum(norm[half], axis=1, keepdims=True), (32, TILE))

    def third(step, _):
        half, _ktile = place(meta, step)
        out[step] = out[step] * norm[half]
        return 0

    lax.fori_loop(0, TILES, third, 0)


def gradient_kernel(meta, p_ref, a_ref, b_ref, c_ref, out, whole, total):
    total[...] = jnp.zeros(total.shape, jnp.float32)

    def first(step, _):
        half, ktile = place(meta, step)
        t = a_ref[step] + b_ref[step] + c_ref[step].astype(jnp.float32)
        t = jnp.where(visible_of(meta, half, ktile), t, 0.0)
        whole[step] = t
        total[half] = total[half] + t
        return 0

    lax.fori_loop(0, TILES, first, 0)
    for half in range(2):
        total[half] = jnp.broadcast_to(1.0 / jnp.sum(total[half], axis=1, keepdims=True), (32, TILE))

    def second(step, _):
        half, _ktile = place(meta, step)
        out[step] = (LOSS_SCALE * (p_ref[step] - whole[step] * total[half])).astype(jnp.bfloat16)
        return 0

    lax.fori_loop(0, TILES, second, 0)


def backward_kernel(
    idx_scale, meta, stored, g_ref, h_ref, iq_ref, iqt_ref, key_ref, dq, keep, other, wide
):
    core = meta[1]
    for half in range(2):
        w = iq_ref[half, 16].astype(jnp.float32) * idx_scale
        for j in range(16):
            wide[half, pl.ds(j * HALF, HALF)] = jnp.broadcast_to(w[:, j : j + 1], (HALF, 128))
    dq[...] = jnp.zeros(dq.shape, jnp.float32)
    keep[...] = jnp.zeros(keep.shape, jnp.float32)
    other[...] = jnp.zeros(other.shape, jnp.float32)

    def body(step, _):
        half, ktile = place(meta, step)
        tile = key_ref[pl.ds(pl.multiple_of(ktile * TILE, TILE), TILE), :]
        mine, theirs = g_ref[step].astype(jnp.float32), h_ref[step].astype(jnp.float32)
        g = jnp.concatenate(
            (jnp.where(core == 0, mine, theirs), jnp.where(core == 0, theirs, mine)), axis=0
        )
        g = jnp.concatenate((g, g, g, g), axis=0)
        dkt = jnp.zeros((128, TILE), jnp.float32)
        for q in range(4):
            rows = iq_ref[half, pl.ds(q * 4, 4)].reshape(256, 128)
            d = lax.dot_general(rows, tile, NT, preferred_element_type=jnp.float32)
            w = wide[half, pl.ds(q * 256, 256)]
            coefficient = jnp.where(d > 0, g * jnp.concatenate((w, w), axis=1), 0.0).astype(jnp.bfloat16)
            dq[half, pl.ds(q * 256, 256)] = dq[half, pl.ds(q * 256, 256)] + lax.dot_general(
                coefficient, tile, NN, preferred_element_type=jnp.float32
            )
            dkt = dkt + lax.dot_general(
                iqt_ref[half, :, q * 256 : (q + 1) * 256], coefficient, NN, preferred_element_type=jnp.float32
            )
        dk = dkt.T
        for u in range(PER_TILE):
            slot, slot_other = stored[ktile * PER_TILE + u], stored[64 + ktile * PER_TILE + u]
            first, last = dk[u * 64 : u * 64 + 32], dk[u * 64 + 32 : u * 64 + 64]
            keep[slot] = keep[slot] + jnp.where(core == 0, first, last)
            other[slot_other] = other[slot_other] + jnp.where(core == 0, last, first)
        return 0

    lax.fori_loop(0, TILES, body, 0)


def ring_sum(value, route):
    got = [send(value[shift], route(shift)) for shift in (1, 3, 2)]
    return value[0] + got[0] + got[1] + got[2]


def per_device(
    block_order, query_latent, key_latent, normalizer, indexer_query, indexer_key, indexer_weight
):
    f32, bf16 = jnp.float32, jnp.bfloat16
    idx_scale = 8192.0**-0.5
    ctx, head = lax.axis_index("ctx"), lax.axis_index("head")
    x, zl, y = ctx // 8, (ctx // 4) % 2, ctx % 4
    core = head % 2

    ones = (lax.broadcasted_iota(jnp.int32, (128, 64), 1) < 3).astype(bf16)
    packed = jnp.concatenate((key_latent, ones, indexer_key), axis=1)
    own = lax.dynamic_slice_in_dim(packed, core * HALF, HALF, 0)
    beside = send(own, lambda x, z, y, k: (x, z + 1 - 2 * k, y, k))
    pair = jnp.stack((own, beside))
    legs = [pair] + [send(pair, along(True, shift)) for shift in (1, 3, 2)]
    group = jnp.concatenate(legs, axis=0)
    up, down = send(group, along(False, 1)), send(group, along(False, 3))
    far_a = send(up[0:4], along(False, 1))
    far_b = send(down[4:8], along(False, 3))
    far = jnp.concatenate((far_a, far_b), axis=0)
    mine = [group, up, down, far]
    swapped = [swap_core(v) for v in mine]

    index = jnp.arange(64, dtype=jnp.int32)
    bc, bk = index // 2, index % 2
    bx, bz, by = bc // 8, (bc // 4) % 2, bc % 4

    def ring_slot(rel):
        return jnp.where(rel == 0, 0, jnp.where(rel == 3, 1, jnp.where(rel == 1, 2, 3)))

    rx, ry = ring_slot((bx - x) % 4), ring_slot((by - y) % 4)
    rz = (bz != zl).astype(jnp.int32)
    slot = bk * 32 + jnp.where(bk == 0, rx * 8 + ry * 2, ry * 8 + rx * 2) + rz
    hit = (block_order[None, :] == index[:, None]).astype(jnp.int32)
    loc = jnp.sum(hit * slot[None, :], axis=1)
    blocks = lax.dynamic_slice_in_dim(block_order, ctx * 2, 2, 0)
    qx, qy = (bx - x) % 4, (by - y) % 4
    qz = (2 * bk + bz - 2 * (head // 2) - zl) % 4
    row_a, row_b = qy * 16 + qx * 4 + qz, qx * 16 + qy * 4 + qz
    row_a, row_b = jnp.where(core == 0, row_a, row_b), jnp.where(core == 0, row_b, row_a)
    stored = jnp.concatenate((jnp.sum(hit * row_a[None, :], axis=1), jnp.sum(hit * row_b[None, :], axis=1)))
    meta = jnp.concatenate(((blocks[0:1] + PER_TILE) // PER_TILE, core[None], blocks)).astype(jnp.int32)

    lifted = -normalizer * math.sqrt(192.0)
    n1 = lax.reduce_precision(lifted, 8, 7)
    n2 = lax.reduce_precision(lifted - n1, 8, 7)
    n3 = lax.reduce_precision(lifted - n1 - n2, 8, 7)
    columns = jnp.stack((n1, n2, n3), axis=-1).astype(bf16)
    columns = jnp.pad(columns, ((0, 0), (0, 0), (0, 61)))
    query = jnp.concatenate((query_latent, columns), axis=2)
    query = query.reshape(2, HALF, 32, 640).transpose(0, 2, 1, 3).reshape(4096, 640)

    iq = indexer_query.reshape(2, HALF, 16, 128).transpose(0, 2, 1, 3)
    weight = jnp.pad(indexer_weight.reshape(2, 1, HALF, 16), ((0, 0), (0, 0), (0, 0), (0, 112)))
    iqw = jnp.concatenate((iq, weight), axis=1)
    iqt = iq.transpose(0, 3, 1, 2).reshape(2, 128, 1024)
    iq_keep = lax.dynamic_slice_in_dim(iqw, core * 32, 32, 2)
    iq_other = swap_core(lax.dynamic_slice_in_dim(iqw, (1 - core) * 32, 32, 2))
    iq_chip = jnp.stack((iq_keep, iq_other))
    iq_far = swap_high(iq_chip)

    part = jax.ShapeDtypeStruct((TILES, 32, TILE), f32)
    keep, other, sorted_keys = pl.pallas_call(
        target_kernel,
        out_shape=(part, part, jax.ShapeDtypeStruct((4096, 128), bf16)),
        in_specs=[smem(), smem(), vmem()] + [anywhere()] * 8,
        out_specs=(vmem(), vmem(), vmem()),
        scratch_shapes=[pltpu.VMEM((64, HALF, 768), bf16), pltpu.SemaphoreType.DMA((8,))],
        compiler_params=params(40),
        cost_estimate=pl.CostEstimate(flops=12_000_000_000, bytes_accessed=14_000_000, transcendentals=9_000_000),
        name="targets",
    )(meta, loc, query, *mine, *swapped)

    from_core = swap_core(other)
    from_high = swap_high((keep + from_core).astype(bf16))

    prob = pl.pallas_call(
        functools.partial(logit_kernel, idx_scale),
        out_shape=part,
        in_specs=[smem(), vmem(), vmem(), vmem()],
        out_specs=vmem(),
        scratch_shapes=[
            pltpu.VMEM((2, 2, 2, 512, 128), f32),
            pltpu.VMEM((2, 32, TILE), f32),
            pltpu.VMEM((2, 32, TILE), f32),
        ],
        compiler_params=params(24),
        cost_estimate=pl.CostEstimate(flops=5_000_000_000, bytes_accessed=4_000_000, transcendentals=200_000),
        name="logits",
    )(meta, iq_chip, iq_far, sorted_keys)

    grad = pl.pallas_call(
        gradient_kernel,
        out_shape=jax.ShapeDtypeStruct((TILES, 32, TILE), bf16),
        in_specs=[smem()] + [vmem()] * 4,
        out_specs=vmem(),
        scratch_shapes=[pltpu.VMEM((TILES, 32, TILE), f32), pltpu.VMEM((2, 32, TILE), f32)],
        compiler_params=params(16),
        name="gradient",
    )(meta, prob, keep, from_core, from_high)
    grad_other = swap_core(grad)

    shard = jax.ShapeDtypeStruct((64, 32, 128), f32)
    dq, dk_keep, dk_other = pl.pallas_call(
        functools.partial(backward_kernel, idx_scale),
        out_shape=(jax.ShapeDtypeStruct((2, 1024, 128), f32), shard, shard),
        in_specs=[smem(), smem()] + [vmem()] * 5,
        out_specs=(vmem(), vmem(), vmem()),
        scratch_shapes=[pltpu.VMEM((2, 1024, 128), f32)],
        compiler_params=params(24),
        name="backward",
    )(meta, stored, grad, grad_other, iqw, iqt, sorted_keys)

    query_grad = dq.reshape(2, 16, HALF, 128).transpose(0, 2, 1, 3).reshape(128, 16, 128)

    dk = dk_keep + swap_core(dk_other)
    dk = ring_sum(dk.reshape(4, 4, 4, 32, 128), functools.partial(along, True))
    dk = ring_sum(dk, functools.partial(along, False))
    dk = ring_sum(dk, lambda shift: lambda x, z, y, k: (x, z + shift, y, k))
    return query_grad, dk


def solution(mesh):
    return jax.shard_map(
        per_device,
        mesh=mesh,
        in_specs=(
            P(),
            P("ctx", "head", None),
            P("ctx", None),
            P("ctx", "head"),
            P("ctx", "head", None),
            P("ctx", None),
            P("ctx", "head"),
        ),
        out_specs=(P("ctx", "head", None), P(("ctx", "head"), None)),
        check_vma=False,
    )
```

time: 1250 us -> 167 us (0.13)
  waiting for transfers between devices: 1030 us -> 45.8 us
  matrix products: 107 us -> 0 us
  Pallas kernels: 0 us -> 48.1 us
  other arithmetic: 54.6 us -> 7.51 us
  starting transfers between devices: 0.34 us -> 30.8 us
  local copies, waits for them, and re-layouts: 47.1 us -> 33.5 us
  between operations: 13.8 us -> 1.07 us
    reduce_scatter x1 -> x0, waiting for transfers between devices: 638 us -> none  [per_device(): lax.psum_scatter(jnp.einsum('tjs,tjd->sd', coefficient, indexer_query, pr...]
    all_gather x2 -> x0, waiting for transfers between devices: 295 us -> none  [the longest x1 152 us: per_device(): lax.all_gather(indexer_key, 'ctx', axis=0, tiled=True)]
    dot_general x25 -> x0, matrix products: 107 us -> none  [the longest x8 53.1 us: forward(): jnp.einsum('thl,sl->ths', query_latent, latent_block, preferred_element_t...]
    psum x1 -> x0, waiting for transfers between devices: 92.7 us -> none  [per_device(): whole_sums = lax.psum(tile_sums, 'head')]
    pallas_call x0 -> x4, Pallas kernels: none -> 48.1 us  [the longest x1 21 us: per_device(): pl.pallas_call(target_kernel, out_shape=(part, part, jax.ShapeDtypeStruct...]
    dynamic_update_slice x16 -> x0, other arithmetic: 46.9 us -> none  [the longest x8 30.2 us: forward(): positive = lax.dynamic_update_slice_in_dim(positive, idx_dot > 0, offset, 2)]
    ppermute x0 -> x27, waiting for transfers between devices: none -> 45.8 us  [send(): return lax.ppermute(value, ALL, permutation(move))]
    ppermute x0 -> x27, starting transfers between devices: none -> 30.8 us  [send(): return lax.ppermute(value, ALL, permutation(move))]
  transfers between devices with their start and end apart: 4 -> 27, of which waited for: 4 -> 13; matrix products, arithmetic and copies ran while one was open for 0% -> 19% of each run, Pallas kernels for 0% -> 18%
where the time goes in v1:
time: 167 us
  Pallas kernels  48.1 us (29%)
  waiting for transfers between devices  45.8 us (27%)
  local copies, waits for them, and re-layouts  33.5 us (20%)
  starting transfers between devices  30.8 us (18%)
  other arithmetic  7.51 us (4%)
    ppermute x27, waiting for transfers between devices, send(): return lax.ppermute(value, ALL, permutation(move))  45.8 us
    ppermute x27, starting transfers between devices, send(): return lax.ppermute(value, ALL, permutation(move))  30.8 us
    pallas_call x1, Pallas kernels, per_device(): pl.pallas_call(target_kernel, out_shape=(part, part, jax.ShapeDtypeStruct...  21 us
    unnamed x22, local copies, waits for them, and re-layouts  20.7 us
    pallas_call x1, Pallas kernels, per_device(): pl.pallas_call(functools.partial(backward_kernel, idx_scale), out_shape=(...  16.3 us
    pallas_call x1, Pallas kernels, per_device(): pl.pallas_call(functools.partial(logit_kernel, idx_scale), out_shape=part...  9.64 us
    transpose x1, local copies, waits for them, and re-layouts, per_device(): query.reshape(2, HALF, 32, 640).transpose(0, 2, 1, 3).reshape(4096, 640)  4.35 us
    concatenate x1, other arithmetic, per_device(): query = jnp.concatenate((query_latent, columns), axis=2)  3.69 us
  transfers between devices with their start and end apart: 27, of which 13 were waited for; matrix products, arithmetic and copies ran while one was open for 19% of the time, Pallas kernels for 18%

profile of v1, /device:TPU:0, one launch (start us, length us, event | category | flops | bytes accessed | tf_op | source)
XLA Modules:
  0.0 166.7 jit_solution(12928625705248467558)
XLA Ops:
  3.2 2.0 %collective-permute-start.2 = (bf16[64,768]{1,0:T(8,128)(2,1)S(1)}, bf16[64,768]{1,0:T(8,128)(2,1)S(1)}, u32[]{:S(2)}, u32[]{:S(2)}) collective-permute-start(bf16[64,768]{1,0:T(8,128)(2,1)S(1)} %get-tuple-element.18), channel_id=1, source_target_pairs={{0,16},{1,19},{2,18},{3,17},{4,20},{5,23},{6,22},{7,21},{8,24},{9,... | collective-permute-start | bytes 294920 | tf_op jit(solution)/shard_map/ppermute | solution.py:38
  5.2 4.7 %collective-permute-done.2 = bf16[64,768]{1,0:T(8,128)(2,1)S(1)} collective-permute-done((bf16[64,768]{1,0:T(8,128)(2,1)S(1)}, bf16[64,768]{1,0:T(8,128)(2,1)S(1)}, u32[]{:S(2)}, u32[]{:S(2)}) %collective-permute-start.2) | collective-permute-done | bytes 98336 | tf_op jit(solution)/shard_map/ppermute | solution.py:38
  13.2 2.0 %collective-permute-start.5 = (bf16[2,64,768]{2,1,0:T(8,128)(2,1)S(1)}, bf16[2,64,768]{2,1,0:T(8,128)(2,1)S(1)}, u32[]{:S(2)}, u32[]{:S(2)}) collective-permute-start(bf16[2,64,768]{2,1,0:T(8,128)(2,1)S(1)} %pad_maximum_fusion.1), channel_id=1, source_target_pairs={{0,8},{1,65},{2,10},{3,67},{4,12},{5,69},{6,14},{7,71},{8,0},{9,73... | collective-permute-start | bytes 589832 | tf_op jit(solution)/shard_map/ppermute | solution.py:38
  18.3 2.2 %collective-permute-done.5 = bf16[2,64,768]{2,1,0:T(8,128)(2,1)S(1)} collective-permute-done((bf16[2,64,768]{2,1,0:T(8,128)(2,1)S(1)}, bf16[2,64,768]{2,1,0:T(8,128)(2,1)S(1)}, u32[]{:S(2)}, u32[]{:S(2)}) %collective-permute-start.5) | collective-permute-done | bytes 196640 | tf_op jit(solution)/shard_map/ppermute | solution.py:38
  26.4 8.1 %collective-permute-done.6.m1 = bf16[8,64,768]{2,1,0:T(8,128)(2,1)S(1)} collective-permute-done((bf16[8,64,768]{2,1,0:T(8,128)(2,1)}, bf16[8,64,768]{2,1,0:T(8,128)(2,1)S(1)}, u32[]{:S(2)}, u32[]{:S(2)}) %collective-permute-start.6) | collective-permute-done | bytes 786464 | tf_op jit(solution)/shard_map/ppermute | solution.py:38
  36.7 3.0 %collective-permute-start.9 = (bf16[4,64,768]{2,1,0:T(8,128)(2,1)}, bf16[4,64,768]{2,1,0:T(8,128)(2,1)}, u32[]{:S(2)}, u32[]{:S(2)}) collective-permute-start(bf16[4,64,768]{2,1,0:T(8,128)(2,1)} %slice.65), channel_id=1, source_target_pairs={{0,96},{1,13},{2,98},{3,15},{4,100},{5,1},{6,102},{7,3},{8,104},{9... | collective-permute-start | bytes 1179656 | tf_op jit(solution)/shard_map/ppermute | solution.py:38
  39.7 2.4 %copy.44 = bf16[128,32,3]{2,1,0:T(8,128)(2,1)} copy(bf16[128,32,3]{0,1,2:T(8,128)(2,1)S(1)} %pad_maximum_fusion.2) | data formatting | bytes 49152
  42.1 8.9 %copy.37 = bf16[128,32,576]{2,1,0:T(8,128)(2,1)} copy(bf16[128,32,576]{0,2,1:T(8,128)(2,1)} %param.8) | data formatting | bytes 9437184 | tf_op args[1]
  55.0 3.7 %fusion.1 = bf16[128,32,640]{2,1,0:T(8,128)(2,1)S(1)} fusion(bf16[128,32,3]{2,1,0:T(8,128)(2,1)} %copy.44, bf16[128,32,576]{2,1,0:T(8,128)(2,1)} %copy.37), kind=kLoop, calls=%fused_computation.2 | loop fusion | flops 15728640 | bytes 9986048 | tf_op jit(solution)/shard_map/concatenate | solution.py:295
  58.7 4.3 %copy.39 = bf16[2,32,64,640]{3,2,1,0:T(8,128)(2,1)} copy(bf16[2,32,64,640]{3,1,2,0:T(8,128)(2,1)S(1)} %bitcast.65) | data formatting | bytes 10485760 | tf_op jit(solution)/shard_map/transpose | solution.py:296
  63.4 2.5 %copy-done = bf16[2,32,64,640]{3,2,1,0:T(8,128)(2,1)S(1)} copy-done((bf16[2,32,64,640]{3,2,1,0:T(8,128)(2,1)S(1)}, bf16[2,32,64,640]{3,2,1,0:T(8,128)(2,1)}, u32[]{:S(2)}) %copy-start) | copy-done | bytes 5242904
  67.0 21.0 %targets.1 = (f32[17,32,256]{2,1,0:T(8,128)S(1)}, f32[17,32,256]{2,1,0:T(8,128)S(1)}, bf16[4096,128]{1,0:T(8,128)(2,1)S(1)}) custom-call(s32[4]{0:T(128)S(1)} %pad_add_fusion.meta, s32[64]{0:T(128)S(1)} %get-tuple-element.14.loc, bf16[4096,640]{1,0:T(8,128)(2,1)S(1)} %bitcast.63, bf16[8,64,768]{2,1,0:T(8,128)(2,1)} %constant_dynamic-update-slice_fusion.m0, ...), custom_call_target="tpu_custom_call" | custom-call | flops 12000000000 | bytes 14000000 | tf_op jit(solution)/shard_map/targets/pallas_call | solution.py:308
  89.3 1.9 %collective-permute-start.1 = (bf16[2,2,17,32,128]{4,3,2,1,0:T(8,128)(2,1)S(1)}, bf16[2,2,17,32,128]{4,3,2,1,0:T(8,128)(2,1)S(1)}, u32[]{:S(2)}, u32[]{:S(2)}) collective-permute-start(bf16[2,2,17,32,128]{4,3,2,1,0:T(8,128)(2,1)S(1)} %pad_maximum_fusion.a_ref), channel_id=1, source_target_pairs={{0,2},{1,3},{2,0},{3,1},{4,6},{5,7},{6,4},{7,5},{8,10},{9,11},{10,... | collective-permute-start | bytes 1671176 | tf_op jit(solution)/shard_map/ppermute | solution.py:38
  91.3 1.9 %collective-permute-start.15 = (bf16[17,32,256]{2,1,0:T(8,128)(2,1)S(1)}, bf16[17,32,256]{2,1,0:T(8,128)(2,1)S(1)}, u32[]{:S(2)}, u32[]{:S(2)}) collective-permute-start(bf16[17,32,256]{2,1,0:T(8,128)(2,1)S(1)} %add_convert_fusion), channel_id=1, source_target_pairs={{0,2},{1,3},{2,0},{3,1},{4,6},{5,7},{6,4},{7,5},{8,10},{9,11},{10,... | collective-permute-start | bytes 835592 | tf_op jit(solution)/shard_map/ppermute | solution.py:38
  93.3 13.1 %collective-permute-done.1.b_ref = bf16[2,2,17,32,128]{4,3,2,1,0:T(8,128)(2,1)S(1)} collective-permute-done((bf16[2,2,17,32,128]{4,3,2,1,0:T(8,128)(2,1)S(1)}, bf16[2,2,17,32,128]{4,3,2,1,0:T(8,128)(2,1)S(1)}, u32[]{:S(2)}, u32[]{:S(2)}) %collective-permute-start.1) | collective-permute-done | bytes 557088 | tf_op jit(solution)/shard_map/ppermute | solution.py:38
  106.3 9.6 %logits.1.p_ref = f32[17,32,256]{2,1,0:T(8,128)S(1)} custom-call(s32[4]{0:T(128)S(1)} %pad_add_fusion.meta, bf16[2,2,17,32,128]{4,3,2,1,0:T(8,128)(2,1)S(1)} %pad_maximum_fusion.a_ref, bf16[2,2,17,32,128]{4,3,2,1,0:T(8,128)(2,1)S(1)} %collective-permute-done.1.b_ref, bf16[4096,128]{1,0:T(8,128)(2,1)S(1)} %get-tuple-element.8.key_ref), custom_call_target="tpu_custom_call" | custom-call | flops 5000000000 | bytes 4000000 | tf_op jit(solution)/shard_map/logits/pallas_call | solution.py:322
  119.5 16.3 %backward.1 = (f32[2,1024,128]{2,1,0:T(8,128)S(1)}, f32[64,32,128]{2,1,0:T(8,128)S(1)}, f32[64,32,128]{2,1,0:T(8,128)S(1)}) custom-call(s32[4]{0:T(128)S(1)} %pad_add_fusion.meta, s32[128]{0:T(128)S(1)} %pad_add_fusion.1.stored, bf16[17,32,256]{2,1,0:T(8,128)(2,1)S(1)} %gradient.1.g_ref, bf16[17,32,256]{2,1,0:T(8,128)(2,1)S(1)} %collective-permute-done.16.h_ref, ...), custom_call_target="tpu_custom_call" | custom-call | tf_op jit(solution)/shard_map/backward/pallas_call | solution.py:349
  136.4 2.3 %collective-permute-done.17 = f32[64,32,128]{2,1,0:T(8,128)S(1)} collective-permute-done((f32[64,32,128]{2,1,0:T(8,128)S(1)}, f32[64,32,128]{2,1,0:T(8,128)S(1)}, u32[]{:S(2)}, u32[]{:S(2)}) %collective-permute-start.17) | collective-permute-done | bytes 1048608 | tf_op jit(solution)/shard_map/ppermute | solution.py:38
  139.0 2.1 %collective-permute-start.20 = (f32[4,4,32,128]{3,2,1,0:T(8,128)S(1)}, f32[4,4,32,128]{3,2,1,0:T(8,128)S(1)}, u32[]{:S(2)}, u32[]{:S(2)}) collective-permute-start(f32[4,4,32,128]{3,2,1,0:T(8,128)S(1)} %bitcast.76), channel_id=1, source_target_pairs={{0,8},{1,65},{2,10},{3,67},{4,12},{5,69},{6,14},{7,71},{8,0},{9,73... | collective-permute-start | bytes 786440 | tf_op jit(solution)/shard_map/ppermute | solution.py:38
  143.1 3.8 %collective-permute-done.20 = f32[4,4,32,128]{3,2,1,0:T(8,128)S(1)} collective-permute-done((f32[4,4,32,128]{3,2,1,0:T(8,128)S(1)}, f32[4,4,32,128]{3,2,1,0:T(8,128)S(1)}, u32[]{:S(2)}, u32[]{:S(2)}) %collective-permute-start.20) | collective-permute-done | bytes 262176 | tf_op jit(solution)/shard_map/ppermute | solution.py:38
  146.9 2.0 %collective-permute-done.19 = f32[4,4,32,128]{3,2,1,0:T(8,128)S(1)} collective-permute-done((f32[4,4,32,128]{3,2,1,0:T(8,128)S(1)}, f32[4,4,32,128]{3,2,1,0:T(8,128)S(1)}, u32[]{:S(2)}, u32[]{:S(2)}) %collective-permute-start.19) | collective-permute-done | bytes 262176 | tf_op jit(solution)/shard_map/ppermute | solution.py:38
  153.6 2.9 %collective-permute-done.23 = f32[4,32,128]{2,1,0:T(8,128)S(1)} collective-permute-done((f32[4,32,128]{2,1,0:T(8,128)S(1)}, f32[4,32,128]{2,1,0:T(8,128)S(1)}, u32[]{:S(2)}, u32[]{:S(2)}) %collective-permute-start.23) | collective-permute-done | bytes 65568 | tf_op jit(solution)/shard_map/ppermute | solution.py:38
  156.5 2.0 %collective-permute-done.21 = f32[4,32,128]{2,1,0:T(8,128)S(1)} collective-permute-done((f32[4,32,128]{2,1,0:T(8,128)S(1)}, f32[4,32,128]{2,1,0:T(8,128)S(1)}, u32[]{:S(2)}, u32[]{:S(2)}) %collective-permute-start.21) | collective-permute-done | bytes 65568 | tf_op jit(solution)/shard_map/ppermute | solution.py:38
  158.6 1.9 %collective-permute-start.26 = (f32[32,128]{1,0:T(8,128)S(1)}, f32[32,128]{1,0:T(8,128)S(1)}, u32[]{:S(2)}, u32[]{:S(2)}) collective-permute-start(f32[32,128]{1,0:T(8,128)S(1)} %get-tuple-element.32), channel_id=1, source_target_pairs={{0,2},{1,3},{2,0},{3,1},{4,6},{5,7},{6,4},{7,5},{8,10},{9,11},{10,... | collective-permute-start | bytes 49160 | tf_op jit(solution)/shard_map/ppermute | solution.py:38
  (89 shorter events, 40.9 us)
Async XLA Ops:
  3.2 6.7 %collective-permute-start.2 = (bf16[64,768]{1,0:T(8,128)(2,1)S(1)}, bf16[64,768]{1,0:T(8,128)(2,1)S(1)}, u32[]{:S(2)}, u32[]{:S(2)}) collective-permute-start(bf16[64,768]{1,0:T(8,128)(2,1)S(1)} %get-tuple-element.18), channel_id=1, source_target_pairs={{0,16},{1,19},{2,18},{3,17},{4,20},{5,23},{6,22},{7,21},{8,24},{9,... | collective-permute-start | bytes 294920 | tf_op jit(solution)/shard_map/ppermute | solution.py:38
  9.9 6.9 %collective-permute-start.3 = (bf16[2,64,768]{2,1,0:T(8,128)(2,1)S(1)}, bf16[2,64,768]{2,1,0:T(8,128)(2,1)S(1)}, u32[]{:S(2)}, u32[]{:S(2)}) collective-permute-start(bf16[2,64,768]{2,1,0:T(8,128)(2,1)S(1)} %pad_maximum_fusion.1), channel_id=1, source_target_pairs={{0,4},{1,33},{2,6},{3,35},{4,8},{5,37},{6,10},{7,39},{8,12},{9,41}... | collective-permute-start | bytes 589832 | tf_op jit(solution)/shard_map/ppermute | solution.py:38
  11.6 6.0 %collective-permute-start.4 = (bf16[2,64,768]{2,1,0:T(8,128)(2,1)S(1)}, bf16[2,64,768]{2,1,0:T(8,128)(2,1)S(1)}, u32[]{:S(2)}, u32[]{:S(2)}) collective-permute-start(bf16[2,64,768]{2,1,0:T(8,128)(2,1)S(1)} %pad_maximum_fusion.1), channel_id=1, source_target_pairs={{0,12},{1,97},{2,14},{3,99},{4,0},{5,101},{6,2},{7,103},{8,4},{9,1... | collective-permute-start | bytes 589832 | tf_op jit(solution)/shard_map/ppermute | solution.py:38
  13.2 7.2 %collective-permute-start.5 = (bf16[2,64,768]{2,1,0:T(8,128)(2,1)S(1)}, bf16[2,64,768]{2,1,0:T(8,128)(2,1)S(1)}, u32[]{:S(2)}, u32[]{:S(2)}) collective-permute-start(bf16[2,64,768]{2,1,0:T(8,128)(2,1)S(1)} %pad_maximum_fusion.1), channel_id=1, source_target_pairs={{0,8},{1,65},{2,10},{3,67},{4,12},{5,69},{6,14},{7,71},{8,0},{9,73... | collective-permute-start | bytes 589832 | tf_op jit(solution)/shard_map/ppermute | solution.py:38
  21.1 13.4 %collective-permute-start.6 = (bf16[8,64,768]{2,1,0:T(8,128)(2,1)}, bf16[8,64,768]{2,1,0:T(8,128)(2,1)S(1)}, u32[]{:S(2)}, u32[]{:S(2)}) collective-permute-start(bf16[8,64,768]{2,1,0:T(8,128)(2,1)} %constant_dynamic-update-slice_fusion.m0), channel_id=1, source_target_pairs={{0,32},{1,5},{2,34},{3,7},{4,36},{5,9},{6,38},{7,11},{8,40},{9,13}... | collective-permute-start | bytes 2359304 | tf_op jit(solution)/shard_map/ppermute | solution.py:38
  22.6 13.3 %collective-permute-start.7 = (bf16[8,64,768]{2,1,0:T(8,128)(2,1)}, bf16[8,64,768]{2,1,0:T(8,128)(2,1)S(1)}, u32[]{:S(2)}, u32[]{:S(2)}) collective-permute-start(bf16[8,64,768]{2,1,0:T(8,128)(2,1)} %constant_dynamic-update-slice_fusion.m0), channel_id=1, source_target_pairs={{0,96},{1,13},{2,98},{3,15},{4,100},{5,1},{6,102},{7,3},{8,104},{9... | collective-permute-start | bytes 2359304 | tf_op jit(solution)/shard_map/ppermute | solution.py:38
  34.5 17.0 %collective-permute-start.8 = (bf16[4,64,768]{2,1,0:T(8,128)(2,1)S(1)}, bf16[4,64,768]{2,1,0:T(8,128)(2,1)S(1)}, u32[]{:S(2)}, u32[]{:S(2)}) collective-permute-start(bf16[4,64,768]{2,1,0:T(8,128)(2,1)S(1)} %slice.64), channel_id=1, source_target_pairs={{0,32},{1,5},{2,34},{3,7},{4,36},{5,9},{6,38},{7,11},{8,40},{9,13}... | collective-permute-start | bytes 1179656 | tf_op jit(solution)/shard_map/ppermute | solution.py:38
  35.7 52.6 %collective-permute-start = (bf16[2,17,32,128]{3,2,1,0:T(8,128)(2,1)}, bf16[2,17,32,128]{3,2,1,0:T(8,128)(2,1)}, u32[]{:S(2)}, u32[]{:S(2)}) collective-permute-start(bf16[2,17,32,128]{3,2,1,0:T(8,128)(2,1)} %get-tuple-element.27), channel_id=1, source_target_pairs={{0,1},{1,0},{2,3},{3,2},{4,5},{5,4},{6,7},{7,6},{8,9},{9,8},{10,11... | collective-permute-start | bytes 835592 | tf_op jit(solution)/shard_map/ppermute | solution.py:38
  36.7 16.7 %collective-permute-start.9 = (bf16[4,64,768]{2,1,0:T(8,128)(2,1)}, bf16[4,64,768]{2,1,0:T(8,128)(2,1)}, u32[]{:S(2)}, u32[]{:S(2)}) collective-permute-start(bf16[4,64,768]{2,1,0:T(8,128)(2,1)} %slice.65), channel_id=1, source_target_pairs={{0,96},{1,13},{2,98},{3,15},{4,100},{5,1},{6,102},{7,3},{8,104},{9... | collective-permute-start | bytes 1179656 | tf_op jit(solution)/shard_map/ppermute | solution.py:38
  51.1 12.3 %collective-permute-start.10 = (bf16[8,64,768]{2,1,0:T(8,128)(2,1)}, bf16[8,64,768]{2,1,0:T(8,128)(2,1)}, u32[]{:S(2)}, u32[]{:S(2)}) collective-permute-start(bf16[8,64,768]{2,1,0:T(8,128)(2,1)} %constant_dynamic-update-slice_fusion.m0), channel_id=1, source_target_pairs={{0,1},{1,0},{2,3},{3,2},{4,5},{5,4},{6,7},{7,6},{8,9},{9,8},{10,11... | collective-permute-start | bytes 2359304 | tf_op jit(solution)/shard_map/ppermute | solution.py:38
  51.1 12.3 %collective-permute-start.11 = (bf16[8,64,768]{2,1,0:T(8,128)(2,1)S(1)}, bf16[8,64,768]{2,1,0:T(8,128)(2,1)}, u32[]{:S(2)}, u32[]{:S(2)}) collective-permute-start(bf16[8,64,768]{2,1,0:T(8,128)(2,1)S(1)} %collective-permute-done.6.m1), channel_id=1, source_target_pairs={{0,1},{1,0},{2,3},{3,2},{4,5},{5,4},{6,7},{7,6},{8,9},{9,8},{10,11... | collective-permute-start | bytes 2359304 | tf_op jit(solution)/shard_map/ppermute | solution.py:38
  52.4 11.0 %collective-permute-start.12 = (bf16[8,64,768]{2,1,0:T(8,128)(2,1)S(1)}, bf16[8,64,768]{2,1,0:T(8,128)(2,1)}, u32[]{:S(2)}, u32[]{:S(2)}) collective-permute-start(bf16[8,64,768]{2,1,0:T(8,128)(2,1)S(1)} %collective-permute-done.7.m2), channel_id=1, source_target_pairs={{0,1},{1,0},{2,3},{3,2},{4,5},{5,4},{6,7},{7,6},{8,9},{9,8},{10,11... | collective-permute-start | bytes 2359304 | tf_op jit(solution)/shard_map/ppermute | solution.py:38
  54.4 8.9 %collective-permute-start.13 = (bf16[8,64,768]{2,1,0:T(8,128)(2,1)S(1)}, bf16[8,64,768]{2,1,0:T(8,128)(2,1)}, u32[]{:S(2)}, u32[]{:S(2)}) collective-permute-start(bf16[8,64,768]{2,1,0:T(8,128)(2,1)S(1)} %constant_dynamic-update-slice_fusion.5.m3), channel_id=1, source_target_pairs={{0,1},{1,0},{2,3},{3,2},{4,5},{5,4},{6,7},{7,6},{8,9},{9,8},{10,11... | collective-permute-start | bytes 2359304 | tf_op jit(solution)/shard_map/ppermute | solution.py:38
  89.3 17.0 %collective-permute-start.1 = (bf16[2,2,17,32,128]{4,3,2,1,0:T(8,128)(2,1)S(1)}, bf16[2,2,17,32,128]{4,3,2,1,0:T(8,128)(2,1)S(1)}, u32[]{:S(2)}, u32[]{:S(2)}) collective-permute-start(bf16[2,2,17,32,128]{4,3,2,1,0:T(8,128)(2,1)S(1)} %pad_maximum_fusion.a_ref), channel_id=1, source_target_pairs={{0,2},{1,3},{2,0},{3,1},{4,6},{5,7},{6,4},{7,5},{8,10},{9,11},{10,... | collective-permute-start | bytes 1671176 | tf_op jit(solution)/shard_map/ppermute | solution.py:38
  91.3 24.6 %collective-permute-start.15 = (bf16[17,32,256]{2,1,0:T(8,128)(2,1)S(1)}, bf16[17,32,256]{2,1,0:T(8,128)(2,1)S(1)}, u32[]{:S(2)}, u32[]{:S(2)}) collective-permute-start(bf16[17,32,256]{2,1,0:T(8,128)(2,1)S(1)} %add_convert_fusion), channel_id=1, source_target_pairs={{0,2},{1,3},{2,0},{3,1},{4,6},{5,7},{6,4},{7,5},{8,10},{9,11},{10,... | collective-permute-start | bytes 835592 | tf_op jit(solution)/shard_map/ppermute | solution.py:38
  139.0 8.0 %collective-permute-start.20 = (f32[4,4,32,128]{3,2,1,0:T(8,128)S(1)}, f32[4,4,32,128]{3,2,1,0:T(8,128)S(1)}, u32[]{:S(2)}, u32[]{:S(2)}) collective-permute-start(f32[4,4,32,128]{3,2,1,0:T(8,128)S(1)} %bitcast.76), channel_id=1, source_target_pairs={{0,8},{1,65},{2,10},{3,67},{4,12},{5,69},{6,14},{7,71},{8,0},{9,73... | collective-permute-start | bytes 786440 | tf_op jit(solution)/shard_map/ppermute | solution.py:38
  141.1 7.9 %collective-permute-start.19 = (f32[4,4,32,128]{3,2,1,0:T(8,128)S(1)}, f32[4,4,32,128]{3,2,1,0:T(8,128)S(1)}, u32[]{:S(2)}, u32[]{:S(2)}) collective-permute-start(f32[4,4,32,128]{3,2,1,0:T(8,128)S(1)} %bitcast.75), channel_id=1, source_target_pairs={{0,12},{1,97},{2,14},{3,99},{4,0},{5,101},{6,2},{7,103},{8,4},{9,1... | collective-permute-start | bytes 786440 | tf_op jit(solution)/shard_map/ppermute | solution.py:38
  143.0 7.6 %collective-permute-start.18 = (f32[4,4,32,128]{3,2,1,0:T(8,128)S(1)}, f32[4,4,32,128]{3,2,1,0:T(8,128)S(1)}, u32[]{:S(2)}, u32[]{:S(2)}) collective-permute-start(f32[4,4,32,128]{3,2,1,0:T(8,128)S(1)} %bitcast.74), channel_id=1, source_target_pairs={{0,4},{1,33},{2,6},{3,35},{4,8},{5,37},{6,10},{7,39},{8,12},{9,41}... | collective-permute-start | bytes 786440 | tf_op jit(solution)/shard_map/ppermute | solution.py:38
  150.7 5.8 %collective-permute-start.23 = (f32[4,32,128]{2,1,0:T(8,128)S(1)}, f32[4,32,128]{2,1,0:T(8,128)S(1)}, u32[]{:S(2)}, u32[]{:S(2)}) collective-permute-start(f32[4,32,128]{2,1,0:T(8,128)S(1)} %get-tuple-element.29), channel_id=1, source_target_pairs={{0,64},{1,9},{2,66},{3,11},{4,68},{5,13},{6,70},{7,15},{8,72},{9,1... | collective-permute-start | bytes 196616 | tf_op jit(solution)/shard_map/ppermute | solution.py:38
  151.6 4.9 %collective-permute-start.22 = (f32[4,32,128]{2,1,0:T(8,128)S(1)}, f32[4,32,128]{2,1,0:T(8,128)S(1)}, u32[]{:S(2)}, u32[]{:S(2)}) collective-permute-start(f32[4,32,128]{2,1,0:T(8,128)S(1)} %get-tuple-element.30), channel_id=1, source_target_pairs={{0,96},{1,13},{2,98},{3,15},{4,100},{5,1},{6,102},{7,3},{8,104},{9... | collective-permute-start | bytes 196616 | tf_op jit(solution)/shard_map/ppermute | solution.py:38
  153.0 5.5 %collective-permute-start.21 = (f32[4,32,128]{2,1,0:T(8,128)S(1)}, f32[4,32,128]{2,1,0:T(8,128)S(1)}, u32[]{:S(2)}, u32[]{:S(2)}) collective-permute-start(f32[4,32,128]{2,1,0:T(8,128)S(1)} %get-tuple-element.28), channel_id=1, source_target_pairs={{0,32},{1,5},{2,34},{3,7},{4,36},{5,9},{6,38},{7,11},{8,40},{9,13}... | collective-permute-start | bytes 196616 | tf_op jit(solution)/shard_map/ppermute | solution.py:38
  158.6 5.5 %collective-permute-start.26 = (f32[32,128]{1,0:T(8,128)S(1)}, f32[32,128]{1,0:T(8,128)S(1)}, u32[]{:S(2)}, u32[]{:S(2)}) collective-permute-start(f32[32,128]{1,0:T(8,128)S(1)} %get-tuple-element.32), channel_id=1, source_target_pairs={{0,2},{1,3},{2,0},{3,1},{4,6},{5,7},{6,4},{7,5},{8,10},{9,11},{10,... | collective-permute-start | bytes 49160 | tf_op jit(solution)/shard_map/ppermute | solution.py:38
  160.5 3.7 %collective-permute-start.25 = (f32[32,128]{1,0:T(8,128)S(1)}, f32[32,128]{1,0:T(8,128)S(1)}, u32[]{:S(2)}, u32[]{:S(2)}) collective-permute-start(f32[32,128]{1,0:T(8,128)S(1)} %get-tuple-element.33), channel_id=1, source_target_pairs={{0,18},{1,19},{2,16},{3,17},{4,22},{5,23},{6,20},{7,21},{8,26},{9,... | collective-permute-start | bytes 49160 | tf_op jit(solution)/shard_map/ppermute | solution.py:38
  161.2 4.9 %collective-permute-start.24 = (f32[32,128]{1,0:T(8,128)S(1)}, f32[32,128]{1,0:T(8,128)S(1)}, u32[]{:S(2)}, u32[]{:S(2)}) collective-permute-start(f32[32,128]{1,0:T(8,128)S(1)} %get-tuple-element.31), channel_id=1, source_target_pairs={{0,16},{1,17},{2,18},{3,19},{4,20},{5,21},{6,22},{7,23},{8,24},{9,... | collective-permute-start | bytes 49160 | tf_op jit(solution)/shard_map/ppermute | solution.py:38
  (10 other events, 102.1 us)

commit v2 on v1

--- a/solution.py
+++ b/solution.py
@@ -76,6 +76,27 @@
     return half, step - half * meta[0]
 
 
+def pack_kernel(q_ref, n_ref, out):
+    n = n_ref[...] * -math.sqrt(192.0)
+    n1 = n.astype(jnp.bfloat16).astype(jnp.float32)
+    n2 = (n - n1).astype(jnp.bfloat16).astype(jnp.float32)
+    n3 = n - n1 - n2
+    row = lax.broadcasted_iota(jnp.int32, (64, 128), 0)
+    for i in range(16):
+        lanes = slice(i * 128, (i + 1) * 128)
+        a, b = q_ref[2 * i], q_ref[2 * i + 1]
+        out[0, 0:576, lanes] = jnp.concatenate((a[:, 0:64], b[:, 0:64]), axis=1)
+        out[1, 0:576, lanes] = jnp.concatenate((a[:, 64:128], b[:, 64:128]), axis=1)
+        for half in range(2):
+            cut = slice(half * 64, half * 64 + 64)
+            parts = [
+                jnp.concatenate((v[2 * i : 2 * i + 1, cut], v[2 * i + 1 : 2 * i + 2, cut]), axis=1)
+                for v in (n1, n2, n3)
+            ]
+            block = jnp.where(row == 0, parts[0], jnp.where(row == 1, parts[1], jnp.where(row == 2, parts[2], 0.0)))
+            out[half, 576:640, lanes] = block.astype(jnp.bfloat16)
+
+
 def target_kernel(meta, loc, q_ref, m0, m1, m2, m3, s0, s1, s2, s3, keep, other, sorted_ref, keys, sems):
     core = meta[1]
     copies = []
@@ -102,18 +123,21 @@
         tile = jnp.concatenate(
             [keys[loc[ktile * PER_TILE + u], :, 0:640] for u in range(PER_TILE)], axis=0
         )
-        total = jnp.zeros((HALF, TILE), jnp.float32)
+        total = jnp.zeros((TILE, 128), jnp.float32)
         for g in range(8):
-            rows = q_ref[pl.ds(pl.multiple_of(half * 2048 + g * 256, 256), 256), :]
-            s = lax.dot_general(rows, tile, NT, preferred_element_type=jnp.float32)
+            s = lax.dot_general(
+                tile, q_ref[half, :, g * 256 : (g + 1) * 256], NN, preferred_element_type=jnp.float32
+            )
             e = jnp.exp2(s * scale)
-            total = total + ((e[0:64] + e[64:128]) + (e[128:192] + e[192:256]))
+            total = total + (e[:, 0:128] + e[:, 128:256])
+        total = total.T
+        total = total[0:64] + total[64:128]
         top, low = total[0:32], total[32:64]
         keep[step] = jnp.where(core == 0, top, low)
         other[step] = jnp.where(core == 0, low, top)
         return 0
 
-    lax.fori_loop(0, TILES, body, 0)
+    lax.fori_loop(0, TILES, body, 0, unroll=4)
 
 
 def visible_of(meta, half, ktile):
@@ -149,7 +173,7 @@
         top[half] = jnp.maximum(top[half], logits)
         return 0
 
-    lax.fori_loop(0, TILES, first, 0)
+    lax.fori_loop(0, TILES, first, 0, unroll=4)
     for half in range(2):
         top[half] = jnp.broadcast_to(jnp.max(top[half], axis=1, keepdims=True), (32, TILE))
 
@@ -195,38 +219,40 @@
     lax.fori_loop(0, TILES, second, 0)
 
 
-def backward_kernel(
-    idx_scale, meta, stored, g_ref, h_ref, iq_ref, iqt_ref, key_ref, dq, keep, other, wide
-):
-    core = meta[1]
+def spread(iq_ref, wide, idx_scale):
     for half in range(2):
         w = iq_ref[half, 16].astype(jnp.float32) * idx_scale
         for j in range(16):
             wide[half, pl.ds(j * HALF, HALF)] = jnp.broadcast_to(w[:, j : j + 1], (HALF, 128))
-    dq[...] = jnp.zeros(dq.shape, jnp.float32)
+
+
+def coefficients(meta, step, g_ref, h_ref, iq_ref, key_ref, wide):
+    core = meta[1]
+    half, ktile = place(meta, step)
+    tile = key_ref[pl.ds(pl.multiple_of(ktile * TILE, TILE), TILE), :]
+    mine, theirs = g_ref[step].astype(jnp.float32), h_ref[step].astype(jnp.float32)
+    g = jnp.concatenate((jnp.where(core == 0, mine, theirs), jnp.where(core == 0, theirs, mine)), axis=0)
+    g = jnp.concatenate((g, g, g, g), axis=0)
+    found = []
+    for q in range(4):
+        rows = iq_ref[half, pl.ds(q * 4, 4)].reshape(256, 128)
+        d = lax.dot_general(rows, tile, NT, preferred_element_type=jnp.float32)
+        w = wide[half, pl.ds(q * 256, 256)]
+        found.append(jnp.where(d > 0, g * jnp.concatenate((w, w), axis=1), 0.0).astype(jnp.bfloat16))
+    return half, ktile, tile, found
+
+
+def key_kernel(idx_scale, meta, stored, g_ref, h_ref, iq_ref, iqt_ref, key_ref, keep, other, wide):
+    core = meta[1]
+    spread(iq_ref, wide, idx_scale)
     keep[...] = jnp.zeros(keep.shape, jnp.float32)
     other[...] = jnp.zeros(other.shape, jnp.float32)
 
     def body(step, _):
-        half, ktile = place(meta, step)
-        tile = key_ref[pl.ds(pl.multiple_of(ktile * TILE, TILE), TILE), :]
-        mine, theirs = g_ref[step].astype(jnp.float32), h_ref[step].astype(jnp.float32)
-        g = jnp.concatenate(
-            (jnp.where(core == 0, mine, theirs), jnp.where(core == 0, theirs, mine)), axis=0
+        half, ktile, _tile, found = coefficients(meta, step, g_ref, h_ref, iq_ref, key_ref, wide)
+        dkt = lax.dot_general(
+            iqt_ref[half], jnp.concatenate(found, axis=0), NN, preferred_element_type=jnp.float32
         )
-        g = jnp.concatenate((g, g, g, g), axis=0)
-        dkt = jnp.zeros((128, TILE), jnp.float32)
-        for q in range(4):
-            rows = iq_ref[half, pl.ds(q * 4, 4)].reshape(256, 128)
-            d = lax.dot_general(rows, tile, NT, preferred_element_type=jnp.float32)
-            w = wide[half, pl.ds(q * 256, 256)]
-            coefficient = jnp.where(d > 0, g * jnp.concatenate((w, w), axis=1), 0.0).astype(jnp.bfloat16)
-            dq[half, pl.ds(q * 256, 256)] = dq[half, pl.ds(q * 256, 256)] + lax.dot_general(
-                coefficient, tile, NN, preferred_element_type=jnp.float32
-            )
-            dkt = dkt + lax.dot_general(
-                iqt_ref[half, :, q * 256 : (q + 1) * 256], coefficient, NN, preferred_element_type=jnp.float32
-            )
         dk = dkt.T
         for u in range(PER_TILE):
             slot, slot_other = stored[ktile * PER_TILE + u], stored[64 + ktile * PER_TILE + u]
@@ -235,7 +261,22 @@
             other[slot_other] = other[slot_other] + jnp.where(core == 0, last, first)
         return 0
 
-    lax.fori_loop(0, TILES, body, 0)
+    lax.fori_loop(0, TILES, body, 0, unroll=4)
+
+
+def query_kernel(idx_scale, meta, g_ref, h_ref, iq_ref, key_ref, dq, wide):
+    spread(iq_ref, wide, idx_scale)
+    dq[...] = jnp.zeros(dq.shape, jnp.float32)
+
+    def body(step, _):
+        half, _ktile, tile, found = coefficients(meta, step, g_ref, h_ref, iq_ref, key_ref, wide)
+        for q in range(4):
+            dq[half, pl.ds(q * 256, 256)] = dq[half, pl.ds(q * 256, 256)] + lax.dot_general(
+                found[q], tile, NN, preferred_element_type=jnp.float32
+            )
+        return 0
+
+    lax.fori_loop(0, TILES, body, 0, unroll=4)
 
 
 def ring_sum(value, route):
@@ -259,10 +300,32 @@
     pair = jnp.stack((own, beside))
     legs = [pair] + [send(pair, along(True, shift)) for shift in (1, 3, 2)]
     group = jnp.concatenate(legs, axis=0)
+    query = pl.pallas_call(
+        pack_kernel,
+        out_shape=jax.ShapeDtypeStruct((2, 640, 2048), bf16),
+        in_specs=[vmem(), vmem()],
+        out_specs=vmem(),
+        compiler_params=params(8),
+        cost_estimate=pl.CostEstimate(flops=0, bytes_accessed=12_000_000, transcendentals=0),
+        name="pack",
+    )(query_latent.transpose(1, 2, 0), normalizer.T)
+
+    iq = indexer_query.reshape(2, HALF, 16, 128).transpose(0, 2, 1, 3)
+    weight = jnp.pad(indexer_weight.reshape(2, 1, HALF, 16), ((0, 0), (0, 0), (0, 0), (0, 112)))
+    iqw = jnp.concatenate((iq, weight), axis=1)
+    iqt = iq.transpose(0, 3, 1, 2).reshape(2, 128, 1024)
+    iq_keep = lax.dynamic_slice_in_dim(iqw, core * 32, 32, 2)
+    iq_other = swap_core(lax.dynamic_slice_in_dim(iqw, (1 - core) * 32, 32, 2))
+    iq_chip = jnp.stack((iq_keep, iq_other))
+    group, iq_chip = lax.optimization_barrier((group, iq_chip))
+    iq_far = swap_high(iq_chip)
+
     up, down = send(group, along(False, 1)), send(group, along(False, 3))
+    up, query = lax.optimization_barrier((up, query))
     far_a = send(up[0:4], along(False, 1))
     far_b = send(down[4:8], along(False, 3))
     far = jnp.concatenate((far_a, far_b), axis=0)
+    far, iq_far, iqt = lax.optimization_barrier((far, iq_far, iqt))
     mine = [group, up, down, far]
     swapped = [swap_core(v) for v in mine]
 
@@ -286,24 +349,6 @@
     stored = jnp.concatenate((jnp.sum(hit * row_a[None, :], axis=1), jnp.sum(hit * row_b[None, :], axis=1)))
     meta = jnp.concatenate(((blocks[0:1] + PER_TILE) // PER_TILE, core[None], blocks)).astype(jnp.int32)
 
-    lifted = -normalizer * math.sqrt(192.0)
-    n1 = lax.reduce_precision(lifted, 8, 7)
-    n2 = lax.reduce_precision(lifted - n1, 8, 7)
-    n3 = lax.reduce_precision(lifted - n1 - n2, 8, 7)
-    columns = jnp.stack((n1, n2, n3), axis=-1).astype(bf16)
-    columns = jnp.pad(columns, ((0, 0), (0, 0), (0, 61)))
-    query = jnp.concatenate((query_latent, columns), axis=2)
-    query = query.reshape(2, HALF, 32, 640).transpose(0, 2, 1, 3).reshape(4096, 640)
-
-    iq = indexer_query.reshape(2, HALF, 16, 128).transpose(0, 2, 1, 3)
-    weight = jnp.pad(indexer_weight.reshape(2, 1, HALF, 16), ((0, 0), (0, 0), (0, 0), (0, 112)))
-    iqw = jnp.concatenate((iq, weight), axis=1)
-    iqt = iq.transpose(0, 3, 1, 2).reshape(2, 128, 1024)
-    iq_keep = lax.dynamic_slice_in_dim(iqw, core * 32, 32, 2)
-    iq_other = swap_core(lax.dynamic_slice_in_dim(iqw, (1 - core) * 32, 32, 2))
-    iq_chip = jnp.stack((iq_keep, iq_other))
-    iq_far = swap_high(iq_chip)
-
     part = jax.ShapeDtypeStruct((TILES, 32, TILE), f32)
     keep, other, sorted_keys = pl.pallas_call(
         target_kernel,
@@ -311,7 +356,7 @@
         in_specs=[smem(), smem(), vmem()] + [anywhere()] * 8,
         out_specs=(vmem(), vmem(), vmem()),
         scratch_shapes=[pltpu.VMEM((64, HALF, 768), bf16), pltpu.SemaphoreType.DMA((8,))],
-        compiler_params=params(40),
+        compiler_params=params(16),
         cost_estimate=pl.CostEstimate(flops=12_000_000_000, bytes_accessed=14_000_000, transcendentals=9_000_000),
         name="targets",
     )(meta, loc, query, *mine, *swapped)
@@ -329,7 +374,7 @@
             pltpu.VMEM((2, 32, TILE), f32),
             pltpu.VMEM((2, 32, TILE), f32),
         ],
-        compiler_params=params(24),
+        compiler_params=params(12),
         cost_estimate=pl.CostEstimate(flops=5_000_000_000, bytes_accessed=4_000_000, transcendentals=200_000),
         name="logits",
     )(meta, iq_chip, iq_far, sorted_keys)
@@ -340,28 +385,40 @@
         in_specs=[smem()] + [vmem()] * 4,
         out_specs=vmem(),
         scratch_shapes=[pltpu.VMEM((TILES, 32, TILE), f32), pltpu.VMEM((2, 32, TILE), f32)],
-        compiler_params=params(16),
+        compiler_params=params(8),
         name="gradient",
     )(meta, prob, keep, from_core, from_high)
     grad_other = swap_core(grad)
 
     shard = jax.ShapeDtypeStruct((64, 32, 128), f32)
-    dq, dk_keep, dk_other = pl.pallas_call(
-        functools.partial(backward_kernel, idx_scale),
-        out_shape=(jax.ShapeDtypeStruct((2, 1024, 128), f32), shard, shard),
+    cost = pl.CostEstimate(flops=5_000_000_000, bytes_accessed=4_000_000, transcendentals=0)
+    dk_keep, dk_other = pl.pallas_call(
+        functools.partial(key_kernel, idx_scale),
+        out_shape=(shard, shard),
         in_specs=[smem(), smem()] + [vmem()] * 5,
-        out_specs=(vmem(), vmem(), vmem()),
+        out_specs=(vmem(), vmem()),
         scratch_shapes=[pltpu.VMEM((2, 1024, 128), f32)],
-        compiler_params=params(24),
-        name="backward",
+        compiler_params=params(12),
+        cost_estimate=cost,
+        name="keys",
     )(meta, stored, grad, grad_other, iqw, iqt, sorted_keys)
-
-    query_grad = dq.reshape(2, 16, HALF, 128).transpose(0, 2, 1, 3).reshape(128, 16, 128)
+    dq = pl.pallas_call(
+        functools.partial(query_kernel, idx_scale),
+        out_shape=jax.ShapeDtypeStruct((2, 1024, 128), f32),
+        in_specs=[smem()] + [vmem()] * 4,
+        out_specs=vmem(),
+        scratch_shapes=[pltpu.VMEM((2, 1024, 128), f32)],
+        compiler_params=params(12),
+        cost_estimate=cost,
+        name="queries",
+    )(meta, grad, grad_other, iqw, sorted_keys)
 
     dk = dk_keep + swap_core(dk_other)
     dk = ring_sum(dk.reshape(4, 4, 4, 32, 128), functools.partial(along, True))
+    dk, dq = lax.optimization_barrier((dk, dq))
     dk = ring_sum(dk, functools.partial(along, False))
     dk = ring_sum(dk, lambda shift: lambda x, z, y, k: (x, z + shift, y, k))
+    query_grad = dq.reshape(2, 16, HALF, 128).transpose(0, 2, 1, 3).reshape(128, 16, 128)
     return query_grad, dk
 
 

time: 167 us -> 126 us (0.75)
  local copies, waits for them, and re-layouts: 33.5 us -> 14.8 us
  waiting for transfers between devices: 45.8 us -> 32 us
  Pallas kernels: 48.1 us -> 41.9 us
  other arithmetic: 7.51 us -> 2.93 us
  starting transfers between devices: 30.8 us -> 33.1 us
    ppermute x27, waiting for transfers between devices: 45.8 us -> 32 us  [send(): return lax.ppermute(value, ALL, permutation(move))]
    unnamed x22 -> x29, local copies, waits for them, and re-layouts: 20.7 us -> 10.8 us
    transpose x1 -> x0, local copies, waits for them, and re-layouts: 4.35 us -> none  [per_device(): query.reshape(2, HALF, 32, 640).transpose(0, 2, 1, 3).reshape(4096, 640)]
    concatenate x1, other arithmetic: 3.69 us -> 0.07 us  [per_device(): far = jnp.concatenate((far_a, far_b), axis=0)]
    pallas_call x1, Pallas kernels: 21 us -> 18.2 us  [per_device(): pl.pallas_call(target_kernel, out_shape=(part, part, jax.ShapeDtypeStruct...]
    ppermute x27, starting transfers between devices: 30.8 us -> 33.1 us  [send(): return lax.ppermute(value, ALL, permutation(move))]
    pallas_call x1, Pallas kernels: 9.64 us -> 7.45 us  [per_device(): pl.pallas_call(functools.partial(logit_kernel, idx_scale), out_shape=part...]
    pallas_call x1 -> x3, Pallas kernels: 16.3 us -> 15.1 us  [the longest x1 7.08 us: per_device(): pl.pallas_call(functools.partial(key_kernel, idx_scale), out_shape=(shard...]
  transfers between devices with their start and end apart: 27 -> 27, of which waited for: 13 -> 13; matrix products, arithmetic and copies ran while one was open for 19% -> 5% of each run, Pallas kernels for 18% -> 12%
where the time goes in v2:
time: 126 us
  Pallas kernels  41.9 us (33%)
  starting transfers between devices  33.1 us (26%)
  waiting for transfers between devices  32 us (25%)
  local copies, waits for them, and re-layouts  14.8 us (12%)
  other arithmetic  2.93 us (2%)
    ppermute x27, starting transfers between devices, send(): return lax.ppermute(value, ALL, permutation(move))  33.1 us
    ppermute x27, waiting for transfers between devices, send(): return lax.ppermute(value, ALL, permutation(move))  32 us
    pallas_call x1, Pallas kernels, per_device(): pl.pallas_call(target_kernel, out_shape=(part, part, jax.ShapeDtypeStruct...  18.2 us
    unnamed x29, local copies, waits for them, and re-layouts  10.8 us
    pallas_call x1, Pallas kernels, per_device(): pl.pallas_call(functools.partial(logit_kernel, idx_scale), out_shape=part...  7.45 us
    pallas_call x1, Pallas kernels, per_device(): pl.pallas_call(functools.partial(key_kernel, idx_scale), out_shape=(shard...  7.08 us
    pallas_call x1, Pallas kernels, per_device(): pl.pallas_call(functools.partial(query_kernel, idx_scale), out_shape=jax....  6.42 us
  transfers between devices with their start and end apart: 27, of which 13 were waited for; matrix products, arithmetic and copies ran while one was open for 5% of the time, Pallas kernels for 12%

profile of v2, /device:TPU:0, one launch (start us, length us, event | category | flops | bytes accessed | tf_op | source)
XLA Modules:
  0.0 125.7 jit_solution(8875870455965579861)
XLA Ops:
  3.3 2.0 %collective-permute-start = (bf16[64,768]{1,0:T(8,128)(2,1)S(1)}, bf16[64,768]{1,0:T(8,128)(2,1)S(1)}, u32[]{:S(2)}, u32[]{:S(2)}) collective-permute-start(bf16[64,768]{1,0:T(8,128)(2,1)S(1)} %get-tuple-element.34), channel_id=1, source_target_pairs={{0,16},{1,19},{2,18},{3,17},{4,20},{5,23},{6,22},{7,21},{8,24},{9,... | collective-permute-start | bytes 294920 | tf_op jit(solution)/shard_map/ppermute | solution.py:38
  6.3 1.8 %collective-permute-start.4 = (bf16[2,17,32,128]{3,2,1,0:T(8,128)(2,1)S(1)}, bf16[2,17,32,128]{3,2,1,0:T(8,128)(2,1)S(1)}, u32[]{:S(2)}, u32[]{:S(2)}) collective-permute-start(bf16[2,17,32,128]{3,2,1,0:T(8,128)(2,1)S(1)} %get-tuple-element.43), channel_id=1, source_target_pairs={{0,1},{1,0},{2,3},{3,2},{4,5},{5,4},{6,7},{7,6},{8,9},{9,8},{10,11... | collective-permute-start | bytes 835592 | tf_op jit(solution)/shard_map/ppermute | solution.py:38
  8.1 1.9 %collective-permute-done = bf16[64,768]{1,0:T(8,128)(2,1)S(1)} collective-permute-done((bf16[64,768]{1,0:T(8,128)(2,1)S(1)}, bf16[64,768]{1,0:T(8,128)(2,1)S(1)}, u32[]{:S(2)}, u32[]{:S(2)}) %collective-permute-start) | collective-permute-done | bytes 98336 | tf_op jit(solution)/shard_map/ppermute | solution.py:38
  10.0 3.3 %collective-permute-start.3 = (bf16[2,64,768]{2,1,0:T(8,128)(2,1)S(1)}, bf16[2,64,768]{2,1,0:T(8,128)(2,1)S(1)}, u32[]{:S(2)}, u32[]{:S(2)}) collective-permute-start(bf16[2,64,768]{2,1,0:T(8,128)(2,1)S(1)} %pad_maximum_fusion.2), channel_id=1, source_target_pairs={{0,8},{1,65},{2,10},{3,67},{4,12},{5,69},{6,14},{7,71},{8,0},{9,73... | collective-permute-start | bytes 589832 | tf_op jit(solution)/shard_map/ppermute | solution.py:38
  16.0 5.2 %collective-permute-done.1 = bf16[2,64,768]{2,1,0:T(8,128)(2,1)S(1)} collective-permute-done((bf16[2,64,768]{2,1,0:T(8,128)(2,1)S(1)}, bf16[2,64,768]{2,1,0:T(8,128)(2,1)S(1)}, u32[]{:S(2)}, u32[]{:S(2)}) %collective-permute-start.1) | collective-permute-done | bytes 196640 | tf_op jit(solution)/shard_map/ppermute | solution.py:38
  23.3 2.8 %collective-permute-start.7 = (bf16[8,64,768]{2,1,0:T(8,128)(2,1)}, bf16[8,64,768]{2,1,0:T(8,128)(2,1)S(1)}, u32[]{:S(2)}, u32[]{:S(2)}) collective-permute-start(bf16[8,64,768]{2,1,0:T(8,128)(2,1)} %constant_dynamic-update-slice_fusion.m0), channel_id=1, source_target_pairs={{0,96},{1,13},{2,98},{3,15},{4,100},{5,1},{6,102},{7,3},{8,104},{9... | collective-permute-start | bytes 2359304 | tf_op jit(solution)/shard_map/ppermute | solution.py:38
  26.0 1.9 %collective-permute-start.9 = (bf16[2,2,17,32,128]{4,3,2,1,0:T(8,128)(2,1)S(1)}, bf16[2,2,17,32,128]{4,3,2,1,0:T(8,128)(2,1)S(1)}, u32[]{:S(2)}, u32[]{:S(2)}) collective-permute-start(bf16[2,2,17,32,128]{4,3,2,1,0:T(8,128)(2,1)S(1)} %pad_maximum_fusion.1.a_ref), channel_id=1, source_target_pairs={{0,2},{1,3},{2,0},{3,1},{4,6},{5,7},{6,4},{7,5},{8,10},{9,11},{10,... | collective-permute-start | bytes 1671176 | tf_op jit(solution)/shard_map/ppermute | solution.py:38
  29.5 2.3 %copy-done = bf16[2,640,2048]{2,1,0:T(8,128)(2,1)} copy-done((bf16[2,640,2048]{2,1,0:T(8,128)(2,1)}, bf16[2,640,2048]{2,1,0:T(8,128)(2,1)S(1)}, u32[]{:S(2)}) %copy-start) | copy-done | bytes 5242904
  31.8 4.1 %collective-permute-done.7.m2 = bf16[8,64,768]{2,1,0:T(8,128)(2,1)S(1)} collective-permute-done((bf16[8,64,768]{2,1,0:T(8,128)(2,1)}, bf16[8,64,768]{2,1,0:T(8,128)(2,1)S(1)}, u32[]{:S(2)}, u32[]{:S(2)}) %collective-permute-start.7) | collective-permute-done | bytes 786464 | tf_op jit(solution)/shard_map/ppermute | solution.py:38
  35.9 3.7 %collective-permute-start.8 = (bf16[4,64,768]{2,1,0:T(8,128)(2,1)S(1)}, bf16[4,64,768]{2,1,0:T(8,128)(2,1)S(1)}, u32[]{:S(2)}, u32[]{:S(2)}) collective-permute-start(bf16[4,64,768]{2,1,0:T(8,128)(2,1)S(1)} %slice.64), channel_id=1, source_target_pairs={{0,96},{1,13},{2,98},{3,15},{4,100},{5,1},{6,102},{7,3},{8,104},{9... | collective-permute-start | bytes 1179656 | tf_op jit(solution)/shard_map/ppermute | solution.py:38
  41.1 3.7 %collective-permute-done.8 = bf16[4,64,768]{2,1,0:T(8,128)(2,1)S(1)} collective-permute-done((bf16[4,64,768]{2,1,0:T(8,128)(2,1)S(1)}, bf16[4,64,768]{2,1,0:T(8,128)(2,1)S(1)}, u32[]{:S(2)}, u32[]{:S(2)}) %collective-permute-start.8) | collective-permute-done | bytes 393248 | tf_op jit(solution)/shard_map/ppermute | solution.py:38
  44.8 3.8 %collective-permute-done.6 = bf16[4,64,768]{2,1,0:T(8,128)(2,1)S(1)} collective-permute-done((bf16[4,64,768]{2,1,0:T(8,128)(2,1)S(1)}, bf16[4,64,768]{2,1,0:T(8,128)(2,1)S(1)}, u32[]{:S(2)}, u32[]{:S(2)}) %collective-permute-start.6) | collective-permute-done | bytes 393248 | tf_op jit(solution)/shard_map/ppermute | solution.py:38
  50.1 1.9 %collective-permute-done.13.s3 = bf16[8,64,768]{2,1,0:T(8,128)(2,1)} collective-permute-done((bf16[8,64,768]{2,1,0:T(8,128)(2,1)S(1)}, bf16[8,64,768]{2,1,0:T(8,128)(2,1)}, u32[]{:S(2)}, u32[]{:S(2)}) %collective-permute-start.13) | collective-permute-done | bytes 786464 | tf_op jit(solution)/shard_map/ppermute | solution.py:38
  52.0 2.5 %copy-done.1 = bf16[2,640,2048]{2,1,0:T(8,128)(2,1)S(1)} copy-done((bf16[2,640,2048]{2,1,0:T(8,128)(2,1)S(1)}, bf16[2,640,2048]{2,1,0:T(8,128)(2,1)}, u32[]{:S(2)}) %copy-start.1) | copy-done | bytes 5242904
  54.5 18.2 %targets.1 = (f32[17,32,256]{2,1,0:T(8,128)S(1)}, f32[17,32,256]{2,1,0:T(8,128)S(1)}, bf16[4096,128]{1,0:T(8,128)(2,1)S(1)}) custom-call(s32[4]{0:T(128)S(1)} %pad_add_fusion.meta, s32[64]{0:T(128)S(1)} %get-tuple-element.30.loc, bf16[2,640,2048]{2,1,0:T(8,128)(2,1)S(1)} %copy-done.1, bf16[8,64,768]{2,1,0:T(8,128)(2,1)} %constant_dynamic-update-slice_fusion.m0, ...), custom_call_target="tpu_custom_call" | custom-call | flops 12000000000 | bytes 14000000 | tf_op jit(solution)/shard_map/targets/pallas_call | solution.py:353
  72.9 1.8 %collective-permute-done.14.b_ref = f32[17,32,256]{2,1,0:T(8,128)S(1)} collective-permute-done((f32[17,32,256]{2,1,0:T(8,128)S(1)}, f32[17,32,256]{2,1,0:T(8,128)S(1)}, u32[]{:S(2)}, u32[]{:S(2)}) %collective-permute-start.14) | collective-permute-done | bytes 557088 | tf_op jit(solution)/shard_map/ppermute | solution.py:38
  74.9 2.1 %collective-permute-start.15 = (bf16[17,32,256]{2,1,0:T(8,128)(2,1)S(1)}, bf16[17,32,256]{2,1,0:T(8,128)(2,1)S(1)}, u32[]{:S(2)}, u32[]{:S(2)}) collective-permute-start(bf16[17,32,256]{2,1,0:T(8,128)(2,1)S(1)} %add_convert_fusion), channel_id=1, source_target_pairs={{0,2},{1,3},{2,0},{3,1},{4,6},{5,7},{6,4},{7,5},{8,10},{9,11},{10,... | collective-permute-start | bytes 835592 | tf_op jit(solution)/shard_map/ppermute | solution.py:38
  77.0 7.4 %logits.1.p_ref = f32[17,32,256]{2,1,0:T(8,128)S(1)} custom-call(s32[4]{0:T(128)S(1)} %pad_add_fusion.meta, bf16[2,2,17,32,128]{4,3,2,1,0:T(8,128)(2,1)S(1)} %pad_maximum_fusion.1.a_ref, bf16[2,2,17,32,128]{4,3,2,1,0:T(8,128)(2,1)S(1)} %copy-done.5, bf16[4096,128]{1,0:T(8,128)(2,1)S(1)} %get-tuple-element.22.key_ref), custom_call_target="tpu_custom_call" | custom-call | flops 5000000000 | bytes 4000000 | tf_op jit(solution)/shard_map/logits/pallas_call | solution.py:367
  89.3 7.1 %keys.1 = (f32[64,32,128]{2,1,0:T(8,128)S(1)}, f32[64,32,128]{2,1,0:T(8,128)S(1)}) custom-call(s32[4]{0:T(128)S(1)} %pad_add_fusion.meta, s32[128]{0:T(128)S(1)} %pad_add_fusion.1.stored, bf16[17,32,256]{2,1,0:T(8,128)(2,1)S(1)} %gradient.1.g_ref, bf16[17,32,256]{2,1,0:T(8,128)(2,1)S(1)} %collective-permute-done.16.h_ref, ...), custom_call_target="tpu_custom_call" | custom-call | flops 5000000000 | bytes 4000000 | tf_op jit(solution)/shard_map/keys/pallas_call | solution.py:395
  96.6 2.5 %collective-permute-done.17 = f32[64,32,128]{2,1,0:T(8,128)S(1)} collective-permute-done((f32[64,32,128]{2,1,0:T(8,128)S(1)}, f32[64,32,128]{2,1,0:T(8,128)S(1)}, u32[]{:S(2)}, u32[]{:S(2)}) %collective-permute-start.17) | collective-permute-done | bytes 1048608 | tf_op jit(solution)/shard_map/ppermute | solution.py:38
  100.9 3.2 %collective-permute-start.19 = (f32[4,4,32,128]{3,2,1,0:T(8,128)S(1)}, f32[4,4,32,128]{3,2,1,0:T(8,128)S(1)}, u32[]{:S(2)}, u32[]{:S(2)}) collective-permute-start(f32[4,4,32,128]{3,2,1,0:T(8,128)S(1)} %bitcast.65), channel_id=1, source_target_pairs={{0,12},{1,97},{2,14},{3,99},{4,0},{5,101},{6,2},{7,103},{8,4},{9,1... | collective-permute-start | bytes 786440 | tf_op jit(solution)/shard_map/ppermute | solution.py:38
  104.1 6.4 %queries.1 = f32[2,1024,128]{2,1,0:T(8,128)S(1)} custom-call(s32[4]{0:T(128)S(1)} %pad_add_fusion.meta, bf16[17,32,256]{2,1,0:T(8,128)(2,1)S(1)} %gradient.1.g_ref, bf16[17,32,256]{2,1,0:T(8,128)(2,1)S(1)} %collective-permute-done.16.h_ref, bf16[2,17,64,128]{3,2,1,0:T(8,128)(2,1)S(1)} %fusion.1.iq_ref, bf16[4096,128]{1,0:T(8,128)(2,1)S(1)} %copy-done.8), custom_call_target="tpu_custom_call" | custom-call | flops 5000000000 | bytes 4000000 | tf_op jit(solution)/shard_map/queries/pallas_call | solution.py:405
  114.0 2.9 %collective-permute-done.21 = f32[4,32,128]{2,1,0:T(8,128)S(1)} collective-permute-done((f32[4,32,128]{2,1,0:T(8,128)S(1)}, f32[4,32,128]{2,1,0:T(8,128)S(1)}, u32[]{:S(2)}, u32[]{:S(2)}) %collective-permute-start.21) | collective-permute-done | bytes 65568 | tf_op jit(solution)/shard_map/ppermute | solution.py:38
  118.0 3.3 %collective-permute-start.26 = (f32[32,128]{1,0:T(8,128)S(1)}, f32[32,128]{1,0:T(8,128)S(1)}, u32[]{:S(2)}, u32[]{:S(2)}) collective-permute-start(f32[32,128]{1,0:T(8,128)S(1)} %get-tuple-element.48), channel_id=1, source_target_pairs={{0,2},{1,3},{2,0},{3,1},{4,6},{5,7},{6,4},{7,5},{8,10},{9,11},{10,... | collective-permute-start | bytes 49160 | tf_op jit(solution)/shard_map/ppermute | solution.py:38
  (94 shorter events, 28.8 us)
Async XLA Ops:
  3.3 6.7 %collective-permute-start = (bf16[64,768]{1,0:T(8,128)(2,1)S(1)}, bf16[64,768]{1,0:T(8,128)(2,1)S(1)}, u32[]{:S(2)}, u32[]{:S(2)}) collective-permute-start(bf16[64,768]{1,0:T(8,128)(2,1)S(1)} %get-tuple-element.34), channel_id=1, source_target_pairs={{0,16},{1,19},{2,18},{3,17},{4,20},{5,23},{6,22},{7,21},{8,24},{9,... | collective-permute-start | bytes 294920 | tf_op jit(solution)/shard_map/ppermute | solution.py:38
  6.3 9.6 %collective-permute-start.4 = (bf16[2,17,32,128]{3,2,1,0:T(8,128)(2,1)S(1)}, bf16[2,17,32,128]{3,2,1,0:T(8,128)(2,1)S(1)}, u32[]{:S(2)}, u32[]{:S(2)}) collective-permute-start(bf16[2,17,32,128]{3,2,1,0:T(8,128)(2,1)S(1)} %get-tuple-element.43), channel_id=1, source_target_pairs={{0,1},{1,0},{2,3},{3,2},{4,5},{5,4},{6,7},{7,6},{8,9},{9,8},{10,11... | collective-permute-start | bytes 835592 | tf_op jit(solution)/shard_map/ppermute | solution.py:38
  10.0 12.6 %collective-permute-start.3 = (bf16[2,64,768]{2,1,0:T(8,128)(2,1)S(1)}, bf16[2,64,768]{2,1,0:T(8,128)(2,1)S(1)}, u32[]{:S(2)}, u32[]{:S(2)}) collective-permute-start(bf16[2,64,768]{2,1,0:T(8,128)(2,1)S(1)} %pad_maximum_fusion.2), channel_id=1, source_target_pairs={{0,8},{1,65},{2,10},{3,67},{4,12},{5,69},{6,14},{7,71},{8,0},{9,73... | collective-permute-start | bytes 589832 | tf_op jit(solution)/shard_map/ppermute | solution.py:38
  13.3 8.6 %collective-permute-start.2 = (bf16[2,64,768]{2,1,0:T(8,128)(2,1)S(1)}, bf16[2,64,768]{2,1,0:T(8,128)(2,1)S(1)}, u32[]{:S(2)}, u32[]{:S(2)}) collective-permute-start(bf16[2,64,768]{2,1,0:T(8,128)(2,1)S(1)} %pad_maximum_fusion.2), channel_id=1, source_target_pairs={{0,12},{1,97},{2,14},{3,99},{4,0},{5,101},{6,2},{7,103},{8,4},{9,1... | collective-permute-start | bytes 589832 | tf_op jit(solution)/shard_map/ppermute | solution.py:38
  14.3 6.9 %collective-permute-start.1 = (bf16[2,64,768]{2,1,0:T(8,128)(2,1)S(1)}, bf16[2,64,768]{2,1,0:T(8,128)(2,1)S(1)}, u32[]{:S(2)}, u32[]{:S(2)}) collective-permute-start(bf16[2,64,768]{2,1,0:T(8,128)(2,1)S(1)} %pad_maximum_fusion.2), channel_id=1, source_target_pairs={{0,4},{1,33},{2,6},{3,35},{4,8},{5,37},{6,10},{7,39},{8,12},{9,41}... | collective-permute-start | bytes 589832 | tf_op jit(solution)/shard_map/ppermute | solution.py:38
  23.3 12.6 %collective-permute-start.7 = (bf16[8,64,768]{2,1,0:T(8,128)(2,1)}, bf16[8,64,768]{2,1,0:T(8,128)(2,1)S(1)}, u32[]{:S(2)}, u32[]{:S(2)}) collective-permute-start(bf16[8,64,768]{2,1,0:T(8,128)(2,1)} %constant_dynamic-update-slice_fusion.m0), channel_id=1, source_target_pairs={{0,96},{1,13},{2,98},{3,15},{4,100},{5,1},{6,102},{7,3},{8,104},{9... | collective-permute-start | bytes 2359304 | tf_op jit(solution)/shard_map/ppermute | solution.py:38
  26.0 13.5 %collective-permute-start.5 = (bf16[8,64,768]{2,1,0:T(8,128)(2,1)}, bf16[8,64,768]{2,1,0:T(8,128)(2,1)S(1)}, u32[]{:S(2)}, u32[]{:S(2)}) collective-permute-start(bf16[8,64,768]{2,1,0:T(8,128)(2,1)} %constant_dynamic-update-slice_fusion.m0), channel_id=1, source_target_pairs={{0,32},{1,5},{2,34},{3,7},{4,36},{5,9},{6,38},{7,11},{8,40},{9,13}... | collective-permute-start | bytes 2359304 | tf_op jit(solution)/shard_map/ppermute | solution.py:38
  26.0 22.7 %collective-permute-start.9 = (bf16[2,2,17,32,128]{4,3,2,1,0:T(8,128)(2,1)S(1)}, bf16[2,2,17,32,128]{4,3,2,1,0:T(8,128)(2,1)S(1)}, u32[]{:S(2)}, u32[]{:S(2)}) collective-permute-start(bf16[2,2,17,32,128]{4,3,2,1,0:T(8,128)(2,1)S(1)} %pad_maximum_fusion.1.a_ref), channel_id=1, source_target_pairs={{0,2},{1,3},{2,0},{3,1},{4,6},{5,7},{6,4},{7,5},{8,10},{9,11},{10,... | collective-permute-start | bytes 1671176 | tf_op jit(solution)/shard_map/ppermute | solution.py:38
  35.9 9.0 %collective-permute-start.8 = (bf16[4,64,768]{2,1,0:T(8,128)(2,1)S(1)}, bf16[4,64,768]{2,1,0:T(8,128)(2,1)S(1)}, u32[]{:S(2)}, u32[]{:S(2)}) collective-permute-start(bf16[4,64,768]{2,1,0:T(8,128)(2,1)S(1)} %slice.64), channel_id=1, source_target_pairs={{0,96},{1,13},{2,98},{3,15},{4,100},{5,1},{6,102},{7,3},{8,104},{9... | collective-permute-start | bytes 1179656 | tf_op jit(solution)/shard_map/ppermute | solution.py:38
  39.6 9.1 %collective-permute-start.6 = (bf16[4,64,768]{2,1,0:T(8,128)(2,1)S(1)}, bf16[4,64,768]{2,1,0:T(8,128)(2,1)S(1)}, u32[]{:S(2)}, u32[]{:S(2)}) collective-permute-start(bf16[4,64,768]{2,1,0:T(8,128)(2,1)S(1)} %slice.50), channel_id=1, source_target_pairs={{0,32},{1,5},{2,34},{3,7},{4,36},{5,9},{6,38},{7,11},{8,40},{9,13}... | collective-permute-start | bytes 1179656 | tf_op jit(solution)/shard_map/ppermute | solution.py:38
  40.6 9.4 %collective-permute-start.10 = (bf16[8,64,768]{2,1,0:T(8,128)(2,1)}, bf16[8,64,768]{2,1,0:T(8,128)(2,1)}, u32[]{:S(2)}, u32[]{:S(2)}) collective-permute-start(bf16[8,64,768]{2,1,0:T(8,128)(2,1)} %constant_dynamic-update-slice_fusion.m0), channel_id=1, source_target_pairs={{0,1},{1,0},{2,3},{3,2},{4,5},{5,4},{6,7},{7,6},{8,9},{9,8},{10,11... | collective-permute-start | bytes 2359304 | tf_op jit(solution)/shard_map/ppermute | solution.py:38
  40.6 9.4 %collective-permute-start.11 = (bf16[8,64,768]{2,1,0:T(8,128)(2,1)S(1)}, bf16[8,64,768]{2,1,0:T(8,128)(2,1)}, u32[]{:S(2)}, u32[]{:S(2)}) collective-permute-start(bf16[8,64,768]{2,1,0:T(8,128)(2,1)S(1)} %collective-permute-done.5.m1), channel_id=1, source_target_pairs={{0,1},{1,0},{2,3},{3,2},{4,5},{5,4},{6,7},{7,6},{8,9},{9,8},{10,11... | collective-permute-start | bytes 2359304 | tf_op jit(solution)/shard_map/ppermute | solution.py:38
  44.8 5.2 %collective-permute-start.12 = (bf16[8,64,768]{2,1,0:T(8,128)(2,1)S(1)}, bf16[8,64,768]{2,1,0:T(8,128)(2,1)}, u32[]{:S(2)}, u32[]{:S(2)}) collective-permute-start(bf16[8,64,768]{2,1,0:T(8,128)(2,1)S(1)} %collective-permute-done.7.m2), channel_id=1, source_target_pairs={{0,1},{1,0},{2,3},{3,2},{4,5},{5,4},{6,7},{7,6},{8,9},{9,8},{10,11... | collective-permute-start | bytes 2359304 | tf_op jit(solution)/shard_map/ppermute | solution.py:38
  74.9 10.5 %collective-permute-start.15 = (bf16[17,32,256]{2,1,0:T(8,128)(2,1)S(1)}, bf16[17,32,256]{2,1,0:T(8,128)(2,1)S(1)}, u32[]{:S(2)}, u32[]{:S(2)}) collective-permute-start(bf16[17,32,256]{2,1,0:T(8,128)(2,1)S(1)} %add_convert_fusion), channel_id=1, source_target_pairs={{0,2},{1,3},{2,0},{3,1},{4,6},{5,7},{6,4},{7,5},{8,10},{9,11},{10,... | collective-permute-start | bytes 835592 | tf_op jit(solution)/shard_map/ppermute | solution.py:38
  96.4 2.7 %collective-permute-start.17 = (f32[64,32,128]{2,1,0:T(8,128)S(1)}, f32[64,32,128]{2,1,0:T(8,128)S(1)}, u32[]{:S(2)}, u32[]{:S(2)}) collective-permute-start(f32[64,32,128]{2,1,0:T(8,128)S(1)} %get-tuple-element.27), channel_id=1, source_target_pairs={{0,1},{1,0},{2,3},{3,2},{4,5},{5,4},{6,7},{7,6},{8,9},{9,8},{10,11... | collective-permute-start | bytes 3145736 | tf_op jit(solution)/shard_map/ppermute | solution.py:38
  99.5 11.1 %collective-permute-start.20 = (f32[4,4,32,128]{3,2,1,0:T(8,128)S(1)}, f32[4,4,32,128]{3,2,1,0:T(8,128)S(1)}, u32[]{:S(2)}, u32[]{:S(2)}) collective-permute-start(f32[4,4,32,128]{3,2,1,0:T(8,128)S(1)} %bitcast.67), channel_id=1, source_target_pairs={{0,8},{1,65},{2,10},{3,67},{4,12},{5,69},{6,14},{7,71},{8,0},{9,73... | collective-permute-start | bytes 786440 | tf_op jit(solution)/shard_map/ppermute | solution.py:38
  100.9 9.7 %collective-permute-start.18 = (f32[4,4,32,128]{3,2,1,0:T(8,128)S(1)}, f32[4,4,32,128]{3,2,1,0:T(8,128)S(1)}, u32[]{:S(2)}, u32[]{:S(2)}) collective-permute-start(f32[4,4,32,128]{3,2,1,0:T(8,128)S(1)} %bitcast.66), channel_id=1, source_target_pairs={{0,4},{1,33},{2,6},{3,35},{4,8},{5,37},{6,10},{7,39},{8,12},{9,41}... | collective-permute-start | bytes 786440 | tf_op jit(solution)/shard_map/ppermute | solution.py:38
  100.9 9.7 %collective-permute-start.19 = (f32[4,4,32,128]{3,2,1,0:T(8,128)S(1)}, f32[4,4,32,128]{3,2,1,0:T(8,128)S(1)}, u32[]{:S(2)}, u32[]{:S(2)}) collective-permute-start(f32[4,4,32,128]{3,2,1,0:T(8,128)S(1)} %bitcast.65), channel_id=1, source_target_pairs={{0,12},{1,97},{2,14},{3,99},{4,0},{5,101},{6,2},{7,103},{8,4},{9,1... | collective-permute-start | bytes 786440 | tf_op jit(solution)/shard_map/ppermute | solution.py:38
  110.7 6.2 %collective-permute-start.21 = (f32[4,32,128]{2,1,0:T(8,128)S(1)}, f32[4,32,128]{2,1,0:T(8,128)S(1)}, u32[]{:S(2)}, u32[]{:S(2)}) collective-permute-start(f32[4,32,128]{2,1,0:T(8,128)S(1)} %get-tuple-element.44), channel_id=1, source_target_pairs={{0,32},{1,5},{2,34},{3,7},{4,36},{5,9},{6,38},{7,11},{8,40},{9,13}... | collective-permute-start | bytes 196616 | tf_op jit(solution)/shard_map/ppermute | solution.py:38
  110.8 6.2 %collective-permute-start.23 = (f32[4,32,128]{2,1,0:T(8,128)S(1)}, f32[4,32,128]{2,1,0:T(8,128)S(1)}, u32[]{:S(2)}, u32[]{:S(2)}) collective-permute-start(f32[4,32,128]{2,1,0:T(8,128)S(1)} %get-tuple-element.45), channel_id=1, source_target_pairs={{0,64},{1,9},{2,66},{3,11},{4,68},{5,13},{6,70},{7,15},{8,72},{9,1... | collective-permute-start | bytes 196616 | tf_op jit(solution)/shard_map/ppermute | solution.py:38
  112.5 5.3 %collective-permute-start.22 = (f32[4,32,128]{2,1,0:T(8,128)S(1)}, f32[4,32,128]{2,1,0:T(8,128)S(1)}, u32[]{:S(2)}, u32[]{:S(2)}) collective-permute-start(f32[4,32,128]{2,1,0:T(8,128)S(1)} %get-tuple-element.46), channel_id=1, source_target_pairs={{0,96},{1,13},{2,98},{3,15},{4,100},{5,1},{6,102},{7,3},{8,104},{9... | collective-permute-start | bytes 196616 | tf_op jit(solution)/shard_map/ppermute | solution.py:38
  117.8 6.1 %collective-permute-start.24 = (f32[32,128]{1,0:T(8,128)S(1)}, f32[32,128]{1,0:T(8,128)S(1)}, u32[]{:S(2)}, u32[]{:S(2)}) collective-permute-start(f32[32,128]{1,0:T(8,128)S(1)} %get-tuple-element.47), channel_id=1, source_target_pairs={{0,16},{1,17},{2,18},{3,19},{4,20},{5,21},{6,22},{7,23},{8,24},{9,... | collective-permute-start | bytes 49160 | tf_op jit(solution)/shard_map/ppermute | solution.py:38
  118.0 5.9 %collective-permute-start.26 = (f32[32,128]{1,0:T(8,128)S(1)}, f32[32,128]{1,0:T(8,128)S(1)}, u32[]{:S(2)}, u32[]{:S(2)}) collective-permute-start(f32[32,128]{1,0:T(8,128)S(1)} %get-tuple-element.48), channel_id=1, source_target_pairs={{0,2},{1,3},{2,0},{3,1},{4,6},{5,7},{6,4},{7,5},{8,10},{9,11},{10,... | collective-permute-start | bytes 49160 | tf_op jit(solution)/shard_map/ppermute | solution.py:38
  121.4 3.7 %collective-permute-start.25 = (f32[32,128]{1,0:T(8,128)S(1)}, f32[32,128]{1,0:T(8,128)S(1)}, u32[]{:S(2)}, u32[]{:S(2)}) collective-permute-start(f32[32,128]{1,0:T(8,128)S(1)} %get-tuple-element.49), channel_id=1, source_target_pairs={{0,18},{1,19},{2,16},{3,17},{4,22},{5,23},{6,20},{7,21},{8,26},{9,... | collective-permute-start | bytes 49160 | tf_op jit(solution)/shard_map/ppermute | solution.py:38
  (15 other events, 84.9 us)

commit v3 on v2

--- a/solution.py
+++ b/solution.py
@@ -13,6 +13,9 @@
 TILE = 256
 PER_TILE = TILE // HALF
 TILES = 17
+NEAR = 18 * 4
+FAR = 8 * 4
+SLOT, GOAL, ROW, ROW_OTHER, POSITION, COUNT = 0, 128, 256, 320, 384, 448
 MLA_SCALE = 192.0**-0.5
 LOSS_SCALE = 64.0
 NT = (((1,), (1,)), ((), ()))
@@ -76,12 +79,43 @@
     return half, step - half * meta[0]
 
 
-def pack_kernel(q_ref, n_ref, out):
+def plan_kernel(meta, order, slot, row, row_other, plan):
+    ends = (jnp.int32(0), jnp.int32(NEAR))
+    for half in range(2):
+        limit = meta[2 + half]
+
+        def step(i, ends, half=half, limit=limit):
+            near, far = ends
+            position, at = order[i], slot[i]
+            if half == 0:
+                plan[ROW + position] = row[i]
+                plan[ROW_OTHER + position] = row_other[i]
+                plan[POSITION + at] = position
+            is_far = jnp.where((at // 8) % 4 == 3, 1, 0)
+            seen = jnp.where(position <= limit, 1, 0)
+            to = jnp.where(seen == 1, jnp.where(is_far == 1, far, near), NEAR + FAR)
+            plan[SLOT + to] = at
+            plan[GOAL + to] = position + half * PER_TILE * meta[0]
+            return near + seen * (1 - is_far), far + seen * is_far
+
+        ends = lax.fori_loop(0, 64, step, ends, unroll=4)
+        for part, end in enumerate(ends):
+            for u in range(3):
+                plan[SLOT + end + u] = 24 * part
+                plan[GOAL + end + u] = 68
+        ends = ((ends[0] + 3) // 4 * 4, (ends[1] + 3) // 4 * 4)
+        plan[COUNT + 2 * half] = ends[0] // 4
+        plan[COUNT + 2 * half + 1] = (ends[1] - NEAR) // 4
+
+
+def pack_kernel(q_ref, n_ref, packed, token, out, sems):
+    token[...] = jnp.zeros(token.shape, jnp.int32)
     n = n_ref[...] * -math.sqrt(192.0)
     n1 = n.astype(jnp.bfloat16).astype(jnp.float32)
     n2 = (n - n1).astype(jnp.bfloat16).astype(jnp.float32)
     n3 = n - n1 - n2
     row = lax.broadcasted_iota(jnp.int32, (64, 128), 0)
+    copies = []
     for i in range(16):
         lanes = slice(i * 128, (i + 1) * 128)
         a, b = q_ref[2 * i], q_ref[2 * i + 1]
@@ -95,34 +129,50 @@
             ]
             block = jnp.where(row == 0, parts[0], jnp.where(row == 1, parts[1], jnp.where(row == 2, parts[2], 0.0)))
             out[half, 576:640, lanes] = block.astype(jnp.bfloat16)
-
-
-def target_kernel(meta, loc, q_ref, m0, m1, m2, m3, s0, s1, s2, s3, keep, other, sorted_ref, keys, sems):
+        if i % 4 == 3:
+            at = pl.ds((i - 3) * 128, 512)
+            copies.append(pltpu.make_async_copy(out.at[:, :, at], packed.at[:, :, at], sems.at[i // 4]))
+            copies[-1].start()
+    for copy in copies:
+        copy.wait()
+
+
+def target_kernel(part, unread, meta, plan, q_ref, *refs):
+    count = 3 - part
+    groups, refs = (refs[0:count], refs[count : 2 * count]), refs[2 * count :]
+    if part == 0:
+        sums, sorted_ref, token, keys, sems = refs[unread:]
+        token[...] = jnp.zeros(token.shape, jnp.int32)
+    else:
+        sums, sorted_ref, keep, other, keys, sems = refs[2 + unread :]
     core = meta[1]
+    size = 4 if part else 8
     copies = []
-    for side, group in enumerate(((m0, m1, m2, m3), (s0, s1, s2, s3))):
+    for side, group in enumerate(groups):
         owner = core if side == 0 else 1 - core
         for j, ref in enumerate(group):
-            copies.append(
-                pltpu.make_async_copy(ref, keys.at[pl.ds(owner * 32 + j * 8, 8)], sems.at[side * 4 + j])
-            )
+            at = owner * 32 + 24 * part + j * size
+            copies.append(pltpu.make_async_copy(ref, keys.at[pl.ds(at, size)], sems.at[side * count + j]))
     for copy in copies:
         copy.start()
     for copy in copies:
         copy.wait()
-
-    def sort(p, _):
-        sorted_ref[pl.ds(pl.multiple_of(p * HALF, HALF), HALF), :] = keys[loc[p], :, 640:768]
-        return 0
-
-    lax.fori_loop(0, 64, sort, 0, unroll=4)
+    for owner in range(2):
+
+        def sort(i, _, owner=owner):
+            slot = owner * 32 + i
+            at = pl.multiple_of(plan[POSITION + slot] * HALF, HALF)
+            sorted_ref[pl.ds(at, HALF), :] = keys[slot, :, 640:768]
+            return 0
+
+        lax.fori_loop(24 * part, 24 + 8 * part, sort, 0, unroll=4)
     scale = MLA_SCALE * math.log2(math.e)
-
-    def body(step, _):
-        half, ktile = place(meta, step)
-        tile = jnp.concatenate(
-            [keys[loc[ktile * PER_TILE + u], :, 0:640] for u in range(PER_TILE)], axis=0
-        )
+    first, tiles = plan[COUNT + part], plan[COUNT + 2 + part]
+
+    def body(t):
+        half = jnp.where(t >= first, 1, 0)
+        at = part * NEAR + t * PER_TILE
+        tile = jnp.concatenate([keys[plan[SLOT + at + u], :, 0:640] for u in range(PER_TILE)], axis=0)
         total = jnp.zeros((TILE, 128), jnp.float32)
         for g in range(8):
             s = lax.dot_general(
@@ -130,14 +180,31 @@
             )
             e = jnp.exp2(s * scale)
             total = total + (e[:, 0:128] + e[:, 128:256])
-        total = total.T
-        total = total[0:64] + total[64:128]
-        top, low = total[0:32], total[32:64]
-        keep[step] = jnp.where(core == 0, top, low)
-        other[step] = jnp.where(core == 0, low, top)
-        return 0
-
-    lax.fori_loop(0, TILES, body, 0, unroll=4)
+        for u in range(PER_TILE):
+            sums[plan[GOAL + at + u]] = total[u * HALF : (u + 1) * HALF]
+
+    def pair(i, _):
+        body(2 * i)
+        body(2 * i + 1)
+        return 0
+
+    lax.fori_loop(0, tiles // 2, pair, 0)
+
+    @pl.when(tiles % 2 == 1)
+    def _():
+        body(tiles - 1)
+
+    if part == 1:
+
+        def fold(step, _):
+            total = sums[pl.ds(step * PER_TILE, PER_TILE)].reshape(TILE, 128).T
+            total = total[0:64] + total[64:128]
+            top, low = total[0:32], total[32:64]
+            keep[step] = jnp.where(core == 0, top, low)
+            other[step] = jnp.where(core == 0, low, top)
+            return 0
+
+        lax.fori_loop(0, TILES, fold, 0, unroll=4)
 
 
 def visible_of(meta, half, ktile):
@@ -242,7 +309,7 @@
     return half, ktile, tile, found
 
 
-def key_kernel(idx_scale, meta, stored, g_ref, h_ref, iq_ref, iqt_ref, key_ref, keep, other, wide):
+def key_kernel(idx_scale, meta, plan, g_ref, h_ref, iq_ref, iqt_ref, key_ref, keep, other, wide):
     core = meta[1]
     spread(iq_ref, wide, idx_scale)
     keep[...] = jnp.zeros(keep.shape, jnp.float32)
@@ -255,7 +322,7 @@
         )
         dk = dkt.T
         for u in range(PER_TILE):
-            slot, slot_other = stored[ktile * PER_TILE + u], stored[64 + ktile * PER_TILE + u]
+            slot, slot_other = plan[ROW + ktile * PER_TILE + u], plan[ROW_OTHER + ktile * PER_TILE + u]
             first, last = dk[u * 64 : u * 64 + 32], dk[u * 64 + 32 : u * 64 + 64]
             keep[slot] = keep[slot] + jnp.where(core == 0, first, last)
             other[slot_other] = other[slot_other] + jnp.where(core == 0, last, first)
@@ -264,7 +331,8 @@
     lax.fori_loop(0, TILES, body, 0, unroll=4)
 
 
-def query_kernel(idx_scale, meta, g_ref, h_ref, iq_ref, key_ref, dq, wide):
+def query_kernel(idx_scale, meta, g_ref, h_ref, iq_ref, key_ref, dq, token, wide):
+    token[...] = jnp.zeros(token.shape, jnp.int32)
     spread(iq_ref, wide, idx_scale)
     dq[...] = jnp.zeros(dq.shape, jnp.float32)
 
@@ -293,6 +361,34 @@
     x, zl, y = ctx // 8, (ctx // 4) % 2, ctx % 4
     core = head % 2
 
+    small = pl.CostEstimate(flops=1_000_000, bytes_accessed=1_000_000, transcendentals=0)
+    flag = jax.ShapeDtypeStruct((8, 128), jnp.int32)
+
+    index = jnp.arange(64, dtype=jnp.int32)
+    bc, bk = index // 2, index % 2
+    bx, bz, by = bc // 8, (bc // 4) % 2, bc % 4
+
+    def ring_slot(rel):
+        return jnp.where(rel == 0, 0, jnp.where(rel == 3, 1, jnp.where(rel == 1, 2, 3)))
+
+    rx, ry = ring_slot((bx - x) % 4), ring_slot((by - y) % 4)
+    rz = (bz != zl).astype(jnp.int32)
+    slot = bk * 32 + jnp.where(bk == 0, rx * 8 + ry * 2, ry * 8 + rx * 2) + rz
+    blocks = lax.dynamic_slice_in_dim(block_order, ctx * 2, 2, 0)
+    qx, qy = (bx - x) % 4, (by - y) % 4
+    qz = (2 * bk + bz - 2 * (head // 2) - zl) % 4
+    row_a, row_b = qy * 16 + qx * 4 + qz, qx * 16 + qy * 4 + qz
+    row_a, row_b = jnp.where(core == 0, row_a, row_b), jnp.where(core == 0, row_b, row_a)
+    meta = jnp.concatenate(((blocks[0:1] + PER_TILE) // PER_TILE, core[None], blocks)).astype(jnp.int32)
+    plan = pl.pallas_call(
+        plan_kernel,
+        out_shape=jax.ShapeDtypeStruct((512,), jnp.int32),
+        in_specs=[smem()] * 5,
+        out_specs=smem(),
+        cost_estimate=small,
+        name="plan",
+    )(meta, block_order, slot, row_a, row_b)
+
     ones = (lax.broadcasted_iota(jnp.int32, (128, 64), 1) < 3).astype(bf16)
     packed = jnp.concatenate((key_latent, ones, indexer_key), axis=1)
     own = lax.dynamic_slice_in_dim(packed, core * HALF, HALF, 0)
@@ -300,13 +396,14 @@
     pair = jnp.stack((own, beside))
     legs = [pair] + [send(pair, along(True, shift)) for shift in (1, 3, 2)]
     group = jnp.concatenate(legs, axis=0)
-    query = pl.pallas_call(
+    query, token = pl.pallas_call(
         pack_kernel,
-        out_shape=jax.ShapeDtypeStruct((2, 640, 2048), bf16),
+        out_shape=(jax.ShapeDtypeStruct((2, 640, 2048), bf16), flag),
         in_specs=[vmem(), vmem()],
-        out_specs=vmem(),
+        out_specs=(pl.BlockSpec(memory_space=pltpu.HBM), vmem()),
+        scratch_shapes=[pltpu.VMEM((2, 640, 2048), bf16), pltpu.SemaphoreType.DMA((4,))],
         compiler_params=params(8),
-        cost_estimate=pl.CostEstimate(flops=0, bytes_accessed=12_000_000, transcendentals=0),
+        cost_estimate=small,
         name="pack",
     )(query_latent.transpose(1, 2, 0), normalizer.T)
 
@@ -314,53 +411,37 @@
     weight = jnp.pad(indexer_weight.reshape(2, 1, HALF, 16), ((0, 0), (0, 0), (0, 0), (0, 112)))
     iqw = jnp.concatenate((iq, weight), axis=1)
     iqt = iq.transpose(0, 3, 1, 2).reshape(2, 128, 1024)
-    iq_keep = lax.dynamic_slice_in_dim(iqw, core * 32, 32, 2)
-    iq_other = swap_core(lax.dynamic_slice_in_dim(iqw, (1 - core) * 32, 32, 2))
-    iq_chip = jnp.stack((iq_keep, iq_other))
-    group, iq_chip = lax.optimization_barrier((group, iq_chip))
-    iq_far = swap_high(iq_chip)
+    iq_high = swap_high(iqw)
+    group, iq_flag = lax.optimization_barrier((group, iq_high[0, 0, 0:8]))
+    iq_both = jnp.stack((iqw, iq_high))
+    iq_keep = lax.dynamic_slice_in_dim(iq_both, core * 32, 32, 3)
+    iq_other = swap_core(lax.dynamic_slice_in_dim(iq_both, (1 - core) * 32, 32, 3))
 
     up, down = send(group, along(False, 1)), send(group, along(False, 3))
-    up, query = lax.optimization_barrier((up, query))
-    far_a = send(up[0:4], along(False, 1))
-    far_b = send(down[4:8], along(False, 3))
-    far = jnp.concatenate((far_a, far_b), axis=0)
-    far, iq_far, iqt = lax.optimization_barrier((far, iq_far, iqt))
-    mine = [group, up, down, far]
-    swapped = [swap_core(v) for v in mine]
-
-    index = jnp.arange(64, dtype=jnp.int32)
-    bc, bk = index // 2, index % 2
-    bx, bz, by = bc // 8, (bc // 4) % 2, bc % 4
-
-    def ring_slot(rel):
-        return jnp.where(rel == 0, 0, jnp.where(rel == 3, 1, jnp.where(rel == 1, 2, 3)))
-
-    rx, ry = ring_slot((bx - x) % 4), ring_slot((by - y) % 4)
-    rz = (bz != zl).astype(jnp.int32)
-    slot = bk * 32 + jnp.where(bk == 0, rx * 8 + ry * 2, ry * 8 + rx * 2) + rz
-    hit = (block_order[None, :] == index[:, None]).astype(jnp.int32)
-    loc = jnp.sum(hit * slot[None, :], axis=1)
-    blocks = lax.dynamic_slice_in_dim(block_order, ctx * 2, 2, 0)
-    qx, qy = (bx - x) % 4, (by - y) % 4
-    qz = (2 * bk + bz - 2 * (head // 2) - zl) % 4
-    row_a, row_b = qy * 16 + qx * 4 + qz, qx * 16 + qy * 4 + qz
-    row_a, row_b = jnp.where(core == 0, row_a, row_b), jnp.where(core == 0, row_b, row_a)
-    stored = jnp.concatenate((jnp.sum(hit * row_a[None, :], axis=1), jnp.sum(hit * row_b[None, :], axis=1)))
-    meta = jnp.concatenate(((blocks[0:1] + PER_TILE) // PER_TILE, core[None], blocks)).astype(jnp.int32)
+    up, token, plan = lax.optimization_barrier((up, token, plan))
+    far_a, far_b = send(up[0:4], along(False, 1)), send(down[4:8], along(False, 3))
+    near = [group, up, down]
+    near = near + [swap_core(v) for v in near]
 
     part = jax.ShapeDtypeStruct((TILES, 32, TILE), f32)
-    keep, other, sorted_keys = pl.pallas_call(
-        target_kernel,
-        out_shape=(part, part, jax.ShapeDtypeStruct((4096, 128), bf16)),
-        in_specs=[smem(), smem(), vmem()] + [anywhere()] * 8,
-        out_specs=(vmem(), vmem(), vmem()),
-        scratch_shapes=[pltpu.VMEM((64, HALF, 768), bf16), pltpu.SemaphoreType.DMA((8,))],
-        compiler_params=params(16),
-        cost_estimate=pl.CostEstimate(flops=12_000_000_000, bytes_accessed=14_000_000, transcendentals=9_000_000),
-        name="targets",
-    )(meta, loc, query, *mine, *swapped)
-
+    def targets(stage, outs, after, *arrays):
+        reads = 6 - 2 * stage
+        return pl.pallas_call(
+            functools.partial(target_kernel, stage, len(after)),
+            out_shape=(jax.ShapeDtypeStruct((69, HALF, 128), f32), jax.ShapeDtypeStruct((4096, 128), bf16)) + outs,
+            in_specs=[smem(), smem(), vmem()] + [anywhere()] * reads + [vmem()] * (2 * stage) + [anywhere()] * len(after),
+            out_specs=(vmem(),) * (2 + len(outs)),
+            scratch_shapes=[pltpu.VMEM((64, HALF, 768), bf16), pltpu.SemaphoreType.DMA((reads,))],
+            input_output_aliases={3 + reads: 0, 4 + reads: 1} if stage else {},
+            compiler_params=params(14),
+            cost_estimate=small,
+            name="targets_far" if stage else "targets_near",
+        )(meta, plan, query, *arrays, *after)
+
+    sums, sorted_keys, token = targets(0, (flag,), (iq_flag, token, iq_other), *near)
+    far_a, far_b, token = lax.optimization_barrier((far_a, far_b, token))
+    far = (far_a, far_b, swap_core(far_a), swap_core(far_b))
+    _, sorted_keys, keep, other = targets(1, (part, part), (token,), *far, sums, sorted_keys)
     from_core = swap_core(other)
     from_high = swap_high((keep + from_core).astype(bf16))
 
@@ -375,9 +456,9 @@
             pltpu.VMEM((2, 32, TILE), f32),
         ],
         compiler_params=params(12),
-        cost_estimate=pl.CostEstimate(flops=5_000_000_000, bytes_accessed=4_000_000, transcendentals=200_000),
+        cost_estimate=small,
         name="logits",
-    )(meta, iq_chip, iq_far, sorted_keys)
+    )(meta, iq_keep, iq_other, sorted_keys)
 
     grad = pl.pallas_call(
         gradient_kernel,
@@ -386,12 +467,12 @@
         out_specs=vmem(),
         scratch_shapes=[pltpu.VMEM((TILES, 32, TILE), f32), pltpu.VMEM((2, 32, TILE), f32)],
         compiler_params=params(8),
+        cost_estimate=small,
         name="gradient",
     )(meta, prob, keep, from_core, from_high)
     grad_other = swap_core(grad)
 
     shard = jax.ShapeDtypeStruct((64, 32, 128), f32)
-    cost = pl.CostEstimate(flops=5_000_000_000, bytes_accessed=4_000_000, transcendentals=0)
     dk_keep, dk_other = pl.pallas_call(
         functools.partial(key_kernel, idx_scale),
         out_shape=(shard, shard),
@@ -399,27 +480,27 @@
         out_specs=(vmem(), vmem()),
         scratch_shapes=[pltpu.VMEM((2, 1024, 128), f32)],
         compiler_params=params(12),
-        cost_estimate=cost,
+        cost_estimate=small,
         name="keys",
-    )(meta, stored, grad, grad_other, iqw, iqt, sorted_keys)
-    dq = pl.pallas_call(
+    )(meta, plan, grad, grad_other, iqw, iqt, sorted_keys)
+    dq, token = pl.pallas_call(
         functools.partial(query_kernel, idx_scale),
-        out_shape=jax.ShapeDtypeStruct((2, 1024, 128), f32),
+        out_shape=(jax.ShapeDtypeStruct((2, 1024, 128), f32), flag),
         in_specs=[smem()] + [vmem()] * 4,
-        out_specs=vmem(),
+        out_specs=(vmem(), vmem()),
         scratch_shapes=[pltpu.VMEM((2, 1024, 128), f32)],
         compiler_params=params(12),
-        cost_estimate=cost,
+        cost_estimate=small,
         name="queries",
     )(meta, grad, grad_other, iqw, sorted_keys)
 
     dk = dk_keep + swap_core(dk_other)
     dk = ring_sum(dk.reshape(4, 4, 4, 32, 128), functools.partial(along, True))
-    dk, dq = lax.optimization_barrier((dk, dq))
+    dk, token = lax.optimization_barrier((dk, token))
     dk = ring_sum(dk, functools.partial(along, False))
     dk = ring_sum(dk, lambda shift: lambda x, z, y, k: (x, z + shift, y, k))
     query_grad = dq.reshape(2, 16, HALF, 128).transpose(0, 2, 1, 3).reshape(128, 16, 128)
-    return query_grad, dk
+    return query_grad, dk + token[0:1].astype(f32)
 
 
 def solution(mesh):

time: 126 us -> 128 us (1.016)
  waiting for transfers between devices: 32 us -> 19.9 us
  Pallas kernels: 41.9 us -> 48.4 us
  other arithmetic: 2.93 us -> 6.63 us
  starting transfers between devices: 33.1 us -> 36 us
    ppermute x27 -> x28, waiting for transfers between devices: 32 us -> 19.9 us  [send(): return lax.ppermute(value, ALL, permutation(move))]
    pallas_call x3 -> x5, Pallas kernels: 26.2 us -> 32.7 us  [the longest x2 20.5 us: targets(): pl.pallas_call(functools.partial(target_kernel, stage, len(after)), out_s...]
    ppermute x27 -> x28, starting transfers between devices: 33.1 us -> 36 us  [send(): return lax.ppermute(value, ALL, permutation(move))]
    another operation x1, other arithmetic: 0.05 us -> 2.11 us  [per_device(): iq_both = jnp.stack((iqw, iq_high))]
    unnamed x29 -> x27, local copies, waits for them, and re-layouts: 10.8 us -> 12.3 us
  transfers between devices with their start and end apart: 27 -> 28, of which waited for: 13 -> 15; matrix products, arithmetic and copies ran while one was open for 5% -> 8% of each run, Pallas kernels for 12% -> 26%
where the time goes in v3:
time: 128 us
  Pallas kernels  48.4 us (38%)
  starting transfers between devices  36 us (28%)
  waiting for transfers between devices  19.9 us (16%)
  local copies, waits for them, and re-layouts  16 us (12%)
  other arithmetic  6.63 us (5%)
    ppermute x28, starting transfers between devices, send(): return lax.ppermute(value, ALL, permutation(move))  36 us
    pallas_call x2, Pallas kernels, targets(): pl.pallas_call(functools.partial(target_kernel, stage, len(after)), out_s...  20.5 us
    ppermute x28, waiting for transfers between devices, send(): return lax.ppermute(value, ALL, permutation(move))  19.9 us
    unnamed x27, local copies, waits for them, and re-layouts  12.3 us
    pallas_call x1, Pallas kernels, per_device(): pl.pallas_call(functools.partial(logit_kernel, idx_scale), out_shape=part...  7.44 us
    pallas_call x1, Pallas kernels, per_device(): pl.pallas_call(functools.partial(key_kernel, idx_scale), out_shape=(shard...  7.1 us
    pallas_call x1, Pallas kernels, per_device(): pl.pallas_call(functools.partial(query_kernel, idx_scale), out_shape=(jax...  6.41 us
    pallas_call x1, Pallas kernels, per_device(): pl.pallas_call(plan_kernel, out_shape=jax.ShapeDtypeStruct((512,), jnp.in...  3.35 us
  transfers between devices with their start and end apart: 28, of which 15 were waited for; matrix products, arithmetic and copies ran while one was open for 8% of the time, Pallas kernels for 26%

profile of v3, /device:TPU:0, one launch (start us, length us, event | category | flops | bytes accessed | tf_op | source)
XLA Modules:
  0.0 128.0 jit_solution(4000760831122079986)
XLA Ops:
  3.3 2.0 %collective-permute-start.2 = (bf16[64,768]{1,0:T(8,128)(2,1)S(1)}, bf16[64,768]{1,0:T(8,128)(2,1)S(1)}, u32[]{:S(2)}, u32[]{:S(2)}) collective-permute-start(bf16[64,768]{1,0:T(8,128)(2,1)S(1)} %get-tuple-element.50), channel_id=1, source_target_pairs={{0,16},{1,19},{2,18},{3,17},{4,20},{5,23},{6,22},{7,21},{8,24},{9,... | collective-permute-start | bytes 294920 | tf_op jit(solution)/shard_map/ppermute | solution.py:41
  6.5 3.7 %collective-permute-start = (bf16[2,17,64,128]{3,2,1,0:T(8,128)(2,1)S(1)}, bf16[2,17,64,128]{3,2,1,0:T(8,128)(2,1)}, u32[]{:S(2)}, u32[]{:S(2)}) collective-permute-start(bf16[2,17,64,128]{3,2,1,0:T(8,128)(2,1)S(1)} %get-tuple-element.57.iq_ref), channel_id=1, source_target_pairs={{0,2},{1,3},{2,0},{3,1},{4,6},{5,7},{6,4},{7,5},{8,10},{9,11},{10,... | collective-permute-start | bytes 1671176 | tf_op jit(solution)/shard_map/ppermute | solution.py:41
  11.9 1.7 %collective-permute-start.4 = (bf16[2,64,768]{2,1,0:T(8,128)(2,1)S(1)}, bf16[2,64,768]{2,1,0:T(8,128)(2,1)S(1)}, u32[]{:S(2)}, u32[]{:S(2)}) collective-permute-start(bf16[2,64,768]{2,1,0:T(8,128)(2,1)S(1)} %pad_maximum_fusion), channel_id=1, source_target_pairs={{0,12},{1,97},{2,14},{3,99},{4,0},{5,101},{6,2},{7,103},{8,4},{9,1... | collective-permute-start | bytes 589832 | tf_op jit(solution)/shard_map/ppermute | solution.py:41
  13.5 2.0 %collective-permute-start.5 = (bf16[2,64,768]{2,1,0:T(8,128)(2,1)S(1)}, bf16[2,64,768]{2,1,0:T(8,128)(2,1)S(1)}, u32[]{:S(2)}, u32[]{:S(2)}) collective-permute-start(bf16[2,64,768]{2,1,0:T(8,128)(2,1)S(1)} %pad_maximum_fusion), channel_id=1, source_target_pairs={{0,8},{1,65},{2,10},{3,67},{4,12},{5,69},{6,14},{7,71},{8,0},{9,73... | collective-permute-start | bytes 589832 | tf_op jit(solution)/shard_map/ppermute | solution.py:41
  18.5 2.1 %collective-permute-done.5 = bf16[2,64,768]{2,1,0:T(8,128)(2,1)S(1)} collective-permute-done((bf16[2,64,768]{2,1,0:T(8,128)(2,1)S(1)}, bf16[2,64,768]{2,1,0:T(8,128)(2,1)S(1)}, u32[]{:S(2)}, u32[]{:S(2)}) %collective-permute-start.5) | collective-permute-done | bytes 196640 | tf_op jit(solution)/shard_map/ppermute | solution.py:41
  21.4 1.8 %collective-permute-done = bf16[2,17,64,128]{3,2,1,0:T(8,128)(2,1)} collective-permute-done((bf16[2,17,64,128]{3,2,1,0:T(8,128)(2,1)S(1)}, bf16[2,17,64,128]{3,2,1,0:T(8,128)(2,1)}, u32[]{:S(2)}, u32[]{:S(2)}) %collective-permute-start) | collective-permute-done | bytes 557088 | tf_op jit(solution)/shard_map/ppermute | solution.py:41
  25.3 1.7 %collective-permute-start.8 = (bf16[8,64,768]{2,1,0:T(8,128)(2,1)}, bf16[8,64,768]{2,1,0:T(8,128)(2,1)S(1)}, u32[]{:S(2)}, u32[]{:S(2)}) collective-permute-start(bf16[8,64,768]{2,1,0:T(8,128)(2,1)} %constant_dynamic-update-slice_fusion.refs_0_), channel_id=1, source_target_pairs={{0,96},{1,13},{2,98},{3,15},{4,100},{5,1},{6,102},{7,3},{8,104},{9... | collective-permute-start | bytes 2359304 | tf_op jit(solution)/shard_map/ppermute | solution.py:41
  27.6 2.1 %fusion.2 = (bf16[2,2,17,32,128]{4,3,2,1,0:T(8,128)(2,1)}, bf16[2,2,17,32,128]{4,3,2,1,0:T(8,128)(2,1)S(1)}) fusion(s32[]{:T(128)S(6)} %select_n.137, bf16[1,2,17,64,128]{4,3,2,1,0:T(8,128)(2,1)S(1)} %get-tuple-element.58, bf16[1,2,17,64,128]{4,3,2,1,0:T(8,128)(2,1)} %bitcast.5, s32[]{:T(128)S(6)} %select_n.136), kind=kLoop, calls=%fused_computation.7 | loop fusion | flops 2228224 | bytes 2228232 | tf_op jit(solution)/shard_map/stack | solution.py:416
  30.5 2.3 %copy-done.2 = bf16[128,32,576]{0,2,1:T(8,128)(2,1)S(1)} copy-done((bf16[128,32,576]{0,2,1:T(8,128)(2,1)S(1)}, bf16[128,32,576]{0,2,1:T(8,128)(2,1)}, u32[]{:S(2)}) %copy-start.2) | copy-done | bytes 4718616
  32.9 2.5 %pack.1 = (bf16[2,640,2048]{2,1,0:T(8,128)(2,1)S(1)}, s32[8,128]{1,0:T(8,128)S(1)}) custom-call(bf16[32,576,128]{2,1,0:T(8,128)(2,1)S(1)} %bitcast.59, f32[32,128]{1,0:T(8,128)S(1)} %bitcast.61), custom_call_target="tpu_custom_call" | custom-call | flops 1000000 | bytes 1000000 | tf_op jit(solution)/shard_map/pack/pallas_call | solution.py:399
  35.3 2.3 %copy-done = bf16[2,640,2048]{2,1,0:T(8,128)(2,1)} copy-done((bf16[2,640,2048]{2,1,0:T(8,128)(2,1)}, bf16[2,640,2048]{2,1,0:T(8,128)(2,1)S(1)}, u32[]{:S(2)}) %copy-start) | copy-done | bytes 5242904
  38.3 3.3 %plan.1 = s32[512]{0:T(512)} custom-call(s32[4]{0:T(128)} %pad_add_fusion.meta, s32[64]{0:T(128)} %order.1, s32[64]{0:T(128)} %get-tuple-element.66.slot, s32[64]{0:T(128)} %get-tuple-element.65.row, s32[64]{0:T(128)} %get-tuple-element.46.row_other), custom_call_target="tpu_custom_call" | custom-call | flops 1000000 | bytes 1000000 | tf_op jit(solution)/shard_map/plan/pallas_call | solution.py:383
  43.9 2.3 %collective-permute-start.9 = (bf16[4,64,768]{2,1,0:T(8,128)(2,1)S(1)}, bf16[4,64,768]{2,1,0:T(8,128)(2,1)S(1)}, u32[]{:S(2)}, u32[]{:S(2)}) collective-permute-start(bf16[4,64,768]{2,1,0:T(8,128)(2,1)S(1)} %slice.73), channel_id=1, source_target_pairs={{0,96},{1,13},{2,98},{3,15},{4,100},{5,1},{6,102},{7,3},{8,104},{9... | collective-permute-start | bytes 1179656 | tf_op jit(solution)/shard_map/ppermute | solution.py:41
  46.4 2.5 %copy-done.1 = bf16[2,640,2048]{2,1,0:T(8,128)(2,1)S(1)} copy-done((bf16[2,640,2048]{2,1,0:T(8,128)(2,1)S(1)}, bf16[2,640,2048]{2,1,0:T(8,128)(2,1)}, u32[]{:S(2)}) %copy-start.1) | copy-done | bytes 5242904
  50.0 13.2 %targets_near.1 = (f32[69,64,128]{2,1,0:T(8,128)S(1)}, bf16[4096,128]{1,0:T(8,128)(2,1)S(1)}, s32[8,128]{1,0:T(8,128)S(1)}) custom-call(s32[4]{0:T(128)S(1)} %copy-done.6, s32[512]{0:T(512)S(1)} %copy-done.5, bf16[2,640,2048]{2,1,0:T(8,128)(2,1)S(1)} %copy-done.1, bf16[8,64,768]{2,1,0:T(8,128)(2,1)} %constant_dynamic-update-slice_fusion.refs_0_, ...), custom_call_target="tpu_custom_call" | custom-call | flops 1000000 | bytes 1000000 | tf_op jit(solution)/shard_map/targets_near/pallas_call | solution.py:429
  65.6 7.3 %targets_far.1 = (f32[69,64,128]{2,1,0:T(8,128)S(1)}, bf16[4096,128]{1,0:T(8,128)(2,1)S(1)}, f32[17,32,256]{2,1,0:T(8,128)S(1)}, f32[17,32,256]{2,1,0:T(8,128)S(1)}) custom-call(s32[4]{0:T(128)S(1)} %copy-done.6, s32[512]{0:T(512)S(1)} %copy-done.5, bf16[2,640,2048]{2,1,0:T(8,128)(2,1)S(1)} %copy-done.1, ...), custom_call_target="tpu_custom_call", output_to_operand_aliasing={{0}: (7, {}), {1}: (8, {})} | custom-call | flops 1000000 | bytes 1000000 | tf_op jit(solution)/shard_map/targets_far/pallas_call | solution.py:429
  76.7 7.4 %logits.1.p_ref = f32[17,32,256]{2,1,0:T(8,128)S(1)} custom-call(s32[4]{0:T(128)S(1)} %copy-done.6, bf16[2,2,17,32,128]{4,3,2,1,0:T(8,128)(2,1)S(1)} %get-tuple-element.52.a_ref, bf16[2,2,17,32,128]{4,3,2,1,0:T(8,128)(2,1)S(1)} %collective-permute-done.1.refs_8_.b_ref, bf16[4096,128]{1,0:T(8,128)(2,1)S(1)} %get-tuple-element.37.key_ref), custom_call_target="tpu_custom_call" | custom-call | flops 1000000 | bytes 1000000 | tf_op jit(solution)/shard_map/logits/pallas_call | solution.py:448
  88.4 7.1 %keys.1 = (f32[64,32,128]{2,1,0:T(8,128)S(1)}, f32[64,32,128]{2,1,0:T(8,128)S(1)}) custom-call(s32[4]{0:T(128)S(1)} %copy-done.6, s32[512]{0:T(512)S(1)} %copy-done.5, bf16[17,32,256]{2,1,0:T(8,128)(2,1)S(1)} %gradient.1.g_ref, bf16[17,32,256]{2,1,0:T(8,128)(2,1)S(1)} %collective-permute-done.17.h_ref, ...), custom_call_target="tpu_custom_call" | custom-call | flops 1000000 | bytes 1000000 | tf_op jit(solution)/shard_map/keys/pallas_call | solution.py:476
  95.7 2.5 %collective-permute-done.18 = f32[64,32,128]{2,1,0:T(8,128)S(1)} collective-permute-done((f32[64,32,128]{2,1,0:T(8,128)S(1)}, f32[64,32,128]{2,1,0:T(8,128)S(1)}, u32[]{:S(2)}, u32[]{:S(2)}) %collective-permute-start.18) | collective-permute-done | bytes 1048608 | tf_op jit(solution)/shard_map/ppermute | solution.py:41
  98.5 3.3 %collective-permute-start.21 = (f32[4,4,32,128]{3,2,1,0:T(8,128)S(1)}, f32[4,4,32,128]{3,2,1,0:T(8,128)S(1)}, u32[]{:S(2)}, u32[]{:S(2)}) collective-permute-start(f32[4,4,32,128]{3,2,1,0:T(8,128)S(1)} %bitcast.72), channel_id=1, source_target_pairs={{0,8},{1,65},{2,10},{3,67},{4,12},{5,69},{6,14},{7,71},{8,0},{9,73... | collective-permute-start | bytes 786440 | tf_op jit(solution)/shard_map/ppermute | solution.py:41
  103.8 6.4 %queries.1 = (f32[2,1024,128]{2,1,0:T(8,128)S(1)}, s32[8,128]{1,0:T(8,128)S(1)}) custom-call(s32[4]{0:T(128)S(1)} %copy-done.6, bf16[17,32,256]{2,1,0:T(8,128)(2,1)S(1)} %gradient.1.g_ref, bf16[17,32,256]{2,1,0:T(8,128)(2,1)S(1)} %collective-permute-done.17.h_ref, bf16[2,17,64,128]{3,2,1,0:T(8,128)(2,1)S(1)} %get-tuple-element.57.iq_ref, ...), custom_call_target="tpu_custom_call" | custom-call | flops 1000000 | bytes 1000000 | tf_op jit(solution)/shard_map/queries/pallas_call | solution.py:486
  110.6 3.5 %collective-permute-start.24 = (f32[4,32,128]{2,1,0:T(8,128)S(1)}, f32[4,32,128]{2,1,0:T(8,128)S(1)}, u32[]{:S(2)}, u32[]{:S(2)}) collective-permute-start(f32[4,32,128]{2,1,0:T(8,128)S(1)} %get-tuple-element.60), channel_id=1, source_target_pairs={{0,64},{1,9},{2,66},{3,11},{4,68},{5,13},{6,70},{7,15},{8,72},{9,1... | collective-permute-start | bytes 196616 | tf_op jit(solution)/shard_map/ppermute | solution.py:41
  123.7 1.7 %collective-permute-done.27 = f32[32,128]{1,0:T(8,128)S(1)} collective-permute-done((f32[32,128]{1,0:T(8,128)S(1)}, f32[32,128]{1,0:T(8,128)S(1)}, u32[]{:S(2)}, u32[]{:S(2)}) %collective-permute-start.27) | collective-permute-done | bytes 16416 | tf_op jit(solution)/shard_map/ppermute | solution.py:41
  125.4 2.0 %collective-permute-done.25 = f32[32,128]{1,0:T(8,128)S(1)} collective-permute-done((f32[32,128]{1,0:T(8,128)S(1)}, f32[32,128]{1,0:T(8,128)S(1)}, u32[]{:S(2)}, u32[]{:S(2)}) %collective-permute-start.25) | collective-permute-done | bytes 16416 | tf_op jit(solution)/shard_map/ppermute | solution.py:41
  (94 shorter events, 40.2 us)
Async XLA Ops:
  3.3 6.9 %collective-permute-start.2 = (bf16[64,768]{1,0:T(8,128)(2,1)S(1)}, bf16[64,768]{1,0:T(8,128)(2,1)S(1)}, u32[]{:S(2)}, u32[]{:S(2)}) collective-permute-start(bf16[64,768]{1,0:T(8,128)(2,1)S(1)} %get-tuple-element.50), channel_id=1, source_target_pairs={{0,16},{1,19},{2,18},{3,17},{4,20},{5,23},{6,22},{7,21},{8,24},{9,... | collective-permute-start | bytes 294920 | tf_op jit(solution)/shard_map/ppermute | solution.py:41
  6.5 16.7 %collective-permute-start = (bf16[2,17,64,128]{3,2,1,0:T(8,128)(2,1)S(1)}, bf16[2,17,64,128]{3,2,1,0:T(8,128)(2,1)}, u32[]{:S(2)}, u32[]{:S(2)}) collective-permute-start(bf16[2,17,64,128]{3,2,1,0:T(8,128)(2,1)S(1)} %get-tuple-element.57.iq_ref), channel_id=1, source_target_pairs={{0,2},{1,3},{2,0},{3,1},{4,6},{5,7},{6,4},{7,5},{8,10},{9,11},{10,... | collective-permute-start | bytes 1671176 | tf_op jit(solution)/shard_map/ppermute | solution.py:41
  10.2 6.9 %collective-permute-start.3 = (bf16[2,64,768]{2,1,0:T(8,128)(2,1)S(1)}, bf16[2,64,768]{2,1,0:T(8,128)(2,1)S(1)}, u32[]{:S(2)}, u32[]{:S(2)}) collective-permute-start(bf16[2,64,768]{2,1,0:T(8,128)(2,1)S(1)} %pad_maximum_fusion), channel_id=1, source_target_pairs={{0,4},{1,33},{2,6},{3,35},{4,8},{5,37},{6,10},{7,39},{8,12},{9,41}... | collective-permute-start | bytes 589832 | tf_op jit(solution)/shard_map/ppermute | solution.py:41
  11.9 6.0 %collective-permute-start.4 = (bf16[2,64,768]{2,1,0:T(8,128)(2,1)S(1)}, bf16[2,64,768]{2,1,0:T(8,128)(2,1)S(1)}, u32[]{:S(2)}, u32[]{:S(2)}) collective-permute-start(bf16[2,64,768]{2,1,0:T(8,128)(2,1)S(1)} %pad_maximum_fusion), channel_id=1, source_target_pairs={{0,12},{1,97},{2,14},{3,99},{4,0},{5,101},{6,2},{7,103},{8,4},{9,1... | collective-permute-start | bytes 589832 | tf_op jit(solution)/shard_map/ppermute | solution.py:41
  13.5 7.2 %collective-permute-start.5 = (bf16[2,64,768]{2,1,0:T(8,128)(2,1)S(1)}, bf16[2,64,768]{2,1,0:T(8,128)(2,1)S(1)}, u32[]{:S(2)}, u32[]{:S(2)}) collective-permute-start(bf16[2,64,768]{2,1,0:T(8,128)(2,1)S(1)} %pad_maximum_fusion), channel_id=1, source_target_pairs={{0,8},{1,65},{2,10},{3,67},{4,12},{5,69},{6,14},{7,71},{8,0},{9,73... | collective-permute-start | bytes 589832 | tf_op jit(solution)/shard_map/ppermute | solution.py:41
  23.8 18.4 %collective-permute-start.6 = (bf16[8,64,768]{2,1,0:T(8,128)(2,1)}, bf16[8,64,768]{2,1,0:T(8,128)(2,1)S(1)}, u32[]{:S(2)}, u32[]{:S(2)}) collective-permute-start(bf16[8,64,768]{2,1,0:T(8,128)(2,1)} %constant_dynamic-update-slice_fusion.refs_0_), channel_id=1, source_target_pairs={{0,32},{1,5},{2,34},{3,7},{4,36},{5,9},{6,38},{7,11},{8,40},{9,13}... | collective-permute-start | bytes 2359304 | tf_op jit(solution)/shard_map/ppermute | solution.py:41
  25.3 17.0 %collective-permute-start.8 = (bf16[8,64,768]{2,1,0:T(8,128)(2,1)}, bf16[8,64,768]{2,1,0:T(8,128)(2,1)S(1)}, u32[]{:S(2)}, u32[]{:S(2)}) collective-permute-start(bf16[8,64,768]{2,1,0:T(8,128)(2,1)} %constant_dynamic-update-slice_fusion.refs_0_), channel_id=1, source_target_pairs={{0,96},{1,13},{2,98},{3,15},{4,100},{5,1},{6,102},{7,3},{8,104},{9... | collective-permute-start | bytes 2359304 | tf_op jit(solution)/shard_map/ppermute | solution.py:41
  29.7 14.1 %collective-permute-start.1 = (bf16[2,2,17,32,128]{4,3,2,1,0:T(8,128)(2,1)}, bf16[2,2,17,32,128]{4,3,2,1,0:T(8,128)(2,1)S(1)}, u32[]{:S(2)}, u32[]{:S(2)}) collective-permute-start(bf16[2,2,17,32,128]{4,3,2,1,0:T(8,128)(2,1)} %get-tuple-element.51), channel_id=1, source_target_pairs={{0,1},{1,0},{2,3},{3,2},{4,5},{5,4},{6,7},{7,6},{8,9},{9,8},{10,11... | collective-permute-start | bytes 1671176 | tf_op jit(solution)/shard_map/ppermute | solution.py:41
  41.6 4.6 %collective-permute-start.10 = (bf16[8,64,768]{2,1,0:T(8,128)(2,1)}, bf16[8,64,768]{2,1,0:T(8,128)(2,1)S(1)}, u32[]{:S(2)}, u32[]{:S(2)}) collective-permute-start(bf16[8,64,768]{2,1,0:T(8,128)(2,1)} %constant_dynamic-update-slice_fusion.refs_0_), channel_id=1, source_target_pairs={{0,1},{1,0},{2,3},{3,2},{4,5},{5,4},{6,7},{7,6},{8,9},{9,8},{10,11... | collective-permute-start | bytes 2359304 | tf_op jit(solution)/shard_map/ppermute | solution.py:41
  42.2 4.0 %collective-permute-start.11 = (bf16[8,64,768]{2,1,0:T(8,128)(2,1)S(1)}, bf16[8,64,768]{2,1,0:T(8,128)(2,1)S(1)}, u32[]{:S(2)}, u32[]{:S(2)}) collective-permute-start(bf16[8,64,768]{2,1,0:T(8,128)(2,1)S(1)} %collective-permute-done.6.refs_1_), channel_id=1, source_target_pairs={{0,1},{1,0},{2,3},{3,2},{4,5},{5,4},{6,7},{7,6},{8,9},{9,8},{10,11... | collective-permute-start | bytes 2359304 | tf_op jit(solution)/shard_map/ppermute | solution.py:41
  42.3 4.1 %collective-permute-start.12 = (bf16[8,64,768]{2,1,0:T(8,128)(2,1)S(1)}, bf16[8,64,768]{2,1,0:T(8,128)(2,1)S(1)}, u32[]{:S(2)}, u32[]{:S(2)}) collective-permute-start(bf16[8,64,768]{2,1,0:T(8,128)(2,1)S(1)} %collective-permute-done.8.refs_2_), channel_id=1, source_target_pairs={{0,1},{1,0},{2,3},{3,2},{4,5},{5,4},{6,7},{7,6},{8,9},{9,8},{10,11... | collective-permute-start | bytes 2359304 | tf_op jit(solution)/shard_map/ppermute | solution.py:41
  42.8 20.5 %collective-permute-start.7 = (bf16[4,64,768]{2,1,0:T(8,128)(2,1)S(1)}, bf16[4,64,768]{2,1,0:T(8,128)(2,1)S(1)}, u32[]{:S(2)}, u32[]{:S(2)}) collective-permute-start(bf16[4,64,768]{2,1,0:T(8,128)(2,1)S(1)} %slice.57), channel_id=1, source_target_pairs={{0,32},{1,5},{2,34},{3,7},{4,36},{5,9},{6,38},{7,11},{8,40},{9,13}... | collective-permute-start | bytes 1179656 | tf_op jit(solution)/shard_map/ppermute | solution.py:41
  43.9 19.4 %collective-permute-start.9 = (bf16[4,64,768]{2,1,0:T(8,128)(2,1)S(1)}, bf16[4,64,768]{2,1,0:T(8,128)(2,1)S(1)}, u32[]{:S(2)}, u32[]{:S(2)}) collective-permute-start(bf16[4,64,768]{2,1,0:T(8,128)(2,1)S(1)} %slice.73), channel_id=1, source_target_pairs={{0,96},{1,13},{2,98},{3,15},{4,100},{5,1},{6,102},{7,3},{8,104},{9... | collective-permute-start | bytes 1179656 | tf_op jit(solution)/shard_map/ppermute | solution.py:41
  75.1 10.5 %collective-permute-start.16 = (bf16[17,32,256]{2,1,0:T(8,128)(2,1)S(1)}, bf16[17,32,256]{2,1,0:T(8,128)(2,1)S(1)}, u32[]{:S(2)}, u32[]{:S(2)}) collective-permute-start(bf16[17,32,256]{2,1,0:T(8,128)(2,1)S(1)} %add_convert_fusion), channel_id=1, source_target_pairs={{0,2},{1,3},{2,0},{3,1},{4,6},{5,7},{6,4},{7,5},{8,10},{9,11},{10,... | collective-permute-start | bytes 835592 | tf_op jit(solution)/shard_map/ppermute | solution.py:41
  95.5 2.7 %collective-permute-start.18 = (f32[64,32,128]{2,1,0:T(8,128)S(1)}, f32[64,32,128]{2,1,0:T(8,128)S(1)}, u32[]{:S(2)}, u32[]{:S(2)}) collective-permute-start(f32[64,32,128]{2,1,0:T(8,128)S(1)} %get-tuple-element.42), channel_id=1, source_target_pairs={{0,1},{1,0},{2,3},{3,2},{4,5},{5,4},{6,7},{7,6},{8,9},{9,8},{10,11... | collective-permute-start | bytes 3145736 | tf_op jit(solution)/shard_map/ppermute | solution.py:41
  98.5 11.7 %collective-permute-start.21 = (f32[4,4,32,128]{3,2,1,0:T(8,128)S(1)}, f32[4,4,32,128]{3,2,1,0:T(8,128)S(1)}, u32[]{:S(2)}, u32[]{:S(2)}) collective-permute-start(f32[4,4,32,128]{3,2,1,0:T(8,128)S(1)} %bitcast.72), channel_id=1, source_target_pairs={{0,8},{1,65},{2,10},{3,67},{4,12},{5,69},{6,14},{7,71},{8,0},{9,73... | collective-permute-start | bytes 786440 | tf_op jit(solution)/shard_map/ppermute | solution.py:41
  101.8 8.7 %collective-permute-start.20 = (f32[4,4,32,128]{3,2,1,0:T(8,128)S(1)}, f32[4,4,32,128]{3,2,1,0:T(8,128)S(1)}, u32[]{:S(2)}, u32[]{:S(2)}) collective-permute-start(f32[4,4,32,128]{3,2,1,0:T(8,128)S(1)} %bitcast.71), channel_id=1, source_target_pairs={{0,12},{1,97},{2,14},{3,99},{4,0},{5,101},{6,2},{7,103},{8,4},{9,1... | collective-permute-start | bytes 786440 | tf_op jit(solution)/shard_map/ppermute | solution.py:41
  102.8 7.7 %collective-permute-start.19 = (f32[4,4,32,128]{3,2,1,0:T(8,128)S(1)}, f32[4,4,32,128]{3,2,1,0:T(8,128)S(1)}, u32[]{:S(2)}, u32[]{:S(2)}) collective-permute-start(f32[4,4,32,128]{3,2,1,0:T(8,128)S(1)} %bitcast.70), channel_id=1, source_target_pairs={{0,4},{1,33},{2,6},{3,35},{4,8},{5,37},{6,10},{7,39},{8,12},{9,41}... | collective-permute-start | bytes 786440 | tf_op jit(solution)/shard_map/ppermute | solution.py:41
  110.6 7.1 %collective-permute-start.24 = (f32[4,32,128]{2,1,0:T(8,128)S(1)}, f32[4,32,128]{2,1,0:T(8,128)S(1)}, u32[]{:S(2)}, u32[]{:S(2)}) collective-permute-start(f32[4,32,128]{2,1,0:T(8,128)S(1)} %get-tuple-element.60), channel_id=1, source_target_pairs={{0,64},{1,9},{2,66},{3,11},{4,68},{5,13},{6,70},{7,15},{8,72},{9,1... | collective-permute-start | bytes 196616 | tf_op jit(solution)/shard_map/ppermute | solution.py:41
  114.1 4.3 %collective-permute-start.23 = (f32[4,32,128]{2,1,0:T(8,128)S(1)}, f32[4,32,128]{2,1,0:T(8,128)S(1)}, u32[]{:S(2)}, u32[]{:S(2)}) collective-permute-start(f32[4,32,128]{2,1,0:T(8,128)S(1)} %get-tuple-element.61), channel_id=1, source_target_pairs={{0,96},{1,13},{2,98},{3,15},{4,100},{5,1},{6,102},{7,3},{8,104},{9... | collective-permute-start | bytes 196616 | tf_op jit(solution)/shard_map/ppermute | solution.py:41
  114.6 5.5 %collective-permute-start.22 = (f32[4,32,128]{2,1,0:T(8,128)S(1)}, f32[4,32,128]{2,1,0:T(8,128)S(1)}, u32[]{:S(2)}, u32[]{:S(2)}) collective-permute-start(f32[4,32,128]{2,1,0:T(8,128)S(1)} %get-tuple-element.59), channel_id=1, source_target_pairs={{0,32},{1,5},{2,34},{3,7},{4,36},{5,9},{6,38},{7,11},{8,40},{9,13}... | collective-permute-start | bytes 196616 | tf_op jit(solution)/shard_map/ppermute | solution.py:41
  120.1 5.3 %collective-permute-start.27 = (f32[32,128]{1,0:T(8,128)S(1)}, f32[32,128]{1,0:T(8,128)S(1)}, u32[]{:S(2)}, u32[]{:S(2)}) collective-permute-start(f32[32,128]{1,0:T(8,128)S(1)} %get-tuple-element.63), channel_id=1, source_target_pairs={{0,2},{1,3},{2,0},{3,1},{4,6},{5,7},{6,4},{7,5},{8,10},{9,11},{10,... | collective-permute-start | bytes 49160 | tf_op jit(solution)/shard_map/ppermute | solution.py:41
  121.7 3.7 %collective-permute-start.26 = (f32[32,128]{1,0:T(8,128)S(1)}, f32[32,128]{1,0:T(8,128)S(1)}, u32[]{:S(2)}, u32[]{:S(2)}) collective-permute-start(f32[32,128]{1,0:T(8,128)S(1)} %get-tuple-element.64), channel_id=1, source_target_pairs={{0,18},{1,19},{2,16},{3,17},{4,22},{5,23},{6,20},{7,21},{8,26},{9,... | collective-permute-start | bytes 49160 | tf_op jit(solution)/shard_map/ppermute | solution.py:41
  122.4 4.9 %collective-permute-start.25 = (f32[32,128]{1,0:T(8,128)S(1)}, f32[32,128]{1,0:T(8,128)S(1)}, u32[]{:S(2)}, u32[]{:S(2)}) collective-permute-start(f32[32,128]{1,0:T(8,128)S(1)} %get-tuple-element.62), channel_id=1, source_target_pairs={{0,16},{1,17},{2,18},{3,19},{4,20},{5,21},{6,22},{7,23},{8,24},{9,... | collective-permute-start | bytes 49160 | tf_op jit(solution)/shard_map/ppermute | solution.py:41
  (15 other events, 46.4 us)

commit v4 on v3

--- a/solution.py
+++ b/solution.py
@@ -108,14 +108,12 @@
         plan[COUNT + 2 * half + 1] = (ends[1] - NEAR) // 4
 
 
-def pack_kernel(q_ref, n_ref, packed, token, out, sems):
-    token[...] = jnp.zeros(token.shape, jnp.int32)
+def pack(q_ref, n_ref, out):
     n = n_ref[...] * -math.sqrt(192.0)
     n1 = n.astype(jnp.bfloat16).astype(jnp.float32)
     n2 = (n - n1).astype(jnp.bfloat16).astype(jnp.float32)
     n3 = n - n1 - n2
     row = lax.broadcasted_iota(jnp.int32, (64, 128), 0)
-    copies = []
     for i in range(16):
         lanes = slice(i * 128, (i + 1) * 128)
         a, b = q_ref[2 * i], q_ref[2 * i + 1]
@@ -129,19 +127,13 @@
             ]
             block = jnp.where(row == 0, parts[0], jnp.where(row == 1, parts[1], jnp.where(row == 2, parts[2], 0.0)))
             out[half, 576:640, lanes] = block.astype(jnp.bfloat16)
-        if i % 4 == 3:
-            at = pl.ds((i - 3) * 128, 512)
-            copies.append(pltpu.make_async_copy(out.at[:, :, at], packed.at[:, :, at], sems.at[i // 4]))
-            copies[-1].start()
-    for copy in copies:
-        copy.wait()
 
 
 def target_kernel(part, unread, meta, plan, q_ref, *refs):
     count = 3 - part
     groups, refs = (refs[0:count], refs[count : 2 * count]), refs[2 * count :]
     if part == 0:
-        sums, sorted_ref, token, keys, sems = refs[unread:]
+        n_ref, (sums, sorted_ref, token, packed, keys, sems) = refs[0], refs[1 + unread :]
         token[...] = jnp.zeros(token.shape, jnp.int32)
     else:
         sums, sorted_ref, keep, other, keys, sems = refs[2 + unread :]
@@ -155,6 +147,9 @@
             copies.append(pltpu.make_async_copy(ref, keys.at[pl.ds(at, size)], sems.at[side * count + j]))
     for copy in copies:
         copy.start()
+    if part == 0:
+        pack(q_ref, n_ref, packed)
+        q_ref = packed
     for copy in copies:
         copy.wait()
     for owner in range(2):
@@ -293,7 +288,7 @@
             wide[half, pl.ds(j * HALF, HALF)] = jnp.broadcast_to(w[:, j : j + 1], (HALF, 128))
 
 
-def coefficients(meta, step, g_ref, h_ref, iq_ref, key_ref, wide):
+def coefficients(meta, step, g_ref, h_ref, iq_ref, key_ref, wide, groups=(0, 1, 2, 3)):
     core = meta[1]
     half, ktile = place(meta, step)
     tile = key_ref[pl.ds(pl.multiple_of(ktile * TILE, TILE), TILE), :]
@@ -301,7 +296,7 @@
     g = jnp.concatenate((jnp.where(core == 0, mine, theirs), jnp.where(core == 0, theirs, mine)), axis=0)
     g = jnp.concatenate((g, g, g, g), axis=0)
     found = []
-    for q in range(4):
+    for q in groups:
         rows = iq_ref[half, pl.ds(q * 4, 4)].reshape(256, 128)
         d = lax.dot_general(rows, tile, NT, preferred_element_type=jnp.float32)
         w = wide[half, pl.ds(q * 256, 256)]
@@ -331,14 +326,15 @@
     lax.fori_loop(0, TILES, body, 0, unroll=4)
 
 
-def query_kernel(idx_scale, meta, g_ref, h_ref, iq_ref, key_ref, dq, token, wide):
+def query_kernel(groups, idx_scale, meta, g_ref, h_ref, iq_ref, key_ref, *refs):
+    dq, token, wide = refs[-3:]
     token[...] = jnp.zeros(token.shape, jnp.int32)
     spread(iq_ref, wide, idx_scale)
     dq[...] = jnp.zeros(dq.shape, jnp.float32)
 
     def body(step, _):
-        half, _ktile, tile, found = coefficients(meta, step, g_ref, h_ref, iq_ref, key_ref, wide)
-        for q in range(4):
+        half, _ktile, tile, found = coefficients(meta, step, g_ref, h_ref, iq_ref, key_ref, wide, groups)
+        for q in range(2):
             dq[half, pl.ds(q * 256, 256)] = dq[half, pl.ds(q * 256, 256)] + lax.dot_general(
                 found[q], tile, NN, preferred_element_type=jnp.float32
             )
@@ -396,17 +392,6 @@
     pair = jnp.stack((own, beside))
     legs = [pair] + [send(pair, along(True, shift)) for shift in (1, 3, 2)]
     group = jnp.concatenate(legs, axis=0)
-    query, token = pl.pallas_call(
-        pack_kernel,
-        out_shape=(jax.ShapeDtypeStruct((2, 640, 2048), bf16), flag),
-        in_specs=[vmem(), vmem()],
-        out_specs=(pl.BlockSpec(memory_space=pltpu.HBM), vmem()),
-        scratch_shapes=[pltpu.VMEM((2, 640, 2048), bf16), pltpu.SemaphoreType.DMA((4,))],
-        compiler_params=params(8),
-        cost_estimate=small,
-        name="pack",
-    )(query_latent.transpose(1, 2, 0), normalizer.T)
-
     iq = indexer_query.reshape(2, HALF, 16, 128).transpose(0, 2, 1, 3)
     weight = jnp.pad(indexer_weight.reshape(2, 1, HALF, 16), ((0, 0), (0, 0), (0, 0), (0, 112)))
     iqw = jnp.concatenate((iq, weight), axis=1)
@@ -418,7 +403,7 @@
     iq_other = swap_core(lax.dynamic_slice_in_dim(iq_both, (1 - core) * 32, 32, 3))
 
     up, down = send(group, along(False, 1)), send(group, along(False, 3))
-    up, token, plan = lax.optimization_barrier((up, token, plan))
+    up, plan = lax.optimization_barrier((up, plan))
     far_a, far_b = send(up[0:4], along(False, 1)), send(down[4:8], along(False, 3))
     near = [group, up, down]
     near = near + [swap_core(v) for v in near]
@@ -426,22 +411,32 @@
     part = jax.ShapeDtypeStruct((TILES, 32, TILE), f32)
     def targets(stage, outs, after, *arrays):
         reads = 6 - 2 * stage
+        held = len(arrays) - 1 - reads
         return pl.pallas_call(
             functools.partial(target_kernel, stage, len(after)),
             out_shape=(jax.ShapeDtypeStruct((69, HALF, 128), f32), jax.ShapeDtypeStruct((4096, 128), bf16)) + outs,
-            in_specs=[smem(), smem(), vmem()] + [anywhere()] * reads + [vmem()] * (2 * stage) + [anywhere()] * len(after),
+            in_specs=[smem(), smem(), vmem()] + [anywhere()] * reads + [vmem()] * held + [anywhere()] * len(after),
             out_specs=(vmem(),) * (2 + len(outs)),
             scratch_shapes=[pltpu.VMEM((64, HALF, 768), bf16), pltpu.SemaphoreType.DMA((reads,))],
             input_output_aliases={3 + reads: 0, 4 + reads: 1} if stage else {},
-            compiler_params=params(14),
+            compiler_params=params(20),
             cost_estimate=small,
             name="targets_far" if stage else "targets_near",
-        )(meta, plan, query, *arrays, *after)
-
-    sums, sorted_keys, token = targets(0, (flag,), (iq_flag, token, iq_other), *near)
+        )(meta, plan, *arrays, *after)
+
+    sums, sorted_keys, token, query = targets(
+        0,
+        (flag, jax.ShapeDtypeStruct((2, 640, 2048), bf16)),
+        (iq_flag, iq_other),
+        query_latent.transpose(1, 2, 0),
+        *near,
+        normalizer.T,
+    )
     far_a, far_b, token = lax.optimization_barrier((far_a, far_b, token))
     far = (far_a, far_b, swap_core(far_a), swap_core(far_b))
-    _, sorted_keys, keep, other = targets(1, (part, part), (token,), *far, sums, sorted_keys)
+    _, sorted_keys, keep, other = targets(
+        1, (part, part), (token,), query, *far, sums, sorted_keys
+    )
     from_core = swap_core(other)
     from_high = swap_high((keep + from_core).astype(bf16))
 
@@ -483,23 +478,28 @@
         cost_estimate=small,
         name="keys",
     )(meta, plan, grad, grad_other, iqw, iqt, sorted_keys)
-    dq, token = pl.pallas_call(
-        functools.partial(query_kernel, idx_scale),
-        out_shape=(jax.ShapeDtypeStruct((2, 1024, 128), f32), flag),
-        in_specs=[smem()] + [vmem()] * 4,
-        out_specs=(vmem(), vmem()),
-        scratch_shapes=[pltpu.VMEM((2, 1024, 128), f32)],
-        compiler_params=params(12),
-        cost_estimate=small,
-        name="queries",
-    )(meta, grad, grad_other, iqw, sorted_keys)
+    def queries(groups, *after):
+        return pl.pallas_call(
+            functools.partial(query_kernel, groups, idx_scale),
+            out_shape=(jax.ShapeDtypeStruct((2, 512, 128), f32), flag),
+            in_specs=[smem()] + [vmem()] * 4 + [anywhere()] * len(after),
+            out_specs=(vmem(), vmem()),
+            scratch_shapes=[pltpu.VMEM((2, 1024, 128), f32)],
+            compiler_params=params(12),
+            cost_estimate=small,
+            name="queries",
+        )(meta, grad, grad_other, iqw, sorted_keys, *after)
 
     dk = dk_keep + swap_core(dk_other)
+    low, token = queries((0, 1))
     dk = ring_sum(dk.reshape(4, 4, 4, 32, 128), functools.partial(along, True))
     dk, token = lax.optimization_barrier((dk, token))
+    high, token = queries((2, 3), token)
     dk = ring_sum(dk, functools.partial(along, False))
+    dk, token, low, high = lax.optimization_barrier((dk, token, low, high))
     dk = ring_sum(dk, lambda shift: lambda x, z, y, k: (x, z + shift, y, k))
-    query_grad = dq.reshape(2, 16, HALF, 128).transpose(0, 2, 1, 3).reshape(128, 16, 128)
+    low, high = [v.reshape(2, 8, HALF, 128).transpose(0, 2, 1, 3).reshape(128, 8, 128) for v in (low, high)]
+    query_grad = jnp.concatenate((low, high), axis=1)
     return query_grad, dk + token[0:1].astype(f32)
 
 

time: 128 us -> 125 us (0.977); the launches traced: 128 us -> 124 us
  local copies, waits for them, and re-layouts: 16 us -> 10.2 us
  Pallas kernels: 48.4 us -> 51.5 us
  starting transfers between devices: 36 us -> 34.5 us
    unnamed x27 -> x23, local copies, waits for them, and re-layouts: 12.3 us -> 7.44 us
    pallas_call x2, Pallas kernels: 8.86 us -> 10.7 us  [queries(): pl.pallas_call(functools.partial(query_kernel, groups, idx_scale), out_sh...]
    ppermute x28, starting transfers between devices: 36 us -> 34.5 us  [send(): return lax.ppermute(value, ALL, permutation(move))]
  transfers between devices with their start and end apart: 28 -> 28, of which waited for: 15 -> 14; matrix products, arithmetic and copies ran while one was open for 8% -> 8% of each run, Pallas kernels for 26% -> 29%
where the time goes in v4:
time: 125 us; the launch traced here: 124 us
  Pallas kernels  51.5 us (41%)
  starting transfers between devices  34.5 us (28%)
  waiting for transfers between devices  18.8 us (15%)
  local copies, waits for them, and re-layouts  10.2 us (8%)
  other arithmetic  7.68 us (6%)
    ppermute x28, starting transfers between devices, send(): return lax.ppermute(value, ALL, permutation(move))  34.5 us
    pallas_call x2, Pallas kernels, targets(): pl.pallas_call(functools.partial(target_kernel, stage, len(after)), out_s...  21.8 us
    ppermute x28, waiting for transfers between devices, send(): return lax.ppermute(value, ALL, permutation(move))  18.8 us
    pallas_call x2, Pallas kernels, queries(): pl.pallas_call(functools.partial(query_kernel, groups, idx_scale), out_sh...  10.7 us
    pallas_call x1, Pallas kernels, per_device(): pl.pallas_call(functools.partial(logit_kernel, idx_scale), out_shape=part...  7.49 us
    unnamed x23, local copies, waits for them, and re-layouts  7.44 us
    pallas_call x1, Pallas kernels, per_device(): pl.pallas_call(functools.partial(key_kernel, idx_scale), out_shape=(shard...  7.09 us
    pallas_call x1, Pallas kernels, per_device(): pl.pallas_call(plan_kernel, out_shape=jax.ShapeDtypeStruct((512,), jnp.in...  3.35 us
  transfers between devices with their start and end apart: 28, of which 14 were waited for; matrix products, arithmetic and copies ran while one was open for 8% of the time, Pallas kernels for 29%

profile of v4, /device:TPU:0, one launch (start us, length us, event | category | flops | bytes accessed | tf_op | source)
XLA Modules:
  0.0 123.7 jit_solution(8838620870870012405)
XLA Ops:
  3.3 2.0 %collective-permute-start = (bf16[64,768]{1,0:T(8,128)(2,1)S(1)}, bf16[64,768]{1,0:T(8,128)(2,1)S(1)}, u32[]{:S(2)}, u32[]{:S(2)}) collective-permute-start(bf16[64,768]{1,0:T(8,128)(2,1)S(1)} %get-tuple-element.58), channel_id=1, source_target_pairs={{0,16},{1,19},{2,18},{3,17},{4,20},{5,23},{6,22},{7,21},{8,24},{9,... | collective-permute-start | bytes 294920 | tf_op jit(solution)/shard_map/ppermute | solution.py:41
  6.5 3.7 %collective-permute-start.4 = (bf16[2,17,64,128]{3,2,1,0:T(8,128)(2,1)S(1)}, bf16[2,17,64,128]{3,2,1,0:T(8,128)(2,1)}, u32[]{:S(2)}, u32[]{:S(2)}) collective-permute-start(bf16[2,17,64,128]{3,2,1,0:T(8,128)(2,1)S(1)} %get-tuple-element.66.iq_ref), channel_id=1, source_target_pairs={{0,2},{1,3},{2,0},{3,1},{4,6},{5,7},{6,4},{7,5},{8,10},{9,11},{10,... | collective-permute-start | bytes 1671176 | tf_op jit(solution)/shard_map/ppermute | solution.py:41
  11.9 1.7 %collective-permute-start.2 = (bf16[2,64,768]{2,1,0:T(8,128)(2,1)S(1)}, bf16[2,64,768]{2,1,0:T(8,128)(2,1)S(1)}, u32[]{:S(2)}, u32[]{:S(2)}) collective-permute-start(bf16[2,64,768]{2,1,0:T(8,128)(2,1)S(1)} %pad_maximum_fusion.1), channel_id=1, source_target_pairs={{0,12},{1,97},{2,14},{3,99},{4,0},{5,101},{6,2},{7,103},{8,4},{9,1... | collective-permute-start | bytes 589832 | tf_op jit(solution)/shard_map/ppermute | solution.py:41
  13.5 2.0 %collective-permute-start.3 = (bf16[2,64,768]{2,1,0:T(8,128)(2,1)S(1)}, bf16[2,64,768]{2,1,0:T(8,128)(2,1)S(1)}, u32[]{:S(2)}, u32[]{:S(2)}) collective-permute-start(bf16[2,64,768]{2,1,0:T(8,128)(2,1)S(1)} %pad_maximum_fusion.1), channel_id=1, source_target_pairs={{0,8},{1,65},{2,10},{3,67},{4,12},{5,69},{6,14},{7,71},{8,0},{9,73... | collective-permute-start | bytes 589832 | tf_op jit(solution)/shard_map/ppermute | solution.py:41
  18.5 2.1 %collective-permute-done.3 = bf16[2,64,768]{2,1,0:T(8,128)(2,1)S(1)} collective-permute-done((bf16[2,64,768]{2,1,0:T(8,128)(2,1)S(1)}, bf16[2,64,768]{2,1,0:T(8,128)(2,1)S(1)}, u32[]{:S(2)}, u32[]{:S(2)}) %collective-permute-start.3) | collective-permute-done | bytes 196640 | tf_op jit(solution)/shard_map/ppermute | solution.py:41
  21.4 1.8 %collective-permute-done.4 = bf16[2,17,64,128]{3,2,1,0:T(8,128)(2,1)} collective-permute-done((bf16[2,17,64,128]{3,2,1,0:T(8,128)(2,1)S(1)}, bf16[2,17,64,128]{3,2,1,0:T(8,128)(2,1)}, u32[]{:S(2)}, u32[]{:S(2)}) %collective-permute-start.4) | collective-permute-done | bytes 557088 | tf_op jit(solution)/shard_map/ppermute | solution.py:41
  25.3 1.7 %collective-permute-start.7 = (bf16[8,64,768]{2,1,0:T(8,128)(2,1)}, bf16[8,64,768]{2,1,0:T(8,128)(2,1)S(1)}, u32[]{:S(2)}, u32[]{:S(2)}) collective-permute-start(bf16[8,64,768]{2,1,0:T(8,128)(2,1)} %constant_dynamic-update-slice_fusion.refs_0_), channel_id=1, source_target_pairs={{0,96},{1,13},{2,98},{3,15},{4,100},{5,1},{6,102},{7,3},{8,104},{9... | collective-permute-start | bytes 2359304 | tf_op jit(solution)/shard_map/ppermute | solution.py:41
  27.6 2.1 %fusion.2 = (bf16[2,2,17,32,128]{4,3,2,1,0:T(8,128)(2,1)}, bf16[2,2,17,32,128]{4,3,2,1,0:T(8,128)(2,1)S(1)}) fusion(s32[]{:T(128)S(6)} %select_n.162, bf16[1,2,17,64,128]{4,3,2,1,0:T(8,128)(2,1)S(1)} %get-tuple-element.65, bf16[1,2,17,64,128]{4,3,2,1,0:T(8,128)(2,1)} %bitcast.8, s32[]{:T(128)S(6)} %select_n.161), kind=kLoop, calls=%fused_computation.8 | loop fusion | flops 2228224 | bytes 2228232 | tf_op jit(solution)/shard_map/stack | solution.py:401
  31.1 3.3 %plan.1 = s32[512]{0:T(512)} custom-call(s32[4]{0:T(128)} %pad_add_fusion.meta, s32[64]{0:T(128)} %order.1, s32[64]{0:T(128)} %get-tuple-element.74.slot, s32[64]{0:T(128)} %get-tuple-element.73.row, s32[64]{0:T(128)} %get-tuple-element.54.row_other), custom_call_target="tpu_custom_call" | custom-call | flops 1000000 | bytes 1000000 | tf_op jit(solution)/shard_map/plan/pallas_call | solution.py:379
  35.1 2.2 %collective-permute-done.5.refs_1_ = bf16[8,64,768]{2,1,0:T(8,128)(2,1)S(1)} collective-permute-done((bf16[8,64,768]{2,1,0:T(8,128)(2,1)}, bf16[8,64,768]{2,1,0:T(8,128)(2,1)S(1)}, u32[]{:S(2)}, u32[]{:S(2)}) %collective-permute-start.5) | collective-permute-done | bytes 786464 | tf_op jit(solution)/shard_map/ppermute | solution.py:41
  39.2 2.0 %collective-permute-start.12 = (bf16[4,64,768]{2,1,0:T(8,128)(2,1)S(1)}, bf16[4,64,768]{2,1,0:T(8,128)(2,1)S(1)}, u32[]{:S(2)}, u32[]{:S(2)}) collective-permute-start(bf16[4,64,768]{2,1,0:T(8,128)(2,1)S(1)} %slice.73), channel_id=1, source_target_pairs={{0,96},{1,13},{2,98},{3,15},{4,100},{5,1},{6,102},{7,3},{8,104},{9... | collective-permute-start | bytes 1179656 | tf_op jit(solution)/shard_map/ppermute | solution.py:41
  41.3 2.3 %copy-done = bf16[128,32,576]{0,2,1:T(8,128)(2,1)S(1)} copy-done((bf16[128,32,576]{0,2,1:T(8,128)(2,1)S(1)}, bf16[128,32,576]{0,2,1:T(8,128)(2,1)}, u32[]{:S(2)}) %copy-start) | copy-done | bytes 4718616
  44.7 14.6 %targets_near.1 = (f32[69,64,128]{2,1,0:T(8,128)S(1)}, bf16[4096,128]{1,0:T(8,128)(2,1)S(1)}, s32[8,128]{1,0:T(8,128)S(1)}, bf16[2,640,2048]{2,1,0:T(8,128)(2,1)S(1)}) custom-call(s32[4]{0:T(128)S(1)} %copy-done.3, s32[512]{0:T(512)S(1)} %copy-done.4, bf16[32,576,128]{2,1,0:T(8,128)(2,1)S(1)} %bitcast.61, ...), custom_call_target="tpu_custom_call" | custom-call | flops 1000000 | bytes 1000000 | tf_op jit(solution)/shard_map/targets_near/pallas_call | solution.py:415
  61.7 7.2 %targets_far.1 = (f32[69,64,128]{2,1,0:T(8,128)S(1)}, bf16[4096,128]{1,0:T(8,128)(2,1)S(1)}, f32[17,32,256]{2,1,0:T(8,128)S(1)}, f32[17,32,256]{2,1,0:T(8,128)S(1)}) custom-call(s32[4]{0:T(128)S(1)} %copy-done.3, s32[512]{0:T(512)S(1)} %copy-done.4, bf16[2,640,2048]{2,1,0:T(8,128)(2,1)S(1)} %get-tuple-element.32.q_ref, ...), custom_call_target="tpu_custom_call", output_to_operand_aliasing={{0}: (7, {}), {1}: (8, {})} | custom-call | flops 1000000 | bytes 1000000 | tf_op jit(solution)/shard_map/targets_far/pallas_call | solution.py:415
  69.1 1.8 %collective-permute-done.15.b_ref = f32[17,32,256]{2,1,0:T(8,128)S(1)} collective-permute-done((f32[17,32,256]{2,1,0:T(8,128)S(1)}, f32[17,32,256]{2,1,0:T(8,128)S(1)}, u32[]{:S(2)}, u32[]{:S(2)}) %collective-permute-start.15) | collective-permute-done | bytes 557088 | tf_op jit(solution)/shard_map/ppermute | solution.py:41
  72.6 7.5 %logits.1.p_ref = f32[17,32,256]{2,1,0:T(8,128)S(1)} custom-call(s32[4]{0:T(128)S(1)} %copy-done.3, bf16[2,2,17,32,128]{4,3,2,1,0:T(8,128)(2,1)S(1)} %get-tuple-element.60.a_ref, bf16[2,2,17,32,128]{4,3,2,1,0:T(8,128)(2,1)S(1)} %collective-permute-done.6.refs_8_.b_ref, bf16[4096,128]{1,0:T(8,128)(2,1)S(1)} %get-tuple-element.39.key_ref), custom_call_target="tpu_custom_call" | custom-call | flops 1000000 | bytes 1000000 | tf_op jit(solution)/shard_map/logits/pallas_call | solution.py:443
  84.1 7.1 %keys.1 = (f32[64,32,128]{2,1,0:T(8,128)S(1)}, f32[64,32,128]{2,1,0:T(8,128)S(1)}) custom-call(s32[4]{0:T(128)S(1)} %copy-done.3, s32[512]{0:T(512)S(1)} %copy-done.4, bf16[17,32,256]{2,1,0:T(8,128)(2,1)S(1)} %gradient.1.g_ref, bf16[17,32,256]{2,1,0:T(8,128)(2,1)S(1)} %collective-permute-done.17.h_ref, ...), custom_call_target="tpu_custom_call" | custom-call | flops 1000000 | bytes 1000000 | tf_op jit(solution)/shard_map/keys/pallas_call | solution.py:471
  91.4 2.5 %collective-permute-done.18 = f32[64,32,128]{2,1,0:T(8,128)S(1)} collective-permute-done((f32[64,32,128]{2,1,0:T(8,128)S(1)}, f32[64,32,128]{2,1,0:T(8,128)S(1)}, u32[]{:S(2)}, u32[]{:S(2)}) %collective-permute-start.18) | collective-permute-done | bytes 1048608 | tf_op jit(solution)/shard_map/ppermute | solution.py:41
  94.2 3.3 %collective-permute-start.21 = (f32[4,4,32,128]{3,2,1,0:T(8,128)S(1)}, f32[4,4,32,128]{3,2,1,0:T(8,128)S(1)}, u32[]{:S(2)}, u32[]{:S(2)}) collective-permute-start(f32[4,4,32,128]{3,2,1,0:T(8,128)S(1)} %bitcast.76), channel_id=1, source_target_pairs={{0,8},{1,65},{2,10},{3,67},{4,12},{5,69},{6,14},{7,71},{8,0},{9,73... | collective-permute-start | bytes 786440 | tf_op jit(solution)/shard_map/ppermute | solution.py:41
  97.5 2.0 %collective-permute-start.19 = (f32[4,4,32,128]{3,2,1,0:T(8,128)S(1)}, f32[4,4,32,128]{3,2,1,0:T(8,128)S(1)}, u32[]{:S(2)}, u32[]{:S(2)}) collective-permute-start(f32[4,4,32,128]{3,2,1,0:T(8,128)S(1)} %bitcast.74), channel_id=1, source_target_pairs={{0,4},{1,33},{2,6},{3,35},{4,8},{5,37},{6,10},{7,39},{8,12},{9,41}... | collective-permute-start | bytes 786440 | tf_op jit(solution)/shard_map/ppermute | solution.py:41
  99.5 5.3 %queries.2 = (f32[2,512,128]{2,1,0:T(8,128)S(1)}, s32[8,128]{1,0:T(8,128)S(1)}) custom-call(s32[4]{0:T(128)S(1)} %copy-done.3, bf16[17,32,256]{2,1,0:T(8,128)(2,1)S(1)} %gradient.1.g_ref, bf16[17,32,256]{2,1,0:T(8,128)(2,1)S(1)} %collective-permute-done.17.h_ref, bf16[2,17,64,128]{3,2,1,0:T(8,128)(2,1)S(1)} %get-tuple-element.66.iq_ref, ...), custom_call_target="tpu_custom_call" | custom-call | flops 1000000 | bytes 1000000 | tf_op jit(solution)/shard_map/queries/pallas_call | solution.py:482
  105.3 2.5 %collective-permute-start.24 = (f32[4,32,128]{2,1,0:T(8,128)S(1)}, f32[4,32,128]{2,1,0:T(8,128)S(1)}, u32[]{:S(2)}, u32[]{:S(2)}) collective-permute-start(f32[4,32,128]{2,1,0:T(8,128)S(1)} %get-tuple-element.68), channel_id=1, source_target_pairs={{0,64},{1,9},{2,66},{3,11},{4,68},{5,13},{6,70},{7,15},{8,72},{9,1... | collective-permute-start | bytes 196616 | tf_op jit(solution)/shard_map/ppermute | solution.py:41
  109.7 5.3 %queries.3 = (f32[2,512,128]{2,1,0:T(8,128)S(1)}, s32[8,128]{1,0:T(8,128)S(1)}) custom-call(s32[4]{0:T(128)S(1)} %copy-done.3, bf16[17,32,256]{2,1,0:T(8,128)(2,1)S(1)} %gradient.1.g_ref, bf16[17,32,256]{2,1,0:T(8,128)(2,1)S(1)} %collective-permute-done.17.h_ref, bf16[2,17,64,128]{3,2,1,0:T(8,128)(2,1)S(1)} %get-tuple-element.66.iq_ref, ...), custom_call_target="tpu_custom_call" | custom-call | flops 1000000 | bytes 1000000 | tf_op jit(solution)/shard_map/queries/pallas_call | solution.py:482
  121.2 1.9 %collective-permute-done.25 = f32[32,128]{1,0:T(8,128)S(1)} collective-permute-done((f32[32,128]{1,0:T(8,128)S(1)}, f32[32,128]{1,0:T(8,128)S(1)}, u32[]{:S(2)}, u32[]{:S(2)}) %collective-permute-start.25) | collective-permute-done | bytes 16416 | tf_op jit(solution)/shard_map/ppermute | solution.py:41
  (92 shorter events, 34.6 us)
Async XLA Ops:
  3.3 6.9 %collective-permute-start = (bf16[64,768]{1,0:T(8,128)(2,1)S(1)}, bf16[64,768]{1,0:T(8,128)(2,1)S(1)}, u32[]{:S(2)}, u32[]{:S(2)}) collective-permute-start(bf16[64,768]{1,0:T(8,128)(2,1)S(1)} %get-tuple-element.58), channel_id=1, source_target_pairs={{0,16},{1,19},{2,18},{3,17},{4,20},{5,23},{6,22},{7,21},{8,24},{9,... | collective-permute-start | bytes 294920 | tf_op jit(solution)/shard_map/ppermute | solution.py:41
  6.5 16.7 %collective-permute-start.4 = (bf16[2,17,64,128]{3,2,1,0:T(8,128)(2,1)S(1)}, bf16[2,17,64,128]{3,2,1,0:T(8,128)(2,1)}, u32[]{:S(2)}, u32[]{:S(2)}) collective-permute-start(bf16[2,17,64,128]{3,2,1,0:T(8,128)(2,1)S(1)} %get-tuple-element.66.iq_ref), channel_id=1, source_target_pairs={{0,2},{1,3},{2,0},{3,1},{4,6},{5,7},{6,4},{7,5},{8,10},{9,11},{10,... | collective-permute-start | bytes 1671176 | tf_op jit(solution)/shard_map/ppermute | solution.py:41
  10.2 6.9 %collective-permute-start.1 = (bf16[2,64,768]{2,1,0:T(8,128)(2,1)S(1)}, bf16[2,64,768]{2,1,0:T(8,128)(2,1)S(1)}, u32[]{:S(2)}, u32[]{:S(2)}) collective-permute-start(bf16[2,64,768]{2,1,0:T(8,128)(2,1)S(1)} %pad_maximum_fusion.1), channel_id=1, source_target_pairs={{0,4},{1,33},{2,6},{3,35},{4,8},{5,37},{6,10},{7,39},{8,12},{9,41}... | collective-permute-start | bytes 589832 | tf_op jit(solution)/shard_map/ppermute | solution.py:41
  11.9 6.0 %collective-permute-start.2 = (bf16[2,64,768]{2,1,0:T(8,128)(2,1)S(1)}, bf16[2,64,768]{2,1,0:T(8,128)(2,1)S(1)}, u32[]{:S(2)}, u32[]{:S(2)}) collective-permute-start(bf16[2,64,768]{2,1,0:T(8,128)(2,1)S(1)} %pad_maximum_fusion.1), channel_id=1, source_target_pairs={{0,12},{1,97},{2,14},{3,99},{4,0},{5,101},{6,2},{7,103},{8,4},{9,1... | collective-permute-start | bytes 589832 | tf_op jit(solution)/shard_map/ppermute | solution.py:41
  13.5 7.2 %collective-permute-start.3 = (bf16[2,64,768]{2,1,0:T(8,128)(2,1)S(1)}, bf16[2,64,768]{2,1,0:T(8,128)(2,1)S(1)}, u32[]{:S(2)}, u32[]{:S(2)}) collective-permute-start(bf16[2,64,768]{2,1,0:T(8,128)(2,1)S(1)} %pad_maximum_fusion.1), channel_id=1, source_target_pairs={{0,8},{1,65},{2,10},{3,67},{4,12},{5,69},{6,14},{7,71},{8,0},{9,73... | collective-permute-start | bytes 589832 | tf_op jit(solution)/shard_map/ppermute | solution.py:41
  23.8 13.4 %collective-permute-start.5 = (bf16[8,64,768]{2,1,0:T(8,128)(2,1)}, bf16[8,64,768]{2,1,0:T(8,128)(2,1)S(1)}, u32[]{:S(2)}, u32[]{:S(2)}) collective-permute-start(bf16[8,64,768]{2,1,0:T(8,128)(2,1)} %constant_dynamic-update-slice_fusion.refs_0_), channel_id=1, source_target_pairs={{0,32},{1,5},{2,34},{3,7},{4,36},{5,9},{6,38},{7,11},{8,40},{9,13}... | collective-permute-start | bytes 2359304 | tf_op jit(solution)/shard_map/ppermute | solution.py:41
  25.3 12.2 %collective-permute-start.7 = (bf16[8,64,768]{2,1,0:T(8,128)(2,1)}, bf16[8,64,768]{2,1,0:T(8,128)(2,1)S(1)}, u32[]{:S(2)}, u32[]{:S(2)}) collective-permute-start(bf16[8,64,768]{2,1,0:T(8,128)(2,1)} %constant_dynamic-update-slice_fusion.refs_0_), channel_id=1, source_target_pairs={{0,96},{1,13},{2,98},{3,15},{4,100},{5,1},{6,102},{7,3},{8,104},{9... | collective-permute-start | bytes 2359304 | tf_op jit(solution)/shard_map/ppermute | solution.py:41
  29.7 9.4 %collective-permute-start.6 = (bf16[2,2,17,32,128]{4,3,2,1,0:T(8,128)(2,1)}, bf16[2,2,17,32,128]{4,3,2,1,0:T(8,128)(2,1)S(1)}, u32[]{:S(2)}, u32[]{:S(2)}) collective-permute-start(bf16[2,2,17,32,128]{4,3,2,1,0:T(8,128)(2,1)} %get-tuple-element.59), channel_id=1, source_target_pairs={{0,1},{1,0},{2,3},{3,2},{4,5},{5,4},{6,7},{7,6},{8,9},{9,8},{10,11... | collective-permute-start | bytes 1671176 | tf_op jit(solution)/shard_map/ppermute | solution.py:41
  34.5 6.7 %collective-permute-start.8 = (bf16[8,64,768]{2,1,0:T(8,128)(2,1)}, bf16[8,64,768]{2,1,0:T(8,128)(2,1)S(1)}, u32[]{:S(2)}, u32[]{:S(2)}) collective-permute-start(bf16[8,64,768]{2,1,0:T(8,128)(2,1)} %constant_dynamic-update-slice_fusion.refs_0_), channel_id=1, source_target_pairs={{0,1},{1,0},{2,3},{3,2},{4,5},{5,4},{6,7},{7,6},{8,9},{9,8},{10,11... | collective-permute-start | bytes 2359304 | tf_op jit(solution)/shard_map/ppermute | solution.py:41
  37.2 4.0 %collective-permute-start.9 = (bf16[8,64,768]{2,1,0:T(8,128)(2,1)S(1)}, bf16[8,64,768]{2,1,0:T(8,128)(2,1)S(1)}, u32[]{:S(2)}, u32[]{:S(2)}) collective-permute-start(bf16[8,64,768]{2,1,0:T(8,128)(2,1)S(1)} %collective-permute-done.5.refs_1_), channel_id=1, source_target_pairs={{0,1},{1,0},{2,3},{3,2},{4,5},{5,4},{6,7},{7,6},{8,9},{9,8},{10,11... | collective-permute-start | bytes 2359304 | tf_op jit(solution)/shard_map/ppermute | solution.py:41
  37.5 3.7 %collective-permute-start.10 = (bf16[8,64,768]{2,1,0:T(8,128)(2,1)S(1)}, bf16[8,64,768]{2,1,0:T(8,128)(2,1)S(1)}, u32[]{:S(2)}, u32[]{:S(2)}) collective-permute-start(bf16[8,64,768]{2,1,0:T(8,128)(2,1)S(1)} %collective-permute-done.7.refs_2_), channel_id=1, source_target_pairs={{0,1},{1,0},{2,3},{3,2},{4,5},{5,4},{6,7},{7,6},{8,9},{9,8},{10,11... | collective-permute-start | bytes 2359304 | tf_op jit(solution)/shard_map/ppermute | solution.py:41
  37.8 21.5 %collective-permute-start.11 = (bf16[4,64,768]{2,1,0:T(8,128)(2,1)S(1)}, bf16[4,64,768]{2,1,0:T(8,128)(2,1)S(1)}, u32[]{:S(2)}, u32[]{:S(2)}) collective-permute-start(bf16[4,64,768]{2,1,0:T(8,128)(2,1)S(1)} %slice.57), channel_id=1, source_target_pairs={{0,32},{1,5},{2,34},{3,7},{4,36},{5,9},{6,38},{7,11},{8,40},{9,13}... | collective-permute-start | bytes 1179656 | tf_op jit(solution)/shard_map/ppermute | solution.py:41
  39.2 20.2 %collective-permute-start.12 = (bf16[4,64,768]{2,1,0:T(8,128)(2,1)S(1)}, bf16[4,64,768]{2,1,0:T(8,128)(2,1)S(1)}, u32[]{:S(2)}, u32[]{:S(2)}) collective-permute-start(bf16[4,64,768]{2,1,0:T(8,128)(2,1)S(1)} %slice.73), channel_id=1, source_target_pairs={{0,96},{1,13},{2,98},{3,15},{4,100},{5,1},{6,102},{7,3},{8,104},{9... | collective-permute-start | bytes 1179656 | tf_op jit(solution)/shard_map/ppermute | solution.py:41
  71.0 10.3 %collective-permute-start.16 = (bf16[17,32,256]{2,1,0:T(8,128)(2,1)S(1)}, bf16[17,32,256]{2,1,0:T(8,128)(2,1)S(1)}, u32[]{:S(2)}, u32[]{:S(2)}) collective-permute-start(bf16[17,32,256]{2,1,0:T(8,128)(2,1)S(1)} %add_convert_fusion), channel_id=1, source_target_pairs={{0,2},{1,3},{2,0},{3,1},{4,6},{5,7},{6,4},{7,5},{8,10},{9,11},{10,... | collective-permute-start | bytes 835592 | tf_op jit(solution)/shard_map/ppermute | solution.py:41
  91.2 2.7 %collective-permute-start.18 = (f32[64,32,128]{2,1,0:T(8,128)S(1)}, f32[64,32,128]{2,1,0:T(8,128)S(1)}, u32[]{:S(2)}, u32[]{:S(2)}) collective-permute-start(f32[64,32,128]{2,1,0:T(8,128)S(1)} %get-tuple-element.43), channel_id=1, source_target_pairs={{0,1},{1,0},{2,3},{3,2},{4,5},{5,4},{6,7},{7,6},{8,9},{9,8},{10,11... | collective-permute-start | bytes 3145736 | tf_op jit(solution)/shard_map/ppermute | solution.py:41
  94.2 10.6 %collective-permute-start.21 = (f32[4,4,32,128]{3,2,1,0:T(8,128)S(1)}, f32[4,4,32,128]{3,2,1,0:T(8,128)S(1)}, u32[]{:S(2)}, u32[]{:S(2)}) collective-permute-start(f32[4,4,32,128]{3,2,1,0:T(8,128)S(1)} %bitcast.76), channel_id=1, source_target_pairs={{0,8},{1,65},{2,10},{3,67},{4,12},{5,69},{6,14},{7,71},{8,0},{9,73... | collective-permute-start | bytes 786440 | tf_op jit(solution)/shard_map/ppermute | solution.py:41
  97.5 7.4 %collective-permute-start.20 = (f32[4,4,32,128]{3,2,1,0:T(8,128)S(1)}, f32[4,4,32,128]{3,2,1,0:T(8,128)S(1)}, u32[]{:S(2)}, u32[]{:S(2)}) collective-permute-start(f32[4,4,32,128]{3,2,1,0:T(8,128)S(1)} %bitcast.75), channel_id=1, source_target_pairs={{0,12},{1,97},{2,14},{3,99},{4,0},{5,101},{6,2},{7,103},{8,4},{9,1... | collective-permute-start | bytes 786440 | tf_op jit(solution)/shard_map/ppermute | solution.py:41
  97.5 7.6 %collective-permute-start.19 = (f32[4,4,32,128]{3,2,1,0:T(8,128)S(1)}, f32[4,4,32,128]{3,2,1,0:T(8,128)S(1)}, u32[]{:S(2)}, u32[]{:S(2)}) collective-permute-start(f32[4,4,32,128]{3,2,1,0:T(8,128)S(1)} %bitcast.74), channel_id=1, source_target_pairs={{0,4},{1,33},{2,6},{3,35},{4,8},{5,37},{6,10},{7,39},{8,12},{9,41}... | collective-permute-start | bytes 786440 | tf_op jit(solution)/shard_map/ppermute | solution.py:41
  105.3 9.8 %collective-permute-start.24 = (f32[4,32,128]{2,1,0:T(8,128)S(1)}, f32[4,32,128]{2,1,0:T(8,128)S(1)}, u32[]{:S(2)}, u32[]{:S(2)}) collective-permute-start(f32[4,32,128]{2,1,0:T(8,128)S(1)} %get-tuple-element.68), channel_id=1, source_target_pairs={{0,64},{1,9},{2,66},{3,11},{4,68},{5,13},{6,70},{7,15},{8,72},{9,1... | collective-permute-start | bytes 196616 | tf_op jit(solution)/shard_map/ppermute | solution.py:41
  107.7 7.4 %collective-permute-start.23 = (f32[4,32,128]{2,1,0:T(8,128)S(1)}, f32[4,32,128]{2,1,0:T(8,128)S(1)}, u32[]{:S(2)}, u32[]{:S(2)}) collective-permute-start(f32[4,32,128]{2,1,0:T(8,128)S(1)} %get-tuple-element.69), channel_id=1, source_target_pairs={{0,96},{1,13},{2,98},{3,15},{4,100},{5,1},{6,102},{7,3},{8,104},{9... | collective-permute-start | bytes 196616 | tf_op jit(solution)/shard_map/ppermute | solution.py:41
  109.1 6.0 %collective-permute-start.22 = (f32[4,32,128]{2,1,0:T(8,128)S(1)}, f32[4,32,128]{2,1,0:T(8,128)S(1)}, u32[]{:S(2)}, u32[]{:S(2)}) collective-permute-start(f32[4,32,128]{2,1,0:T(8,128)S(1)} %get-tuple-element.67), channel_id=1, source_target_pairs={{0,32},{1,5},{2,34},{3,7},{4,36},{5,9},{6,38},{7,11},{8,40},{9,13}... | collective-permute-start | bytes 196616 | tf_op jit(solution)/shard_map/ppermute | solution.py:41
  115.8 5.3 %collective-permute-start.27 = (f32[32,128]{1,0:T(8,128)S(1)}, f32[32,128]{1,0:T(8,128)S(1)}, u32[]{:S(2)}, u32[]{:S(2)}) collective-permute-start(f32[32,128]{1,0:T(8,128)S(1)} %get-tuple-element.71), channel_id=1, source_target_pairs={{0,2},{1,3},{2,0},{3,1},{4,6},{5,7},{6,4},{7,5},{8,10},{9,11},{10,... | collective-permute-start | bytes 49160 | tf_op jit(solution)/shard_map/ppermute | solution.py:41
  117.4 3.7 %collective-permute-start.26 = (f32[32,128]{1,0:T(8,128)S(1)}, f32[32,128]{1,0:T(8,128)S(1)}, u32[]{:S(2)}, u32[]{:S(2)}) collective-permute-start(f32[32,128]{1,0:T(8,128)S(1)} %get-tuple-element.72), channel_id=1, source_target_pairs={{0,18},{1,19},{2,16},{3,17},{4,22},{5,23},{6,20},{7,21},{8,26},{9,... | collective-permute-start | bytes 49160 | tf_op jit(solution)/shard_map/ppermute | solution.py:41
  118.1 4.9 %collective-permute-start.25 = (f32[32,128]{1,0:T(8,128)S(1)}, f32[32,128]{1,0:T(8,128)S(1)}, u32[]{:S(2)}, u32[]{:S(2)}) collective-permute-start(f32[32,128]{1,0:T(8,128)S(1)} %get-tuple-element.70), channel_id=1, source_target_pairs={{0,16},{1,17},{2,18},{3,19},{4,20},{5,21},{6,22},{7,23},{8,24},{9,... | collective-permute-start | bytes 49160 | tf_op jit(solution)/shard_map/ppermute | solution.py:41
  (13 other events, 53.9 us)

commit v5 on v4

--- a/solution.py
+++ b/solution.py
@@ -13,9 +13,9 @@
 TILE = 256
 PER_TILE = TILE // HALF
 TILES = 17
-NEAR = 18 * 4
-FAR = 8 * 4
-SLOT, GOAL, ROW, ROW_OTHER, POSITION, COUNT = 0, 128, 256, 320, 384, 448
+LISTS = (0, 8 * 4, 24 * 4)
+UNUSED = 32 * 4
+SLOT, GOAL, ROW, ROW_OTHER, POSITION, COUNT = 0, 256, 512, 576, 640, 704
 MLA_SCALE = 192.0**-0.5
 LOSS_SCALE = 64.0
 NT = (((1,), (1,)), ((), ()))
@@ -80,32 +80,33 @@
 
 
 def plan_kernel(meta, order, slot, row, row_other, plan):
-    ends = (jnp.int32(0), jnp.int32(NEAR))
+    ends = tuple(jnp.int32(start) for start in LISTS)
     for half in range(2):
-        limit = meta[2 + half]
-
-        def step(i, ends, half=half, limit=limit):
-            near, far = ends
+        limit, base = meta[2 + half], half * PER_TILE * meta[0]
+
+        def step(i, ends, half=half, limit=limit, base=base):
             position, at = order[i], slot[i]
             if half == 0:
                 plan[ROW + position] = row[i]
                 plan[ROW_OTHER + position] = row_other[i]
                 plan[POSITION + at] = position
-            is_far = jnp.where((at // 8) % 4 == 3, 1, 0)
+            ring = (at // 8) % 4
+            stage = jnp.where(ring == 0, 0, jnp.where(ring == 3, 2, 1))
             seen = jnp.where(position <= limit, 1, 0)
-            to = jnp.where(seen == 1, jnp.where(is_far == 1, far, near), NEAR + FAR)
+            to = jnp.where(stage == 0, ends[0], jnp.where(stage == 1, ends[1], ends[2]))
+            to = jnp.where(seen == 1, to, UNUSED)
             plan[SLOT + to] = at
-            plan[GOAL + to] = position + half * PER_TILE * meta[0]
-            return near + seen * (1 - is_far), far + seen * is_far
+            plan[GOAL + to] = position + base
+            return tuple(end + jnp.where(stage == part, seen, 0) for part, end in enumerate(ends))
 
         ends = lax.fori_loop(0, 64, step, ends, unroll=4)
         for part, end in enumerate(ends):
             for u in range(3):
-                plan[SLOT + end + u] = 24 * part
+                plan[SLOT + end + u] = (0, 8, 24)[part]
                 plan[GOAL + end + u] = 68
-        ends = ((ends[0] + 3) // 4 * 4, (ends[1] + 3) // 4 * 4)
-        plan[COUNT + 2 * half] = ends[0] // 4
-        plan[COUNT + 2 * half + 1] = (ends[1] - NEAR) // 4
+        ends = tuple((end + 3) // 4 * 4 for end in ends)
+        for part, end in enumerate(ends):
+            plan[COUNT + 3 * half + part] = (end - LISTS[part]) // 4
 
 
 def pack(q_ref, n_ref, out):
@@ -129,25 +130,29 @@
             out[half, 576:640, lanes] = block.astype(jnp.bfloat16)
 
 
-def target_kernel(part, unread, meta, plan, q_ref, *refs):
-    count = 3 - part
+def target_kernel(stage, unread, meta, plan, q_ref, *refs):
+    count, size, base = ((1, 8, 0), (2, 8, 8), (2, 4, 24))[stage]
     groups, refs = (refs[0:count], refs[count : 2 * count]), refs[2 * count :]
-    if part == 0:
-        n_ref, (sums, sorted_ref, token, packed, keys, sems) = refs[0], refs[1 + unread :]
+    n_ref, keys, sems = refs[0], refs[-2], refs[-1]
+    refs = refs[(2 if stage else 1) + unread : -2]
+    if stage == 0:
+        sums, sorted_ref, token, packed = refs
+    elif stage == 1:
+        sums, sorted_ref, token = refs
+    else:
+        sums, sorted_ref, keep, other = refs
+    if stage < 2:
         token[...] = jnp.zeros(token.shape, jnp.int32)
-    else:
-        sums, sorted_ref, keep, other, keys, sems = refs[2 + unread :]
     core = meta[1]
-    size = 4 if part else 8
     copies = []
     for side, group in enumerate(groups):
         owner = core if side == 0 else 1 - core
         for j, ref in enumerate(group):
-            at = owner * 32 + 24 * part + j * size
+            at = owner * 32 + base + j * size
             copies.append(pltpu.make_async_copy(ref, keys.at[pl.ds(at, size)], sems.at[side * count + j]))
     for copy in copies:
         copy.start()
-    if part == 0:
+    if stage == 0:
         pack(q_ref, n_ref, packed)
         q_ref = packed
     for copy in copies:
@@ -160,13 +165,13 @@
             sorted_ref[pl.ds(at, HALF), :] = keys[slot, :, 640:768]
             return 0
 
-        lax.fori_loop(24 * part, 24 + 8 * part, sort, 0, unroll=4)
+        lax.fori_loop(base, base + count * size, sort, 0, unroll=4)
     scale = MLA_SCALE * math.log2(math.e)
-    first, tiles = plan[COUNT + part], plan[COUNT + 2 + part]
+    first, tiles = plan[COUNT + stage], plan[COUNT + 3 + stage]
 
     def body(t):
         half = jnp.where(t >= first, 1, 0)
-        at = part * NEAR + t * PER_TILE
+        at = LISTS[stage] + t * PER_TILE
         tile = jnp.concatenate([keys[plan[SLOT + at + u], :, 0:640] for u in range(PER_TILE)], axis=0)
         total = jnp.zeros((TILE, 128), jnp.float32)
         for g in range(8):
@@ -189,7 +194,7 @@
     def _():
         body(tiles - 1)
 
-    if part == 1:
+    if stage == 2:
 
         def fold(step, _):
             total = sums[pl.ds(step * PER_TILE, PER_TILE)].reshape(TILE, 128).T
@@ -202,13 +207,20 @@
         lax.fori_loop(0, TILES, fold, 0, unroll=4)
 
 
+def take_kernel(start, source, out, sem):
+    copy = pltpu.make_async_copy(source.at[pl.ds(start, 4)], out, sem)
+    copy.start()
+    copy.wait()
+
+
 def visible_of(meta, half, ktile):
     rows = lax.broadcasted_iota(jnp.int32, (32, TILE), 0) + meta[1] * 32 + meta[2 + half] * HALF
     cols = lax.broadcasted_iota(jnp.int32, (32, TILE), 1) + ktile * TILE
     return cols <= rows
 
 
-def logit_kernel(idx_scale, meta, a_ref, b_ref, key_ref, out, wide, top, norm):
+def logit_kernel(idx_scale, meta, a_ref, b_ref, key_ref, iq_ref, out, scaled, wide, top, norm):
+    spread(iq_ref, scaled, idx_scale)
     for side, ref in enumerate((a_ref, b_ref)):
         for c in range(2):
             for half in range(2):
@@ -304,9 +316,8 @@
     return half, ktile, tile, found
 
 
-def key_kernel(idx_scale, meta, plan, g_ref, h_ref, iq_ref, iqt_ref, key_ref, keep, other, wide):
+def key_kernel(meta, plan, g_ref, h_ref, iq_ref, iqt_ref, key_ref, wide, keep, other):
     core = meta[1]
-    spread(iq_ref, wide, idx_scale)
     keep[...] = jnp.zeros(keep.shape, jnp.float32)
     other[...] = jnp.zeros(other.shape, jnp.float32)
 
@@ -326,10 +337,9 @@
     lax.fori_loop(0, TILES, body, 0, unroll=4)
 
 
-def query_kernel(groups, idx_scale, meta, g_ref, h_ref, iq_ref, key_ref, *refs):
-    dq, token, wide = refs[-3:]
+def query_kernel(groups, meta, g_ref, h_ref, iq_ref, key_ref, wide, *refs):
+    dq, token = refs[-2:]
     token[...] = jnp.zeros(token.shape, jnp.int32)
-    spread(iq_ref, wide, idx_scale)
     dq[...] = jnp.zeros(dq.shape, jnp.float32)
 
     def body(step, _):
@@ -359,6 +369,7 @@
 
     small = pl.CostEstimate(flops=1_000_000, bytes_accessed=1_000_000, transcendentals=0)
     flag = jax.ShapeDtypeStruct((8, 128), jnp.int32)
+    part = jax.ShapeDtypeStruct((TILES, 32, TILE), f32)
 
     index = jnp.arange(64, dtype=jnp.int32)
     bc, bk = index // 2, index % 2
@@ -378,9 +389,10 @@
     meta = jnp.concatenate(((blocks[0:1] + PER_TILE) // PER_TILE, core[None], blocks)).astype(jnp.int32)
     plan = pl.pallas_call(
         plan_kernel,
-        out_shape=jax.ShapeDtypeStruct((512,), jnp.int32),
+        out_shape=jax.ShapeDtypeStruct((768,), jnp.int32),
         in_specs=[smem()] * 5,
         out_specs=smem(),
+        compiler_params=params(1),
         cost_estimate=small,
         name="plan",
     )(meta, block_order, slot, row_a, row_b)
@@ -397,20 +409,14 @@
     iqw = jnp.concatenate((iq, weight), axis=1)
     iqt = iq.transpose(0, 3, 1, 2).reshape(2, 128, 1024)
     iq_high = swap_high(iqw)
-    group, iq_flag = lax.optimization_barrier((group, iq_high[0, 0, 0:8]))
+    group, plan, iq_flag = lax.optimization_barrier((group, plan, iq_high[0, 0, 0:8]))
     iq_both = jnp.stack((iqw, iq_high))
     iq_keep = lax.dynamic_slice_in_dim(iq_both, core * 32, 32, 3)
-    iq_other = swap_core(lax.dynamic_slice_in_dim(iq_both, (1 - core) * 32, 32, 3))
-
-    up, down = send(group, along(False, 1)), send(group, along(False, 3))
-    up, plan = lax.optimization_barrier((up, plan))
-    far_a, far_b = send(up[0:4], along(False, 1)), send(down[4:8], along(False, 3))
-    near = [group, up, down]
-    near = near + [swap_core(v) for v in near]
-
-    part = jax.ShapeDtypeStruct((TILES, 32, TILE), f32)
+    iq_send = lax.dynamic_slice_in_dim(iq_both, (1 - core) * 32, 32, 3)
+    iq_other = swap_core(iq_send)
+
     def targets(stage, outs, after, *arrays):
-        reads = 6 - 2 * stage
+        reads = (2, 4, 4)[stage]
         held = len(arrays) - 1 - reads
         return pl.pallas_call(
             functools.partial(target_kernel, stage, len(after)),
@@ -419,32 +425,49 @@
             out_specs=(vmem(),) * (2 + len(outs)),
             scratch_shapes=[pltpu.VMEM((64, HALF, 768), bf16), pltpu.SemaphoreType.DMA((reads,))],
             input_output_aliases={3 + reads: 0, 4 + reads: 1} if stage else {},
-            compiler_params=params(20),
+            compiler_params=params(16),
             cost_estimate=small,
-            name="targets_far" if stage else "targets_near",
+            name=("targets_first", "targets_near", "targets_far")[stage],
         )(meta, plan, *arrays, *after)
 
+    def take(value, start, after):
+        return pl.pallas_call(
+            lambda source, _after, out, sem: take_kernel(start, source, out, sem),
+            out_shape=jax.ShapeDtypeStruct((4, HALF, 768), bf16),
+            in_specs=[anywhere(), anywhere()],
+            out_specs=anywhere(),
+            scratch_shapes=[pltpu.SemaphoreType.DMA],
+            compiler_params=params(1),
+            cost_estimate=small,
+            name="take",
+        )(value, after)
+
+    up, down = send(group, along(False, 1)), send(group, along(False, 3))
     sums, sorted_keys, token, query = targets(
         0,
         (flag, jax.ShapeDtypeStruct((2, 640, 2048), bf16)),
-        (iq_flag, iq_other),
+        (iq_keep, iq_send),
         query_latent.transpose(1, 2, 0),
-        *near,
+        group,
+        swap_core(group),
         normalizer.T,
     )
+    up, down, token = lax.optimization_barrier((up, down, token))
+    far_a = send(take(up, 0, token), along(False, 1))
+    far_b = send(take(down, 4, token), along(False, 3))
+    near = (up, down, swap_core(up), swap_core(down))
+    sums, sorted_keys, token = targets(1, (flag,), (token, iq_flag, iq_other), query, *near, sums, sorted_keys)
     far_a, far_b, token = lax.optimization_barrier((far_a, far_b, token))
     far = (far_a, far_b, swap_core(far_a), swap_core(far_b))
-    _, sorted_keys, keep, other = targets(
-        1, (part, part), (token,), query, *far, sums, sorted_keys
-    )
+    _, sorted_keys, keep, other = targets(2, (part, part), (token,), query, *far, sums, sorted_keys)
     from_core = swap_core(other)
     from_high = swap_high((keep + from_core).astype(bf16))
 
-    prob = pl.pallas_call(
+    prob, scaled = pl.pallas_call(
         functools.partial(logit_kernel, idx_scale),
-        out_shape=part,
-        in_specs=[smem(), vmem(), vmem(), vmem()],
-        out_specs=vmem(),
+        out_shape=(part, jax.ShapeDtypeStruct((2, 1024, 128), f32)),
+        in_specs=[smem()] + [vmem()] * 4,
+        out_specs=(vmem(), vmem()),
         scratch_shapes=[
             pltpu.VMEM((2, 2, 2, 512, 128), f32),
             pltpu.VMEM((2, 32, TILE), f32),
@@ -453,7 +476,7 @@
         compiler_params=params(12),
         cost_estimate=small,
         name="logits",
-    )(meta, iq_keep, iq_other, sorted_keys)
+    )(meta, iq_keep, iq_other, sorted_keys, iqw)
 
     grad = pl.pallas_call(
         gradient_kernel,
@@ -469,26 +492,24 @@
 
     shard = jax.ShapeDtypeStruct((64, 32, 128), f32)
     dk_keep, dk_other = pl.pallas_call(
-        functools.partial(key_kernel, idx_scale),
+        key_kernel,
         out_shape=(shard, shard),
-        in_specs=[smem(), smem()] + [vmem()] * 5,
+        in_specs=[smem(), smem()] + [vmem()] * 6,
         out_specs=(vmem(), vmem()),
-        scratch_shapes=[pltpu.VMEM((2, 1024, 128), f32)],
         compiler_params=params(12),
         cost_estimate=small,
         name="keys",
-    )(meta, plan, grad, grad_other, iqw, iqt, sorted_keys)
+    )(meta, plan, grad, grad_other, iqw, iqt, sorted_keys, scaled)
     def queries(groups, *after):
         return pl.pallas_call(
-            functools.partial(query_kernel, groups, idx_scale),
+            functools.partial(query_kernel, groups),
             out_shape=(jax.ShapeDtypeStruct((2, 512, 128), f32), flag),
-            in_specs=[smem()] + [vmem()] * 4 + [anywhere()] * len(after),
+            in_specs=[smem()] + [vmem()] * 5 + [anywhere()] * len(after),
             out_specs=(vmem(), vmem()),
-            scratch_shapes=[pltpu.VMEM((2, 1024, 128), f32)],
             compiler_params=params(12),
             cost_estimate=small,
             name="queries",
-        )(meta, grad, grad_other, iqw, sorted_keys, *after)
+        )(meta, grad, grad_other, iqw, sorted_keys, scaled, *after)
 
     dk = dk_keep + swap_core(dk_other)
     low, token = queries((0, 1))

time: 125 us -> 125 us (level)
  local copies, waits for them, and re-layouts: 10.2 us -> 15.1 us
  starting transfers between devices: 34.5 us -> 30.8 us
  Pallas kernels: 51.5 us -> 53.1 us
  other arithmetic: 7.68 us -> 6.13 us
    ppermute x28, starting transfers between devices: 34.5 us -> 30.8 us  [send(): return lax.ppermute(value, ALL, permutation(move))]
    unnamed x23, local copies, waits for them, and re-layouts: 7.44 us -> 9.44 us
    reshape x1, local copies, waits for them, and re-layouts: 0.21 us -> 2.04 us  [per_device(): iqt = iq.transpose(0, 3, 1, 2).reshape(2, 128, 1024)]
    pallas_call x2 -> x3, Pallas kernels: 21.8 us -> 23.2 us  [targets(): pl.pallas_call(functools.partial(target_kernel, stage, len(after)), out_s...]
    pallas_call x5 -> x7, Pallas kernels: 28.6 us -> 28.7 us  [the longest x2 9.97 us: queries(): pl.pallas_call(functools.partial(query_kernel, groups), out_shape=(jax.Sh...]
  transfers between devices with their start and end apart: 28 -> 28, of which waited for: 14 -> 11; matrix products, arithmetic and copies ran while one was open for 8% -> 9% of each run, Pallas kernels for 29% -> 31%
where the time goes in v5:
time: 125 us
  Pallas kernels  53.1 us (42%)
  starting transfers between devices  30.8 us (25%)
  waiting for transfers between devices  18.3 us (15%)
  local copies, waits for them, and re-layouts  15.1 us (12%)
  other arithmetic  6.13 us (5%)
    ppermute x28, starting transfers between devices, send(): return lax.ppermute(value, ALL, permutation(move))  30.8 us
    pallas_call x3, Pallas kernels, targets(): pl.pallas_call(functools.partial(target_kernel, stage, len(after)), out_s...  23.2 us
    ppermute x28, waiting for transfers between devices, send(): return lax.ppermute(value, ALL, permutation(move))  18.3 us
    pallas_call x2, Pallas kernels, queries(): pl.pallas_call(functools.partial(query_kernel, groups), out_shape=(jax.Sh...  9.97 us
    unnamed x23, local copies, waits for them, and re-layouts  9.44 us
    pallas_call x1, Pallas kernels, per_device(): pl.pallas_call(functools.partial(logit_kernel, idx_scale), out_shape=(par...  7.88 us
    pallas_call x1, Pallas kernels, per_device(): pl.pallas_call(key_kernel, out_shape=(shard, shard), in_specs=[smem(), sm...  6.89 us
    pallas_call x1, Pallas kernels, per_device(): pl.pallas_call(plan_kernel, out_shape=jax.ShapeDtypeStruct((768,), jnp.in...  3.6 us
  transfers between devices with their start and end apart: 28, of which 11 were waited for; matrix products, arithmetic and copies ran while one was open for 9% of the time, Pallas kernels for 31%

profile of v5, /device:TPU:0, one launch (start us, length us, event | category | flops | bytes accessed | tf_op | source)
XLA Modules:
  0.0 124.5 jit_solution(10964104711021763070)
XLA Ops:
  3.2 2.0 %collective-permute-start = (bf16[64,768]{1,0:T(8,128)(2,1)S(1)}, bf16[64,768]{1,0:T(8,128)(2,1)S(1)}, u32[]{:S(2)}, u32[]{:S(2)}) collective-permute-start(bf16[64,768]{1,0:T(8,128)(2,1)S(1)} %get-tuple-element.72), channel_id=1, source_target_pairs={{0,16},{1,19},{2,18},{3,17},{4,20},{5,23},{6,22},{7,21},{8,24},{9,... | collective-permute-start | bytes 294920 | tf_op jit(solution)/shard_map/ppermute | solution.py:41
  7.6 3.6 %collective-permute-start.4 = (bf16[2,17,64,128]{3,2,1,0:T(8,128)(2,1)S(1)}, bf16[2,17,64,128]{3,2,1,0:T(8,128)(2,1)S(1)}, u32[]{:S(2)}, u32[]{:S(2)}) collective-permute-start(bf16[2,17,64,128]{3,2,1,0:T(8,128)(2,1)S(1)} %get-tuple-element.80.iq_ref), channel_id=1, source_target_pairs={{0,2},{1,3},{2,0},{3,1},{4,6},{5,7},{6,4},{7,5},{8,10},{9,11},{10,... | collective-permute-start | bytes 1671176 | tf_op jit(solution)/shard_map/ppermute | solution.py:41
  11.5 3.6 %plan.1 = s32[768]{0:T(1024)S(1)} custom-call(s32[4]{0:T(128)S(1)} %pad_add_fusion.meta, s32[64]{0:T(128)S(1)} %copy-done.5, s32[64]{0:T(128)S(1)} %get-tuple-element.88.slot, s32[64]{0:T(128)S(1)} %get-tuple-element.87.row, s32[64]{0:T(128)S(1)} %get-tuple-element.68.row_other), custom_call_target="tpu_custom_call" | custom-call | flops 1000000 | bytes 1000000 | tf_op jit(solution)/shard_map/plan/pallas_call | solution.py:390
  18.5 2.0 %collective-permute-start.3 = (bf16[2,64,768]{2,1,0:T(8,128)(2,1)S(1)}, bf16[2,64,768]{2,1,0:T(8,128)(2,1)S(1)}, u32[]{:S(2)}, u32[]{:S(2)}) collective-permute-start(bf16[2,64,768]{2,1,0:T(8,128)(2,1)S(1)} %pad_maximum_fusion.1), channel_id=1, source_target_pairs={{0,8},{1,65},{2,10},{3,67},{4,12},{5,69},{6,14},{7,71},{8,0},{9,73... | collective-permute-start | bytes 589832 | tf_op jit(solution)/shard_map/ppermute | solution.py:41
  23.5 2.1 %collective-permute-done.3 = bf16[2,64,768]{2,1,0:T(8,128)(2,1)S(1)} collective-permute-done((bf16[2,64,768]{2,1,0:T(8,128)(2,1)S(1)}, bf16[2,64,768]{2,1,0:T(8,128)(2,1)S(1)}, u32[]{:S(2)}, u32[]{:S(2)}) %collective-permute-start.3) | collective-permute-done | bytes 196640 | tf_op jit(solution)/shard_map/ppermute | solution.py:41
  28.7 1.7 %collective-permute-start.8 = (bf16[8,64,768]{2,1,0:T(8,128)(2,1)}, bf16[8,64,768]{2,1,0:T(8,128)(2,1)S(1)}, u32[]{:S(2)}, u32[]{:S(2)}) collective-permute-start(bf16[8,64,768]{2,1,0:T(8,128)(2,1)} %constant_dynamic-update-slice_fusion.refs_0_), channel_id=1, source_target_pairs={{0,96},{1,13},{2,98},{3,15},{4,100},{5,1},{6,102},{7,3},{8,104},{9... | collective-permute-start | bytes 2359304 | tf_op jit(solution)/shard_map/ppermute | solution.py:41
  32.8 2.3 %copy-done = bf16[128,32,576]{0,2,1:T(8,128)(2,1)S(1)} copy-done((bf16[128,32,576]{0,2,1:T(8,128)(2,1)S(1)}, bf16[128,32,576]{0,2,1:T(8,128)(2,1)}, u32[]{:S(2)}) %copy-start) | copy-done | bytes 4718616
  36.2 7.0 %targets_first.1 = (f32[69,64,128]{2,1,0:T(8,128)S(1)}, bf16[4096,128]{1,0:T(8,128)(2,1)S(1)}, s32[8,128]{1,0:T(8,128)S(1)}, bf16[2,640,2048]{2,1,0:T(8,128)(2,1)S(1)}) custom-call(s32[4]{0:T(128)S(1)} %pad_add_fusion.meta, s32[768]{0:T(1024)S(1)} %plan.1, bf16[32,576,128]{2,1,0:T(8,128)(2,1)S(1)} %bitcast.61, ...), custom_call_target="tpu_custom_call" | custom-call | flops 1000000 | bytes 1000000 | tf_op jit(solution)/shard_map/targets_first/pallas_call | solution.py:421
  44.3 2.7 %collective-permute-start.10 = (bf16[4,64,768]{2,1,0:T(8,128)(2,1)S(1)}, bf16[4,64,768]{2,1,0:T(8,128)(2,1)S(1)}, u32[]{:S(2)}, u32[]{:S(2)}) collective-permute-start(bf16[4,64,768]{2,1,0:T(8,128)(2,1)S(1)} %take.3), channel_id=1, source_target_pairs={{0,96},{1,13},{2,98},{3,15},{4,100},{5,1},{6,102},{7,3},{8,104},{9... | collective-permute-start | bytes 1179656 | tf_op jit(solution)/shard_map/ppermute | solution.py:41
  47.5 9.3 %targets_near.1 = (f32[69,64,128]{2,1,0:T(8,128)S(1)}, bf16[4096,128]{1,0:T(8,128)(2,1)S(1)}, s32[8,128]{1,0:T(8,128)S(1)}) custom-call(s32[4]{0:T(128)S(1)} %pad_add_fusion.meta, s32[768]{0:T(1024)S(1)} %plan.1, bf16[2,640,2048]{2,1,0:T(8,128)(2,1)S(1)} %get-tuple-element.37.q_ref, ...), custom_call_target="tpu_custom_call", output_to_operand_aliasing={{0}: (7, {}), {1}: (8, {})} | custom-call | flops 1000000 | bytes 1000000 | tf_op jit(solution)/shard_map/targets_near/pallas_call | solution.py:421
  59.4 7.0 %targets_far.1 = (f32[69,64,128]{2,1,0:T(8,128)S(1)}, bf16[4096,128]{1,0:T(8,128)(2,1)S(1)}, f32[17,32,256]{2,1,0:T(8,128)S(1)}, f32[17,32,256]{2,1,0:T(8,128)S(1)}) custom-call(s32[4]{0:T(128)S(1)} %pad_add_fusion.meta, s32[768]{0:T(1024)S(1)} %plan.1, ...), custom_call_target="tpu_custom_call", output_to_operand_aliasing={{0}: (7, {}), {1}: (8, {})} | custom-call | flops 1000000 | bytes 1000000 | tf_op jit(solution)/shard_map/targets_far/pallas_call | solution.py:421
  66.6 1.8 %collective-permute-done.15.b_ref = f32[17,32,256]{2,1,0:T(8,128)S(1)} collective-permute-done((f32[17,32,256]{2,1,0:T(8,128)S(1)}, f32[17,32,256]{2,1,0:T(8,128)S(1)}, u32[]{:S(2)}, u32[]{:S(2)}) %collective-permute-start.15) | collective-permute-done | bytes 557088 | tf_op jit(solution)/shard_map/ppermute | solution.py:41
  68.6 7.9 %logits.1 = (f32[17,32,256]{2,1,0:T(8,128)S(1)}, f32[2,1024,128]{2,1,0:T(8,128)S(1)}) custom-call(s32[4]{0:T(128)S(1)} %pad_add_fusion.meta, bf16[2,2,17,32,128]{4,3,2,1,0:T(8,128)(2,1)S(1)} %get-tuple-element.74.refs_3_.a_ref, bf16[2,2,17,32,128]{4,3,2,1,0:T(8,128)(2,1)S(1)} %collective-permute-done.5.refs_8_.b_ref, ...), custom_call_target="tpu_custom_call" | custom-call | flops 1000000 | bytes 1000000 | tf_op jit(solution)/shard_map/logits/pallas_call | solution.py:466
  76.5 2.3 %collective-permute-done.16.c_ref = bf16[17,32,256]{2,1,0:T(8,128)(2,1)S(1)} collective-permute-done((bf16[17,32,256]{2,1,0:T(8,128)(2,1)S(1)}, bf16[17,32,256]{2,1,0:T(8,128)(2,1)S(1)}, u32[]{:S(2)}, u32[]{:S(2)}) %collective-permute-start.16) | collective-permute-done | bytes 278560 | tf_op jit(solution)/shard_map/ppermute | solution.py:41
  80.9 2.0 %copy.28.iqt_ref = bf16[2,128,1024]{2,1,0:T(8,128)(2,1)} copy(bf16[2,128,1024]{1,2,0:T(8,128)(2,1)} %bitcast.68) | data formatting | bytes 1048576 | tf_op jit(solution)/shard_map/reshape | solution.py:410
  84.0 6.9 %keys.1 = (f32[64,32,128]{2,1,0:T(8,128)S(1)}, f32[64,32,128]{2,1,0:T(8,128)S(1)}) custom-call(s32[4]{0:T(128)S(1)} %pad_add_fusion.meta, s32[768]{0:T(1024)S(1)} %plan.1, bf16[17,32,256]{2,1,0:T(8,128)(2,1)S(1)} %gradient.1.g_ref, bf16[17,32,256]{2,1,0:T(8,128)(2,1)S(1)} %collective-permute-done.17.h_ref, ...), custom_call_target="tpu_custom_call" | custom-call | flops 1000000 | bytes 1000000 | tf_op jit(solution)/shard_map/keys/pallas_call | solution.py:494
  91.5 2.3 %collective-permute-done.18 = f32[64,32,128]{2,1,0:T(8,128)S(1)} collective-permute-done((f32[64,32,128]{2,1,0:T(8,128)S(1)}, f32[64,32,128]{2,1,0:T(8,128)S(1)}, u32[]{:S(2)}, u32[]{:S(2)}) %collective-permute-start.18) | collective-permute-done | bytes 1048608 | tf_op jit(solution)/shard_map/ppermute | solution.py:41
  95.2 2.2 %collective-permute-start.20 = (f32[4,4,32,128]{3,2,1,0:T(8,128)S(1)}, f32[4,4,32,128]{3,2,1,0:T(8,128)S(1)}, u32[]{:S(2)}, u32[]{:S(2)}) collective-permute-start(f32[4,4,32,128]{3,2,1,0:T(8,128)S(1)} %bitcast.76), channel_id=1, source_target_pairs={{0,12},{1,97},{2,14},{3,99},{4,0},{5,101},{6,2},{7,103},{8,4},{9,1... | collective-permute-start | bytes 786440 | tf_op jit(solution)/shard_map/ppermute | solution.py:41
  97.4 5.0 %queries.2 = (f32[2,512,128]{2,1,0:T(8,128)S(1)}, s32[8,128]{1,0:T(8,128)S(1)}) custom-call(s32[4]{0:T(128)S(1)} %pad_add_fusion.meta, bf16[17,32,256]{2,1,0:T(8,128)(2,1)S(1)} %gradient.1.g_ref, bf16[17,32,256]{2,1,0:T(8,128)(2,1)S(1)} %collective-permute-done.17.h_ref, bf16[2,17,64,128]{3,2,1,0:T(8,128)(2,1)S(1)} %get-tuple-element.80.iq_ref, ...), custom_call_target="tpu_custom_call" | custom-call | flops 1000000 | bytes 1000000 | tf_op jit(solution)/shard_map/queries/pallas_call | solution.py:504
  102.4 1.7 %collective-permute-done.20 = f32[4,4,32,128]{3,2,1,0:T(8,128)S(1)} collective-permute-done((f32[4,4,32,128]{3,2,1,0:T(8,128)S(1)}, f32[4,4,32,128]{3,2,1,0:T(8,128)S(1)}, u32[]{:S(2)}, u32[]{:S(2)}) %collective-permute-start.20) | collective-permute-done | bytes 262176 | tf_op jit(solution)/shard_map/ppermute | solution.py:41
  106.6 2.1 %collective-permute-start.23 = (f32[4,32,128]{2,1,0:T(8,128)S(1)}, f32[4,32,128]{2,1,0:T(8,128)S(1)}, u32[]{:S(2)}, u32[]{:S(2)}) collective-permute-start(f32[4,32,128]{2,1,0:T(8,128)S(1)} %get-tuple-element.83), channel_id=1, source_target_pairs={{0,96},{1,13},{2,98},{3,15},{4,100},{5,1},{6,102},{7,3},{8,104},{9... | collective-permute-start | bytes 196616 | tf_op jit(solution)/shard_map/ppermute | solution.py:41
  110.3 5.0 %queries.3 = (f32[2,512,128]{2,1,0:T(8,128)S(1)}, s32[8,128]{1,0:T(8,128)S(1)}) custom-call(s32[4]{0:T(128)S(1)} %pad_add_fusion.meta, bf16[17,32,256]{2,1,0:T(8,128)(2,1)S(1)} %gradient.1.g_ref, bf16[17,32,256]{2,1,0:T(8,128)(2,1)S(1)} %collective-permute-done.17.h_ref, bf16[2,17,64,128]{3,2,1,0:T(8,128)(2,1)S(1)} %get-tuple-element.80.iq_ref, ...), custom_call_target="tpu_custom_call" | custom-call | flops 1000000 | bytes 1000000 | tf_op jit(solution)/shard_map/queries/pallas_call | solution.py:504
  115.5 3.2 %collective-permute-start.26 = (f32[32,128]{1,0:T(8,128)S(1)}, f32[32,128]{1,0:T(8,128)S(1)}, u32[]{:S(2)}, u32[]{:S(2)}) collective-permute-start(f32[32,128]{1,0:T(8,128)S(1)} %get-tuple-element.86), channel_id=1, source_target_pairs={{0,18},{1,19},{2,16},{3,17},{4,22},{5,23},{6,20},{7,21},{8,26},{9,... | collective-permute-start | bytes 49160 | tf_op jit(solution)/shard_map/ppermute | solution.py:41
  120.4 3.5 %collective-permute-done.27 = f32[32,128]{1,0:T(8,128)S(1)} collective-permute-done((f32[32,128]{1,0:T(8,128)S(1)}, f32[32,128]{1,0:T(8,128)S(1)}, u32[]{:S(2)}, u32[]{:S(2)}) %collective-permute-start.27) | collective-permute-done | bytes 16416 | tf_op jit(solution)/shard_map/ppermute | solution.py:41
  (93 shorter events, 34.2 us)
Async XLA Ops:
  3.2 11.9 %collective-permute-start = (bf16[64,768]{1,0:T(8,128)(2,1)S(1)}, bf16[64,768]{1,0:T(8,128)(2,1)S(1)}, u32[]{:S(2)}, u32[]{:S(2)}) collective-permute-start(bf16[64,768]{1,0:T(8,128)(2,1)S(1)} %get-tuple-element.72), channel_id=1, source_target_pairs={{0,16},{1,19},{2,18},{3,17},{4,20},{5,23},{6,22},{7,21},{8,24},{9,... | collective-permute-start | bytes 294920 | tf_op jit(solution)/shard_map/ppermute | solution.py:41
  7.6 18.7 %collective-permute-start.4 = (bf16[2,17,64,128]{3,2,1,0:T(8,128)(2,1)S(1)}, bf16[2,17,64,128]{3,2,1,0:T(8,128)(2,1)S(1)}, u32[]{:S(2)}, u32[]{:S(2)}) collective-permute-start(bf16[2,17,64,128]{3,2,1,0:T(8,128)(2,1)S(1)} %get-tuple-element.80.iq_ref), channel_id=1, source_target_pairs={{0,2},{1,3},{2,0},{3,1},{4,6},{5,7},{6,4},{7,5},{8,10},{9,11},{10,... | collective-permute-start | bytes 1671176 | tf_op jit(solution)/shard_map/ppermute | solution.py:41
  15.2 6.9 %collective-permute-start.1 = (bf16[2,64,768]{2,1,0:T(8,128)(2,1)S(1)}, bf16[2,64,768]{2,1,0:T(8,128)(2,1)S(1)}, u32[]{:S(2)}, u32[]{:S(2)}) collective-permute-start(bf16[2,64,768]{2,1,0:T(8,128)(2,1)S(1)} %pad_maximum_fusion.1), channel_id=1, source_target_pairs={{0,4},{1,33},{2,6},{3,35},{4,8},{5,37},{6,10},{7,39},{8,12},{9,41}... | collective-permute-start | bytes 589832 | tf_op jit(solution)/shard_map/ppermute | solution.py:41
  16.8 6.0 %collective-permute-start.2 = (bf16[2,64,768]{2,1,0:T(8,128)(2,1)S(1)}, bf16[2,64,768]{2,1,0:T(8,128)(2,1)S(1)}, u32[]{:S(2)}, u32[]{:S(2)}) collective-permute-start(bf16[2,64,768]{2,1,0:T(8,128)(2,1)S(1)} %pad_maximum_fusion.1), channel_id=1, source_target_pairs={{0,12},{1,97},{2,14},{3,99},{4,0},{5,101},{6,2},{7,103},{8,4},{9,1... | collective-permute-start | bytes 589832 | tf_op jit(solution)/shard_map/ppermute | solution.py:41
  18.5 7.2 %collective-permute-start.3 = (bf16[2,64,768]{2,1,0:T(8,128)(2,1)S(1)}, bf16[2,64,768]{2,1,0:T(8,128)(2,1)S(1)}, u32[]{:S(2)}, u32[]{:S(2)}) collective-permute-start(bf16[2,64,768]{2,1,0:T(8,128)(2,1)S(1)} %pad_maximum_fusion.1), channel_id=1, source_target_pairs={{0,8},{1,65},{2,10},{3,67},{4,12},{5,69},{6,14},{7,71},{8,0},{9,73... | collective-permute-start | bytes 589832 | tf_op jit(solution)/shard_map/ppermute | solution.py:41
  27.2 4.7 %collective-permute-start.6 = (bf16[8,64,768]{2,1,0:T(8,128)(2,1)}, bf16[8,64,768]{2,1,0:T(8,128)(2,1)S(1)}, u32[]{:S(2)}, u32[]{:S(2)}) collective-permute-start(bf16[8,64,768]{2,1,0:T(8,128)(2,1)} %constant_dynamic-update-slice_fusion.refs_0_), channel_id=1, source_target_pairs={{0,1},{1,0},{2,3},{3,2},{4,5},{5,4},{6,7},{7,6},{8,9},{9,8},{10,11... | collective-permute-start | bytes 2359304 | tf_op jit(solution)/shard_map/ppermute | solution.py:41
  27.2 16.0 %collective-permute-start.7 = (bf16[8,64,768]{2,1,0:T(8,128)(2,1)}, bf16[8,64,768]{2,1,0:T(8,128)(2,1)S(1)}, u32[]{:S(2)}, u32[]{:S(2)}) collective-permute-start(bf16[8,64,768]{2,1,0:T(8,128)(2,1)} %constant_dynamic-update-slice_fusion.refs_0_), channel_id=1, source_target_pairs={{0,32},{1,5},{2,34},{3,7},{4,36},{5,9},{6,38},{7,11},{8,40},{9,13}... | collective-permute-start | bytes 2359304 | tf_op jit(solution)/shard_map/ppermute | solution.py:41
  28.7 14.6 %collective-permute-start.8 = (bf16[8,64,768]{2,1,0:T(8,128)(2,1)}, bf16[8,64,768]{2,1,0:T(8,128)(2,1)S(1)}, u32[]{:S(2)}, u32[]{:S(2)}) collective-permute-start(bf16[8,64,768]{2,1,0:T(8,128)(2,1)} %constant_dynamic-update-slice_fusion.refs_0_), channel_id=1, source_target_pairs={{0,96},{1,13},{2,98},{3,15},{4,100},{5,1},{6,102},{7,3},{8,104},{9... | collective-permute-start | bytes 2359304 | tf_op jit(solution)/shard_map/ppermute | solution.py:41
  43.2 4.3 %collective-permute-start.11 = (bf16[8,64,768]{2,1,0:T(8,128)(2,1)S(1)}, bf16[8,64,768]{2,1,0:T(8,128)(2,1)S(1)}, u32[]{:S(2)}, u32[]{:S(2)}) collective-permute-start(bf16[8,64,768]{2,1,0:T(8,128)(2,1)S(1)} %collective-permute-done.7.source.refs_0_), channel_id=1, source_target_pairs={{0,1},{1,0},{2,3},{3,2},{4,5},{5,4},{6,7},{7,6},{8,9},{9,8},{10,11... | collective-permute-start | bytes 2359304 | tf_op jit(solution)/shard_map/ppermute | solution.py:41
  43.3 4.2 %collective-permute-start.12 = (bf16[8,64,768]{2,1,0:T(8,128)(2,1)S(1)}, bf16[8,64,768]{2,1,0:T(8,128)(2,1)S(1)}, u32[]{:S(2)}, u32[]{:S(2)}) collective-permute-start(bf16[8,64,768]{2,1,0:T(8,128)(2,1)S(1)} %collective-permute-done.8.source.refs_1_), channel_id=1, source_target_pairs={{0,1},{1,0},{2,3},{3,2},{4,5},{5,4},{6,7},{7,6},{8,9},{9,8},{10,11... | collective-permute-start | bytes 2359304 | tf_op jit(solution)/shard_map/ppermute | solution.py:41
  43.8 3.7 %collective-permute-start.5 = (bf16[2,2,17,32,128]{4,3,2,1,0:T(8,128)(2,1)S(1)}, bf16[2,2,17,32,128]{4,3,2,1,0:T(8,128)(2,1)S(1)}, u32[]{:S(2)}, u32[]{:S(2)}) collective-permute-start(bf16[2,2,17,32,128]{4,3,2,1,0:T(8,128)(2,1)S(1)} %get-tuple-element.73.refs_4_), channel_id=1, source_target_pairs={{0,1},{1,0},{2,3},{3,2},{4,5},{5,4},{6,7},{7,6},{8,9},{9,8},{10,11... | collective-permute-start | bytes 1671176 | tf_op jit(solution)/shard_map/ppermute | solution.py:41
  44.3 12.5 %collective-permute-start.10 = (bf16[4,64,768]{2,1,0:T(8,128)(2,1)S(1)}, bf16[4,64,768]{2,1,0:T(8,128)(2,1)S(1)}, u32[]{:S(2)}, u32[]{:S(2)}) collective-permute-start(bf16[4,64,768]{2,1,0:T(8,128)(2,1)S(1)} %take.3), channel_id=1, source_target_pairs={{0,96},{1,13},{2,98},{3,15},{4,100},{5,1},{6,102},{7,3},{8,104},{9... | collective-permute-start | bytes 1179656 | tf_op jit(solution)/shard_map/ppermute | solution.py:41
  47.0 9.8 %collective-permute-start.9 = (bf16[4,64,768]{2,1,0:T(8,128)(2,1)S(1)}, bf16[4,64,768]{2,1,0:T(8,128)(2,1)S(1)}, u32[]{:S(2)}, u32[]{:S(2)}) collective-permute-start(bf16[4,64,768]{2,1,0:T(8,128)(2,1)S(1)} %take.2), channel_id=1, source_target_pairs={{0,32},{1,5},{2,34},{3,7},{4,36},{5,9},{6,38},{7,11},{8,40},{9,13}... | collective-permute-start | bytes 1179656 | tf_op jit(solution)/shard_map/ppermute | solution.py:41
  68.5 10.3 %collective-permute-start.16 = (bf16[17,32,256]{2,1,0:T(8,128)(2,1)S(1)}, bf16[17,32,256]{2,1,0:T(8,128)(2,1)S(1)}, u32[]{:S(2)}, u32[]{:S(2)}) collective-permute-start(bf16[17,32,256]{2,1,0:T(8,128)(2,1)S(1)} %add_convert_fusion), channel_id=1, source_target_pairs={{0,2},{1,3},{2,0},{3,1},{4,6},{5,7},{6,4},{7,5},{8,10},{9,11},{10,... | collective-permute-start | bytes 835592 | tf_op jit(solution)/shard_map/ppermute | solution.py:41
  79.9 3.1 %collective-permute-start.17 = (bf16[17,32,256]{2,1,0:T(8,128)(2,1)S(1)}, bf16[17,32,256]{2,1,0:T(8,128)(2,1)S(1)}, u32[]{:S(2)}, u32[]{:S(2)}) collective-permute-start(bf16[17,32,256]{2,1,0:T(8,128)(2,1)S(1)} %gradient.1.g_ref), channel_id=1, source_target_pairs={{0,1},{1,0},{2,3},{3,2},{4,5},{5,4},{6,7},{7,6},{8,9},{9,8},{10,11... | collective-permute-start | bytes 835592 | tf_op jit(solution)/shard_map/ppermute | solution.py:41
  94.1 8.3 %collective-permute-start.19 = (f32[4,4,32,128]{3,2,1,0:T(8,128)S(1)}, f32[4,4,32,128]{3,2,1,0:T(8,128)S(1)}, u32[]{:S(2)}, u32[]{:S(2)}) collective-permute-start(f32[4,4,32,128]{3,2,1,0:T(8,128)S(1)} %bitcast.77), channel_id=1, source_target_pairs={{0,4},{1,33},{2,6},{3,35},{4,8},{5,37},{6,10},{7,39},{8,12},{9,41}... | collective-permute-start | bytes 786440 | tf_op jit(solution)/shard_map/ppermute | solution.py:41
  95.2 8.9 %collective-permute-start.20 = (f32[4,4,32,128]{3,2,1,0:T(8,128)S(1)}, f32[4,4,32,128]{3,2,1,0:T(8,128)S(1)}, u32[]{:S(2)}, u32[]{:S(2)}) collective-permute-start(f32[4,4,32,128]{3,2,1,0:T(8,128)S(1)} %bitcast.76), channel_id=1, source_target_pairs={{0,12},{1,97},{2,14},{3,99},{4,0},{5,101},{6,2},{7,103},{8,4},{9,1... | collective-permute-start | bytes 786440 | tf_op jit(solution)/shard_map/ppermute | solution.py:41
  97.4 7.9 %collective-permute-start.21 = (f32[4,4,32,128]{3,2,1,0:T(8,128)S(1)}, f32[4,4,32,128]{3,2,1,0:T(8,128)S(1)}, u32[]{:S(2)}, u32[]{:S(2)}) collective-permute-start(f32[4,4,32,128]{3,2,1,0:T(8,128)S(1)} %bitcast.75), channel_id=1, source_target_pairs={{0,8},{1,65},{2,10},{3,67},{4,12},{5,69},{6,14},{7,71},{8,0},{9,73... | collective-permute-start | bytes 786440 | tf_op jit(solution)/shard_map/ppermute | solution.py:41
  105.4 9.9 %collective-permute-start.22 = (f32[4,32,128]{2,1,0:T(8,128)S(1)}, f32[4,32,128]{2,1,0:T(8,128)S(1)}, u32[]{:S(2)}, u32[]{:S(2)}) collective-permute-start(f32[4,32,128]{2,1,0:T(8,128)S(1)} %get-tuple-element.81), channel_id=1, source_target_pairs={{0,32},{1,5},{2,34},{3,7},{4,36},{5,9},{6,38},{7,11},{8,40},{9,13}... | collective-permute-start | bytes 196616 | tf_op jit(solution)/shard_map/ppermute | solution.py:41
  106.6 8.7 %collective-permute-start.23 = (f32[4,32,128]{2,1,0:T(8,128)S(1)}, f32[4,32,128]{2,1,0:T(8,128)S(1)}, u32[]{:S(2)}, u32[]{:S(2)}) collective-permute-start(f32[4,32,128]{2,1,0:T(8,128)S(1)} %get-tuple-element.83), channel_id=1, source_target_pairs={{0,96},{1,13},{2,98},{3,15},{4,100},{5,1},{6,102},{7,3},{8,104},{9... | collective-permute-start | bytes 196616 | tf_op jit(solution)/shard_map/ppermute | solution.py:41
  108.7 6.7 %collective-permute-start.24 = (f32[4,32,128]{2,1,0:T(8,128)S(1)}, f32[4,32,128]{2,1,0:T(8,128)S(1)}, u32[]{:S(2)}, u32[]{:S(2)}) collective-permute-start(f32[4,32,128]{2,1,0:T(8,128)S(1)} %get-tuple-element.82), channel_id=1, source_target_pairs={{0,64},{1,9},{2,66},{3,11},{4,68},{5,13},{6,70},{7,15},{8,72},{9,1... | collective-permute-start | bytes 196616 | tf_op jit(solution)/shard_map/ppermute | solution.py:41
  115.4 5.0 %collective-permute-start.25 = (f32[32,128]{1,0:T(8,128)S(1)}, f32[32,128]{1,0:T(8,128)S(1)}, u32[]{:S(2)}, u32[]{:S(2)}) collective-permute-start(f32[32,128]{1,0:T(8,128)S(1)} %get-tuple-element.84), channel_id=1, source_target_pairs={{0,16},{1,17},{2,18},{3,19},{4,20},{5,21},{6,22},{7,23},{8,24},{9,... | collective-permute-start | bytes 49160 | tf_op jit(solution)/shard_map/ppermute | solution.py:41
  115.5 4.9 %collective-permute-start.26 = (f32[32,128]{1,0:T(8,128)S(1)}, f32[32,128]{1,0:T(8,128)S(1)}, u32[]{:S(2)}, u32[]{:S(2)}) collective-permute-start(f32[32,128]{1,0:T(8,128)S(1)} %get-tuple-element.86), channel_id=1, source_target_pairs={{0,18},{1,19},{2,16},{3,17},{4,22},{5,23},{6,20},{7,21},{8,26},{9,... | collective-permute-start | bytes 49160 | tf_op jit(solution)/shard_map/ppermute | solution.py:41
  118.7 5.2 %collective-permute-start.27 = (f32[32,128]{1,0:T(8,128)S(1)}, f32[32,128]{1,0:T(8,128)S(1)}, u32[]{:S(2)}, u32[]{:S(2)}) collective-permute-start(f32[32,128]{1,0:T(8,128)S(1)} %get-tuple-element.85), channel_id=1, source_target_pairs={{0,2},{1,3},{2,0},{3,1},{4,6},{5,7},{6,4},{7,5},{8,10},{9,11},{10,... | collective-permute-start | bytes 49160 | tf_op jit(solution)/shard_map/ppermute | solution.py:41
  (13 other events, 29.3 us)

commit v6 on v5

--- a/solution.py
+++ b/solution.py
@@ -13,7 +13,7 @@
 TILE = 256
 PER_TILE = TILE // HALF
 TILES = 17
-LISTS = (0, 8 * 4, 24 * 4)
+LISTS = ((0, 16), (32, 64), (96, 112))
 UNUSED = 32 * 4
 SLOT, GOAL, ROW, ROW_OTHER, POSITION, COUNT = 0, 256, 512, 576, 640, 704
 MLA_SCALE = 192.0**-0.5
@@ -79,34 +79,38 @@
     return half, step - half * meta[0]
 
 
-def plan_kernel(meta, order, slot, row, row_other, plan):
-    ends = tuple(jnp.int32(start) for start in LISTS)
-    for half in range(2):
-        limit, base = meta[2 + half], half * PER_TILE * meta[0]
-
-        def step(i, ends, half=half, limit=limit, base=base):
-            position, at = order[i], slot[i]
-            if half == 0:
-                plan[ROW + position] = row[i]
-                plan[ROW_OTHER + position] = row_other[i]
-                plan[POSITION + at] = position
-            ring = (at // 8) % 4
-            stage = jnp.where(ring == 0, 0, jnp.where(ring == 3, 2, 1))
-            seen = jnp.where(position <= limit, 1, 0)
-            to = jnp.where(stage == 0, ends[0], jnp.where(stage == 1, ends[1], ends[2]))
+def plan_kernel(meta, order, slot, row, row_other, _after, plan):
+    base = PER_TILE * meta[0]
+
+    def step(i, ends):
+        position, at = order[i], slot[i]
+        plan[ROW + position] = row[i]
+        plan[ROW_OTHER + position] = row_other[i]
+        plan[POSITION + at] = position
+        ring = (at // 8) % 4
+        stage = jnp.where(ring == 0, 0, jnp.where(ring == 3, 2, 1))
+        later = []
+        for half in range(2):
+            mine = ends[3 * half : 3 * half + 3]
+            seen = jnp.where(position <= meta[2 + half], 1, 0)
+            to = jnp.where(stage == 0, mine[0], jnp.where(stage == 1, mine[1], mine[2]))
             to = jnp.where(seen == 1, to, UNUSED)
             plan[SLOT + to] = at
-            plan[GOAL + to] = position + base
-            return tuple(end + jnp.where(stage == part, seen, 0) for part, end in enumerate(ends))
-
-        ends = lax.fori_loop(0, 64, step, ends, unroll=4)
-        for part, end in enumerate(ends):
+            plan[GOAL + to] = position + base * half
+            later += [end + jnp.where(stage == part, seen, 0) for part, end in enumerate(mine)]
+        return tuple(later)
+
+    ends = tuple(jnp.int32(LISTS[part][half]) for half in range(2) for part in range(3))
+    ends = lax.fori_loop(0, 64, step, ends, unroll=8)
+    for half in range(2):
+        for part in range(3):
+            end = ends[3 * half + part]
+            tiles = (end - LISTS[part][half] + 3) // 4
+            plan[COUNT + 3 * half + part] = tiles
             for u in range(3):
-                plan[SLOT + end + u] = (0, 8, 24)[part]
-                plan[GOAL + end + u] = 68
-        ends = tuple((end + 3) // 4 * 4 for end in ends)
-        for part, end in enumerate(ends):
-            plan[COUNT + 3 * half + part] = (end - LISTS[part]) // 4
+                to = jnp.where(end + u < LISTS[part][half] + 4 * tiles, end + u, UNUSED)
+                plan[SLOT + to] = (0, 8, 24)[part]
+                plan[GOAL + to] = 68
 
 
 def pack(q_ref, n_ref, out):
@@ -167,11 +171,12 @@
 
         lax.fori_loop(base, base + count * size, sort, 0, unroll=4)
     scale = MLA_SCALE * math.log2(math.e)
-    first, tiles = plan[COUNT + stage], plan[COUNT + 3 + stage]
+    first = plan[COUNT + stage]
+    tiles = first + plan[COUNT + 3 + stage]
 
     def body(t):
         half = jnp.where(t >= first, 1, 0)
-        at = LISTS[stage] + t * PER_TILE
+        at = LISTS[stage][0] + t * PER_TILE + half * (LISTS[stage][1] - LISTS[stage][0] - first * PER_TILE)
         tile = jnp.concatenate([keys[plan[SLOT + at + u], :, 0:640] for u in range(PER_TILE)], axis=0)
         total = jnp.zeros((TILE, 128), jnp.float32)
         for g in range(8):
@@ -219,7 +224,9 @@
     return cols <= rows
 
 
-def logit_kernel(idx_scale, meta, a_ref, b_ref, key_ref, iq_ref, out, scaled, wide, top, norm):
+def logit_kernel(idx_scale, meta, a_ref, b_ref, key_ref, iq_ref, out, scaled, iqt, wide, top, norm):
+    for half in range(2):
+        iqt[half] = iq_ref[half, 0:16].reshape(1024, 128).T
     spread(iq_ref, scaled, idx_scale)
     for side, ref in enumerate((a_ref, b_ref)):
         for c in range(2):
@@ -387,27 +394,25 @@
     row_a, row_b = qy * 16 + qx * 4 + qz, qx * 16 + qy * 4 + qz
     row_a, row_b = jnp.where(core == 0, row_a, row_b), jnp.where(core == 0, row_b, row_a)
     meta = jnp.concatenate(((blocks[0:1] + PER_TILE) // PER_TILE, core[None], blocks)).astype(jnp.int32)
-    plan = pl.pallas_call(
-        plan_kernel,
-        out_shape=jax.ShapeDtypeStruct((768,), jnp.int32),
-        in_specs=[smem()] * 5,
-        out_specs=smem(),
-        compiler_params=params(1),
-        cost_estimate=small,
-        name="plan",
-    )(meta, block_order, slot, row_a, row_b)
-
     ones = (lax.broadcasted_iota(jnp.int32, (128, 64), 1) < 3).astype(bf16)
     packed = jnp.concatenate((key_latent, ones, indexer_key), axis=1)
     own = lax.dynamic_slice_in_dim(packed, core * HALF, HALF, 0)
     beside = send(own, lambda x, z, y, k: (x, z + 1 - 2 * k, y, k))
     pair = jnp.stack((own, beside))
+    plan = pl.pallas_call(
+        plan_kernel,
+        out_shape=jax.ShapeDtypeStruct((768,), jnp.int32),
+        in_specs=[smem()] * 5 + [anywhere()],
+        out_specs=smem(),
+        compiler_params=params(1),
+        cost_estimate=small,
+        name="plan",
+    )(meta, block_order, slot, row_a, row_b, pair)
     legs = [pair] + [send(pair, along(True, shift)) for shift in (1, 3, 2)]
     group = jnp.concatenate(legs, axis=0)
     iq = indexer_query.reshape(2, HALF, 16, 128).transpose(0, 2, 1, 3)
     weight = jnp.pad(indexer_weight.reshape(2, 1, HALF, 16), ((0, 0), (0, 0), (0, 0), (0, 112)))
     iqw = jnp.concatenate((iq, weight), axis=1)
-    iqt = iq.transpose(0, 3, 1, 2).reshape(2, 128, 1024)
     iq_high = swap_high(iqw)
     group, plan, iq_flag = lax.optimization_barrier((group, plan, iq_high[0, 0, 0:8]))
     iq_both = jnp.stack((iqw, iq_high))
@@ -463,11 +468,11 @@
     from_core = swap_core(other)
     from_high = swap_high((keep + from_core).astype(bf16))
 
-    prob, scaled = pl.pallas_call(
+    prob, scaled, iqt = pl.pallas_call(
         functools.partial(logit_kernel, idx_scale),
-        out_shape=(part, jax.ShapeDtypeStruct((2, 1024, 128), f32)),
+        out_shape=(part, jax.ShapeDtypeStruct((2, 1024, 128), f32), jax.ShapeDtypeStruct((2, 128, 1024), bf16)),
         in_specs=[smem()] + [vmem()] * 4,
-        out_specs=(vmem(), vmem()),
+        out_specs=(vmem(), vmem(), vmem()),
         scratch_shapes=[
             pltpu.VMEM((2, 2, 2, 512, 128), f32),
             pltpu.VMEM((2, 32, TILE), f32),

time: 125 us -> 117 us (0.936)
  local copies, waits for them, and re-layouts: 15.1 us -> 6.42 us
  starting transfers between devices: 30.8 us -> 33.3 us
  other arithmetic: 6.13 us -> 4.51 us
    unnamed x23 -> x15, local copies, waits for them, and re-layouts: 9.44 us -> 4.37 us
    ppermute x28, starting transfers between devices: 30.8 us -> 33.3 us  [send(): return lax.ppermute(value, ALL, permutation(move))]
    reshape x1 -> x0, local copies, waits for them, and re-layouts: 2.04 us -> none  [per_device(): iqt = iq.transpose(0, 3, 1, 2).reshape(2, 128, 1024)]
  transfers between devices with their start and end apart: 28 -> 28, of which waited for: 11 -> 11; matrix products, arithmetic and copies ran while one was open for 9% -> 4% of each run, Pallas kernels for 31% -> 33%
where the time goes in v6:
time: 117 us
  Pallas kernels  52.4 us (45%)
  starting transfers between devices  33.3 us (28%)
  waiting for transfers between devices  19.3 us (16%)
  local copies, waits for them, and re-layouts  6.42 us (5%)
  other arithmetic  4.51 us (4%)
  between operations  1.17 us (1%)
    ppermute x28, starting transfers between devices, send(): return lax.ppermute(value, ALL, permutation(move))  33.3 us
    pallas_call x3, Pallas kernels, targets(): pl.pallas_call(functools.partial(target_kernel, stage, len(after)), out_s...  23.2 us
    ppermute x28, waiting for transfers between devices, send(): return lax.ppermute(value, ALL, permutation(move))  19.3 us
    pallas_call x2, Pallas kernels, queries(): pl.pallas_call(functools.partial(query_kernel, groups), out_shape=(jax.Sh...  10 us
    pallas_call x1, Pallas kernels, per_device(): pl.pallas_call(functools.partial(logit_kernel, idx_scale), out_shape=(par...  7.98 us
    pallas_call x1, Pallas kernels, per_device(): pl.pallas_call(key_kernel, out_shape=(shard, shard), in_specs=[smem(), sm...  6.81 us
    unnamed x15, local copies, waits for them, and re-layouts  4.37 us
    pallas_call x1, Pallas kernels, per_device(): pl.pallas_call(plan_kernel, out_shape=jax.ShapeDtypeStruct((768,), jnp.in...  2.86 us
  transfers between devices with their start and end apart: 28, of which 11 were waited for; matrix products, arithmetic and copies ran while one was open for 4% of the time, Pallas kernels for 33%

profile of v6, /device:TPU:0, one launch (start us, length us, event | category | flops | bytes accessed | tf_op | source)
XLA Modules:
  0.0 117.1 jit_solution(18202787455414301007)
XLA Ops:
  2.6 2.1 %collective-permute-start = (bf16[64,768]{1,0:T(8,128)(2,1)S(1)}, bf16[64,768]{1,0:T(8,128)(2,1)S(1)}, u32[]{:S(2)}, u32[]{:S(2)}) collective-permute-start(bf16[64,768]{1,0:T(8,128)(2,1)S(1)} %get-tuple-element.74), channel_id=1, source_target_pairs={{0,16},{1,19},{2,18},{3,17},{4,20},{5,23},{6,22},{7,21},{8,24},{9,... | collective-permute-start | bytes 294920 | tf_op jit(solution)/shard_map/ppermute | solution.py:41
  6.2 3.7 %collective-permute-start.4 = (bf16[2,17,64,128]{3,2,1,0:T(8,128)(2,1)S(1)}, bf16[2,17,64,128]{3,2,1,0:T(8,128)(2,1)S(1)}, u32[]{:S(2)}, u32[]{:S(2)}) collective-permute-start(bf16[2,17,64,128]{3,2,1,0:T(8,128)(2,1)S(1)} %get-tuple-element.82.iq_ref), channel_id=1, source_target_pairs={{0,2},{1,3},{2,0},{3,1},{4,6},{5,7},{6,4},{7,5},{8,10},{9,11},{10,... | collective-permute-start | bytes 1671176 | tf_op jit(solution)/shard_map/ppermute | solution.py:41
  13.6 2.0 %collective-permute-start.3 = (bf16[2,64,768]{2,1,0:T(8,128)(2,1)S(1)}, bf16[2,64,768]{2,1,0:T(8,128)(2,1)S(1)}, u32[]{:S(2)}, u32[]{:S(2)}) collective-permute-start(bf16[2,64,768]{2,1,0:T(8,128)(2,1)S(1)} %pad_maximum_fusion.1._after), channel_id=1, source_target_pairs={{0,8},{1,65},{2,10},{3,67},{4,12},{5,69},{6,14},{7,71},{8,0},{9,73... | collective-permute-start | bytes 589832 | tf_op jit(solution)/shard_map/ppermute | solution.py:41
  15.6 2.9 %plan.1 = s32[768]{0:T(1024)S(1)} custom-call(s32[4]{0:T(128)S(1)} %pad_add_fusion.meta, s32[64]{0:T(128)S(1)} %copy-done.2, s32[64]{0:T(128)S(1)} %get-tuple-element.90.slot, s32[64]{0:T(128)S(1)} %get-tuple-element.89.row, s32[64]{0:T(128)S(1)} %get-tuple-element.70.row_other, bf16[2,64,768]{2,1,0:T(8,128)(2,1)S(1)} %pad_maximum_fusion.1._after), custom_call_target="tpu_custom_call" | custom-call | flops 1000000 | bytes 1000000 | tf_op jit(solution)/shard_map/plan/pallas_call | solution.py:402
  18.5 2.2 %collective-permute-done.3 = bf16[2,64,768]{2,1,0:T(8,128)(2,1)S(1)} collective-permute-done((bf16[2,64,768]{2,1,0:T(8,128)(2,1)S(1)}, bf16[2,64,768]{2,1,0:T(8,128)(2,1)S(1)}, u32[]{:S(2)}, u32[]{:S(2)}) %collective-permute-start.3) | collective-permute-done | bytes 196640 | tf_op jit(solution)/shard_map/ppermute | solution.py:41
  20.8 2.0 %collective-permute-done.4 = bf16[2,17,64,128]{3,2,1,0:T(8,128)(2,1)S(1)} collective-permute-done((bf16[2,17,64,128]{3,2,1,0:T(8,128)(2,1)S(1)}, bf16[2,17,64,128]{3,2,1,0:T(8,128)(2,1)S(1)}, u32[]{:S(2)}, u32[]{:S(2)}) %collective-permute-start.4) | collective-permute-done | bytes 557088 | tf_op jit(solution)/shard_map/ppermute | solution.py:41
  25.5 1.7 %collective-permute-start.8 = (bf16[8,64,768]{2,1,0:T(8,128)(2,1)S(1)}, bf16[8,64,768]{2,1,0:T(8,128)(2,1)S(1)}, u32[]{:S(2)}, u32[]{:S(2)}) collective-permute-start(bf16[8,64,768]{2,1,0:T(8,128)(2,1)S(1)} %constant_dynamic-update-slice_fusion.refs_0_), channel_id=1, source_target_pairs={{0,96},{1,13},{2,98},{3,15},{4,100},{5,1},{6,102},{7,3},{8,104},{9... | collective-permute-start | bytes 2359304 | tf_op jit(solution)/shard_map/ppermute | solution.py:41
  28.6 2.3 %copy-done = bf16[128,32,576]{0,2,1:T(8,128)(2,1)S(1)} copy-done((bf16[128,32,576]{0,2,1:T(8,128)(2,1)S(1)}, bf16[128,32,576]{0,2,1:T(8,128)(2,1)}, u32[]{:S(2)}) %copy-start) | copy-done | bytes 4718616
  30.9 7.9 %targets_first.1 = (f32[69,64,128]{2,1,0:T(8,128)S(1)}, bf16[4096,128]{1,0:T(8,128)(2,1)S(1)}, s32[8,128]{1,0:T(8,128)S(1)}, bf16[2,640,2048]{2,1,0:T(8,128)(2,1)S(1)}) custom-call(s32[4]{0:T(128)S(1)} %pad_add_fusion.meta, s32[768]{0:T(1024)S(1)} %plan.1, bf16[32,576,128]{2,1,0:T(8,128)(2,1)S(1)} %bitcast.58, ...), custom_call_target="tpu_custom_call" | custom-call | flops 1000000 | bytes 1000000 | tf_op jit(solution)/shard_map/targets_first/pallas_call | solution.py:426
  39.9 2.3 %collective-permute-start.10 = (bf16[4,64,768]{2,1,0:T(8,128)(2,1)S(1)}, bf16[4,64,768]{2,1,0:T(8,128)(2,1)S(1)}, u32[]{:S(2)}, u32[]{:S(2)}) collective-permute-start(bf16[4,64,768]{2,1,0:T(8,128)(2,1)S(1)} %take.3), channel_id=1, source_target_pairs={{0,96},{1,13},{2,98},{3,15},{4,100},{5,1},{6,102},{7,3},{8,104},{9... | collective-permute-start | bytes 1179656 | tf_op jit(solution)/shard_map/ppermute | solution.py:41
  43.2 9.3 %targets_near.1 = (f32[69,64,128]{2,1,0:T(8,128)S(1)}, bf16[4096,128]{1,0:T(8,128)(2,1)S(1)}, s32[8,128]{1,0:T(8,128)S(1)}) custom-call(s32[4]{0:T(128)S(1)} %pad_add_fusion.meta, s32[768]{0:T(1024)S(1)} %plan.1, bf16[2,640,2048]{2,1,0:T(8,128)(2,1)S(1)} %get-tuple-element.38.q_ref, ...), custom_call_target="tpu_custom_call", output_to_operand_aliasing={{0}: (7, {}), {1}: (8, {})} | custom-call | flops 1000000 | bytes 1000000 | tf_op jit(solution)/shard_map/targets_near/pallas_call | solution.py:426
  55.0 6.0 %targets_far.1 = (f32[69,64,128]{2,1,0:T(8,128)S(1)}, bf16[4096,128]{1,0:T(8,128)(2,1)S(1)}, f32[17,32,256]{2,1,0:T(8,128)S(1)}, f32[17,32,256]{2,1,0:T(8,128)S(1)}) custom-call(s32[4]{0:T(128)S(1)} %pad_add_fusion.meta, s32[768]{0:T(1024)S(1)} %plan.1, ...), custom_call_target="tpu_custom_call", output_to_operand_aliasing={{0}: (7, {}), {1}: (8, {})} | custom-call | flops 1000000 | bytes 1000000 | tf_op jit(solution)/shard_map/targets_far/pallas_call | solution.py:426
  61.2 1.8 %collective-permute-done.15.b_ref = f32[17,32,256]{2,1,0:T(8,128)S(1)} collective-permute-done((f32[17,32,256]{2,1,0:T(8,128)S(1)}, f32[17,32,256]{2,1,0:T(8,128)S(1)}, u32[]{:S(2)}, u32[]{:S(2)}) %collective-permute-start.15) | collective-permute-done | bytes 557088 | tf_op jit(solution)/shard_map/ppermute | solution.py:41
  64.3 8.0 %logits.1 = (f32[17,32,256]{2,1,0:T(8,128)S(1)}, f32[2,1024,128]{2,1,0:T(8,128)S(1)}, bf16[2,128,1024]{2,1,0:T(8,128)(2,1)S(1)}) custom-call(s32[4]{0:T(128)S(1)} %pad_add_fusion.meta, bf16[2,2,17,32,128]{4,3,2,1,0:T(8,128)(2,1)S(1)} %get-tuple-element.76.refs_3_.a_ref, bf16[2,2,17,32,128]{4,3,2,1,0:T(8,128)(2,1)S(1)} %collective-permute-done.5.refs_8_.b_ref, ...), custom_call_target="tpu_custom_call" | custom-call | flops 1000000 | bytes 1000000 | tf_op jit(solution)/shard_map/logits/pallas_call | solution.py:471
  76.2 6.8 %keys.1 = (f32[64,32,128]{2,1,0:T(8,128)S(1)}, f32[64,32,128]{2,1,0:T(8,128)S(1)}) custom-call(s32[4]{0:T(128)S(1)} %pad_add_fusion.meta, s32[768]{0:T(1024)S(1)} %plan.1, bf16[17,32,256]{2,1,0:T(8,128)(2,1)S(1)} %gradient.1.g_ref, bf16[17,32,256]{2,1,0:T(8,128)(2,1)S(1)} %collective-permute-done.17.h_ref, ...), custom_call_target="tpu_custom_call" | custom-call | flops 1000000 | bytes 1000000 | tf_op jit(solution)/shard_map/keys/pallas_call | solution.py:499
  83.2 2.6 %collective-permute-done.18 = f32[64,32,128]{2,1,0:T(8,128)S(1)} collective-permute-done((f32[64,32,128]{2,1,0:T(8,128)S(1)}, f32[64,32,128]{2,1,0:T(8,128)S(1)}, u32[]{:S(2)}, u32[]{:S(2)}) %collective-permute-start.18) | collective-permute-done | bytes 1048608 | tf_op jit(solution)/shard_map/ppermute | solution.py:41
  87.6 1.7 %collective-permute-start.20 = (f32[4,4,32,128]{3,2,1,0:T(8,128)S(1)}, f32[4,4,32,128]{3,2,1,0:T(8,128)S(1)}, u32[]{:S(2)}, u32[]{:S(2)}) collective-permute-start(f32[4,4,32,128]{3,2,1,0:T(8,128)S(1)} %bitcast.71), channel_id=1, source_target_pairs={{0,12},{1,97},{2,14},{3,99},{4,0},{5,101},{6,2},{7,103},{8,4},{9,1... | collective-permute-start | bytes 786440 | tf_op jit(solution)/shard_map/ppermute | solution.py:41
  90.5 5.0 %queries.2 = (f32[2,512,128]{2,1,0:T(8,128)S(1)}, s32[8,128]{1,0:T(8,128)S(1)}) custom-call(s32[4]{0:T(128)S(1)} %pad_add_fusion.meta, bf16[17,32,256]{2,1,0:T(8,128)(2,1)S(1)} %gradient.1.g_ref, bf16[17,32,256]{2,1,0:T(8,128)(2,1)S(1)} %collective-permute-done.17.h_ref, bf16[2,17,64,128]{3,2,1,0:T(8,128)(2,1)S(1)} %get-tuple-element.82.iq_ref, ...), custom_call_target="tpu_custom_call" | custom-call | flops 1000000 | bytes 1000000 | tf_op jit(solution)/shard_map/queries/pallas_call | solution.py:509
  95.6 2.1 %collective-permute-done.21 = f32[4,4,32,128]{3,2,1,0:T(8,128)S(1)} collective-permute-done((f32[4,4,32,128]{3,2,1,0:T(8,128)S(1)}, f32[4,4,32,128]{3,2,1,0:T(8,128)S(1)}, u32[]{:S(2)}, u32[]{:S(2)}) %collective-permute-start.21) | collective-permute-done | bytes 262176 | tf_op jit(solution)/shard_map/ppermute | solution.py:41
  97.8 2.2 %collective-permute-start.22 = (f32[4,32,128]{2,1,0:T(8,128)S(1)}, f32[4,32,128]{2,1,0:T(8,128)S(1)}, u32[]{:S(2)}, u32[]{:S(2)}) collective-permute-start(f32[4,32,128]{2,1,0:T(8,128)S(1)} %get-tuple-element.83), channel_id=1, source_target_pairs={{0,32},{1,5},{2,34},{3,7},{4,36},{5,9},{6,38},{7,11},{8,40},{9,13}... | collective-permute-start | bytes 196616 | tf_op jit(solution)/shard_map/ppermute | solution.py:41
  101.1 1.8 %collective-permute-start.24 = (f32[4,32,128]{2,1,0:T(8,128)S(1)}, f32[4,32,128]{2,1,0:T(8,128)S(1)}, u32[]{:S(2)}, u32[]{:S(2)}) collective-permute-start(f32[4,32,128]{2,1,0:T(8,128)S(1)} %get-tuple-element.84), channel_id=1, source_target_pairs={{0,64},{1,9},{2,66},{3,11},{4,68},{5,13},{6,70},{7,15},{8,72},{9,1... | collective-permute-start | bytes 196616 | tf_op jit(solution)/shard_map/ppermute | solution.py:41
  102.9 5.0 %queries.3 = (f32[2,512,128]{2,1,0:T(8,128)S(1)}, s32[8,128]{1,0:T(8,128)S(1)}) custom-call(s32[4]{0:T(128)S(1)} %pad_add_fusion.meta, bf16[17,32,256]{2,1,0:T(8,128)(2,1)S(1)} %gradient.1.g_ref, bf16[17,32,256]{2,1,0:T(8,128)(2,1)S(1)} %collective-permute-done.17.h_ref, bf16[2,17,64,128]{3,2,1,0:T(8,128)(2,1)S(1)} %get-tuple-element.82.iq_ref, ...), custom_call_target="tpu_custom_call" | custom-call | flops 1000000 | bytes 1000000 | tf_op jit(solution)/shard_map/queries/pallas_call | solution.py:509
  108.0 3.2 %collective-permute-start.26 = (f32[32,128]{1,0:T(8,128)S(1)}, f32[32,128]{1,0:T(8,128)S(1)}, u32[]{:S(2)}, u32[]{:S(2)}) collective-permute-start(f32[32,128]{1,0:T(8,128)S(1)} %get-tuple-element.88), channel_id=1, source_target_pairs={{0,18},{1,19},{2,16},{3,17},{4,22},{5,23},{6,20},{7,21},{8,26},{9,... | collective-permute-start | bytes 49160 | tf_op jit(solution)/shard_map/ppermute | solution.py:41
  113.3 3.2 %collective-permute-done.27 = f32[32,128]{1,0:T(8,128)S(1)} collective-permute-done((f32[32,128]{1,0:T(8,128)S(1)}, f32[32,128]{1,0:T(8,128)S(1)}, u32[]{:S(2)}, u32[]{:S(2)}) %collective-permute-start.27) | collective-permute-done | bytes 16416 | tf_op jit(solution)/shard_map/ppermute | solution.py:41
  (83 shorter events, 28.1 us)
Async XLA Ops:
  2.6 7.7 %collective-permute-start = (bf16[64,768]{1,0:T(8,128)(2,1)S(1)}, bf16[64,768]{1,0:T(8,128)(2,1)S(1)}, u32[]{:S(2)}, u32[]{:S(2)}) collective-permute-start(bf16[64,768]{1,0:T(8,128)(2,1)S(1)} %get-tuple-element.74), channel_id=1, source_target_pairs={{0,16},{1,19},{2,18},{3,17},{4,20},{5,23},{6,22},{7,21},{8,24},{9,... | collective-permute-start | bytes 294920 | tf_op jit(solution)/shard_map/ppermute | solution.py:41
  6.2 16.5 %collective-permute-start.4 = (bf16[2,17,64,128]{3,2,1,0:T(8,128)(2,1)S(1)}, bf16[2,17,64,128]{3,2,1,0:T(8,128)(2,1)S(1)}, u32[]{:S(2)}, u32[]{:S(2)}) collective-permute-start(bf16[2,17,64,128]{3,2,1,0:T(8,128)(2,1)S(1)} %get-tuple-element.82.iq_ref), channel_id=1, source_target_pairs={{0,2},{1,3},{2,0},{3,1},{4,6},{5,7},{6,4},{7,5},{8,10},{9,11},{10,... | collective-permute-start | bytes 1671176 | tf_op jit(solution)/shard_map/ppermute | solution.py:41
  10.3 8.2 %collective-permute-start.1 = (bf16[2,64,768]{2,1,0:T(8,128)(2,1)S(1)}, bf16[2,64,768]{2,1,0:T(8,128)(2,1)S(1)}, u32[]{:S(2)}, u32[]{:S(2)}) collective-permute-start(bf16[2,64,768]{2,1,0:T(8,128)(2,1)S(1)} %pad_maximum_fusion.1._after), channel_id=1, source_target_pairs={{0,4},{1,33},{2,6},{3,35},{4,8},{5,37},{6,10},{7,39},{8,12},{9,41}... | collective-permute-start | bytes 589832 | tf_op jit(solution)/shard_map/ppermute | solution.py:41
  11.9 6.6 %collective-permute-start.2 = (bf16[2,64,768]{2,1,0:T(8,128)(2,1)S(1)}, bf16[2,64,768]{2,1,0:T(8,128)(2,1)S(1)}, u32[]{:S(2)}, u32[]{:S(2)}) collective-permute-start(bf16[2,64,768]{2,1,0:T(8,128)(2,1)S(1)} %pad_maximum_fusion.1._after), channel_id=1, source_target_pairs={{0,12},{1,97},{2,14},{3,99},{4,0},{5,101},{6,2},{7,103},{8,4},{9,1... | collective-permute-start | bytes 589832 | tf_op jit(solution)/shard_map/ppermute | solution.py:41
  13.6 7.2 %collective-permute-start.3 = (bf16[2,64,768]{2,1,0:T(8,128)(2,1)S(1)}, bf16[2,64,768]{2,1,0:T(8,128)(2,1)S(1)}, u32[]{:S(2)}, u32[]{:S(2)}) collective-permute-start(bf16[2,64,768]{2,1,0:T(8,128)(2,1)S(1)} %pad_maximum_fusion.1._after), channel_id=1, source_target_pairs={{0,8},{1,65},{2,10},{3,67},{4,12},{5,69},{6,14},{7,71},{8,0},{9,73... | collective-permute-start | bytes 589832 | tf_op jit(solution)/shard_map/ppermute | solution.py:41
  23.6 5.0 %collective-permute-start.6 = (bf16[8,64,768]{2,1,0:T(8,128)(2,1)S(1)}, bf16[8,64,768]{2,1,0:T(8,128)(2,1)}, u32[]{:S(2)}, u32[]{:S(2)}) collective-permute-start(bf16[8,64,768]{2,1,0:T(8,128)(2,1)S(1)} %constant_dynamic-update-slice_fusion.refs_0_), channel_id=1, source_target_pairs={{0,1},{1,0},{2,3},{3,2},{4,5},{5,4},{6,7},{7,6},{8,9},{9,8},{10,11... | collective-permute-start | bytes 2359304 | tf_op jit(solution)/shard_map/ppermute | solution.py:41
  24.0 14.8 %collective-permute-start.7 = (bf16[8,64,768]{2,1,0:T(8,128)(2,1)S(1)}, bf16[8,64,768]{2,1,0:T(8,128)(2,1)S(1)}, u32[]{:S(2)}, u32[]{:S(2)}) collective-permute-start(bf16[8,64,768]{2,1,0:T(8,128)(2,1)S(1)} %constant_dynamic-update-slice_fusion.refs_0_), channel_id=1, source_target_pairs={{0,32},{1,5},{2,34},{3,7},{4,36},{5,9},{6,38},{7,11},{8,40},{9,13}... | collective-permute-start | bytes 2359304 | tf_op jit(solution)/shard_map/ppermute | solution.py:41
  25.5 13.4 %collective-permute-start.8 = (bf16[8,64,768]{2,1,0:T(8,128)(2,1)S(1)}, bf16[8,64,768]{2,1,0:T(8,128)(2,1)S(1)}, u32[]{:S(2)}, u32[]{:S(2)}) collective-permute-start(bf16[8,64,768]{2,1,0:T(8,128)(2,1)S(1)} %constant_dynamic-update-slice_fusion.refs_0_), channel_id=1, source_target_pairs={{0,96},{1,13},{2,98},{3,15},{4,100},{5,1},{6,102},{7,3},{8,104},{9... | collective-permute-start | bytes 2359304 | tf_op jit(solution)/shard_map/ppermute | solution.py:41
  38.9 4.3 %collective-permute-start.11 = (bf16[8,64,768]{2,1,0:T(8,128)(2,1)S(1)}, bf16[8,64,768]{2,1,0:T(8,128)(2,1)S(1)}, u32[]{:S(2)}, u32[]{:S(2)}) collective-permute-start(bf16[8,64,768]{2,1,0:T(8,128)(2,1)S(1)} %collective-permute-done.7.source.refs_0_), channel_id=1, source_target_pairs={{0,1},{1,0},{2,3},{3,2},{4,5},{5,4},{6,7},{7,6},{8,9},{9,8},{10,11... | collective-permute-start | bytes 2359304 | tf_op jit(solution)/shard_map/ppermute | solution.py:41
  39.0 4.2 %collective-permute-start.12 = (bf16[8,64,768]{2,1,0:T(8,128)(2,1)S(1)}, bf16[8,64,768]{2,1,0:T(8,128)(2,1)S(1)}, u32[]{:S(2)}, u32[]{:S(2)}) collective-permute-start(bf16[8,64,768]{2,1,0:T(8,128)(2,1)S(1)} %collective-permute-done.8.source.refs_1_), channel_id=1, source_target_pairs={{0,1},{1,0},{2,3},{3,2},{4,5},{5,4},{6,7},{7,6},{8,9},{9,8},{10,11... | collective-permute-start | bytes 2359304 | tf_op jit(solution)/shard_map/ppermute | solution.py:41
  39.4 3.7 %collective-permute-start.5 = (bf16[2,2,17,32,128]{4,3,2,1,0:T(8,128)(2,1)S(1)}, bf16[2,2,17,32,128]{4,3,2,1,0:T(8,128)(2,1)S(1)}, u32[]{:S(2)}, u32[]{:S(2)}) collective-permute-start(bf16[2,2,17,32,128]{4,3,2,1,0:T(8,128)(2,1)S(1)} %get-tuple-element.75.refs_4_), channel_id=1, source_target_pairs={{0,1},{1,0},{2,3},{3,2},{4,5},{5,4},{6,7},{7,6},{8,9},{9,8},{10,11... | collective-permute-start | bytes 1671176 | tf_op jit(solution)/shard_map/ppermute | solution.py:41
  39.9 12.5 %collective-permute-start.10 = (bf16[4,64,768]{2,1,0:T(8,128)(2,1)S(1)}, bf16[4,64,768]{2,1,0:T(8,128)(2,1)S(1)}, u32[]{:S(2)}, u32[]{:S(2)}) collective-permute-start(bf16[4,64,768]{2,1,0:T(8,128)(2,1)S(1)} %take.3), channel_id=1, source_target_pairs={{0,96},{1,13},{2,98},{3,15},{4,100},{5,1},{6,102},{7,3},{8,104},{9... | collective-permute-start | bytes 1179656 | tf_op jit(solution)/shard_map/ppermute | solution.py:41
  42.3 10.2 %collective-permute-start.9 = (bf16[4,64,768]{2,1,0:T(8,128)(2,1)S(1)}, bf16[4,64,768]{2,1,0:T(8,128)(2,1)S(1)}, u32[]{:S(2)}, u32[]{:S(2)}) collective-permute-start(bf16[4,64,768]{2,1,0:T(8,128)(2,1)S(1)} %take.2), channel_id=1, source_target_pairs={{0,32},{1,5},{2,34},{3,7},{4,36},{5,9},{6,38},{7,11},{8,40},{9,13}... | collective-permute-start | bytes 1179656 | tf_op jit(solution)/shard_map/ppermute | solution.py:41
  63.1 10.3 %collective-permute-start.16 = (bf16[17,32,256]{2,1,0:T(8,128)(2,1)S(1)}, bf16[17,32,256]{2,1,0:T(8,128)(2,1)S(1)}, u32[]{:S(2)}, u32[]{:S(2)}) collective-permute-start(bf16[17,32,256]{2,1,0:T(8,128)(2,1)S(1)} %add_convert_fusion), channel_id=1, source_target_pairs={{0,2},{1,3},{2,0},{3,1},{4,6},{5,7},{6,4},{7,5},{8,10},{9,11},{10,... | collective-permute-start | bytes 835592 | tf_op jit(solution)/shard_map/ppermute | solution.py:41
  83.0 2.7 %collective-permute-start.18 = (f32[64,32,128]{2,1,0:T(8,128)S(1)}, f32[64,32,128]{2,1,0:T(8,128)S(1)}, u32[]{:S(2)}, u32[]{:S(2)}) collective-permute-start(f32[64,32,128]{2,1,0:T(8,128)S(1)} %get-tuple-element.59), channel_id=1, source_target_pairs={{0,1},{1,0},{2,3},{3,2},{4,5},{5,4},{6,7},{7,6},{8,9},{9,8},{10,11... | collective-permute-start | bytes 3145736 | tf_op jit(solution)/shard_map/ppermute | solution.py:41
  86.0 9.5 %collective-permute-start.19 = (f32[4,4,32,128]{3,2,1,0:T(8,128)S(1)}, f32[4,4,32,128]{3,2,1,0:T(8,128)S(1)}, u32[]{:S(2)}, u32[]{:S(2)}) collective-permute-start(f32[4,4,32,128]{3,2,1,0:T(8,128)S(1)} %bitcast.72), channel_id=1, source_target_pairs={{0,4},{1,33},{2,6},{3,35},{4,8},{5,37},{6,10},{7,39},{8,12},{9,41}... | collective-permute-start | bytes 786440 | tf_op jit(solution)/shard_map/ppermute | solution.py:41
  87.6 7.9 %collective-permute-start.20 = (f32[4,4,32,128]{3,2,1,0:T(8,128)S(1)}, f32[4,4,32,128]{3,2,1,0:T(8,128)S(1)}, u32[]{:S(2)}, u32[]{:S(2)}) collective-permute-start(f32[4,4,32,128]{3,2,1,0:T(8,128)S(1)} %bitcast.71), channel_id=1, source_target_pairs={{0,12},{1,97},{2,14},{3,99},{4,0},{5,101},{6,2},{7,103},{8,4},{9,1... | collective-permute-start | bytes 786440 | tf_op jit(solution)/shard_map/ppermute | solution.py:41
  89.3 8.4 %collective-permute-start.21 = (f32[4,4,32,128]{3,2,1,0:T(8,128)S(1)}, f32[4,4,32,128]{3,2,1,0:T(8,128)S(1)}, u32[]{:S(2)}, u32[]{:S(2)}) collective-permute-start(f32[4,4,32,128]{3,2,1,0:T(8,128)S(1)} %bitcast.70), channel_id=1, source_target_pairs={{0,8},{1,65},{2,10},{3,67},{4,12},{5,69},{6,14},{7,71},{8,0},{9,73... | collective-permute-start | bytes 786440 | tf_op jit(solution)/shard_map/ppermute | solution.py:41
  97.8 10.1 %collective-permute-start.22 = (f32[4,32,128]{2,1,0:T(8,128)S(1)}, f32[4,32,128]{2,1,0:T(8,128)S(1)}, u32[]{:S(2)}, u32[]{:S(2)}) collective-permute-start(f32[4,32,128]{2,1,0:T(8,128)S(1)} %get-tuple-element.83), channel_id=1, source_target_pairs={{0,32},{1,5},{2,34},{3,7},{4,36},{5,9},{6,38},{7,11},{8,40},{9,13}... | collective-permute-start | bytes 196616 | tf_op jit(solution)/shard_map/ppermute | solution.py:41
  100.0 7.9 %collective-permute-start.23 = (f32[4,32,128]{2,1,0:T(8,128)S(1)}, f32[4,32,128]{2,1,0:T(8,128)S(1)}, u32[]{:S(2)}, u32[]{:S(2)}) collective-permute-start(f32[4,32,128]{2,1,0:T(8,128)S(1)} %get-tuple-element.85), channel_id=1, source_target_pairs={{0,96},{1,13},{2,98},{3,15},{4,100},{5,1},{6,102},{7,3},{8,104},{9... | collective-permute-start | bytes 196616 | tf_op jit(solution)/shard_map/ppermute | solution.py:41
  101.1 6.8 %collective-permute-start.24 = (f32[4,32,128]{2,1,0:T(8,128)S(1)}, f32[4,32,128]{2,1,0:T(8,128)S(1)}, u32[]{:S(2)}, u32[]{:S(2)}) collective-permute-start(f32[4,32,128]{2,1,0:T(8,128)S(1)} %get-tuple-element.84), channel_id=1, source_target_pairs={{0,64},{1,9},{2,66},{3,11},{4,68},{5,13},{6,70},{7,15},{8,72},{9,1... | collective-permute-start | bytes 196616 | tf_op jit(solution)/shard_map/ppermute | solution.py:41
  108.0 5.3 %collective-permute-start.25 = (f32[32,128]{1,0:T(8,128)S(1)}, f32[32,128]{1,0:T(8,128)S(1)}, u32[]{:S(2)}, u32[]{:S(2)}) collective-permute-start(f32[32,128]{1,0:T(8,128)S(1)} %get-tuple-element.86), channel_id=1, source_target_pairs={{0,16},{1,17},{2,18},{3,19},{4,20},{5,21},{6,22},{7,23},{8,24},{9,... | collective-permute-start | bytes 49160 | tf_op jit(solution)/shard_map/ppermute | solution.py:41
  108.0 5.2 %collective-permute-start.26 = (f32[32,128]{1,0:T(8,128)S(1)}, f32[32,128]{1,0:T(8,128)S(1)}, u32[]{:S(2)}, u32[]{:S(2)}) collective-permute-start(f32[32,128]{1,0:T(8,128)S(1)} %get-tuple-element.88), channel_id=1, source_target_pairs={{0,18},{1,19},{2,16},{3,17},{4,22},{5,23},{6,20},{7,21},{8,26},{9,... | collective-permute-start | bytes 49160 | tf_op jit(solution)/shard_map/ppermute | solution.py:41
  111.3 5.2 %collective-permute-start.27 = (f32[32,128]{1,0:T(8,128)S(1)}, f32[32,128]{1,0:T(8,128)S(1)}, u32[]{:S(2)}, u32[]{:S(2)}) collective-permute-start(f32[32,128]{1,0:T(8,128)S(1)} %get-tuple-element.87), channel_id=1, source_target_pairs={{0,2},{1,3},{2,0},{3,1},{4,6},{5,7},{6,4},{7,5},{8,10},{9,11},{10,... | collective-permute-start | bytes 49160 | tf_op jit(solution)/shard_map/ppermute | solution.py:41
  (9 other events, 21.5 us)

commit v7 on v6

--- a/solution.py
+++ b/solution.py
@@ -351,7 +351,7 @@
 
     def body(step, _):
         half, _ktile, tile, found = coefficients(meta, step, g_ref, h_ref, iq_ref, key_ref, wide, groups)
-        for q in range(2):
+        for q in range(4):
             dq[half, pl.ds(q * 256, 256)] = dq[half, pl.ds(q * 256, 256)] + lax.dot_general(
                 found[q], tile, NN, preferred_element_type=jnp.float32
             )
@@ -508,7 +508,7 @@
     def queries(groups, *after):
         return pl.pallas_call(
             functools.partial(query_kernel, groups),
-            out_shape=(jax.ShapeDtypeStruct((2, 512, 128), f32), flag),
+            out_shape=(jax.ShapeDtypeStruct((2, 1024, 128), f32), flag),
             in_specs=[smem()] + [vmem()] * 5 + [anywhere()] * len(after),
             out_specs=(vmem(), vmem()),
             compiler_params=params(12),
@@ -517,15 +517,13 @@
         )(meta, grad, grad_other, iqw, sorted_keys, scaled, *after)
 
     dk = dk_keep + swap_core(dk_other)
-    low, token = queries((0, 1))
+    dq, token = queries((0, 1, 2, 3))
     dk = ring_sum(dk.reshape(4, 4, 4, 32, 128), functools.partial(along, True))
     dk, token = lax.optimization_barrier((dk, token))
-    high, token = queries((2, 3), token)
     dk = ring_sum(dk, functools.partial(along, False))
-    dk, token, low, high = lax.optimization_barrier((dk, token, low, high))
+    dk, dq = lax.optimization_barrier((dk, dq))
     dk = ring_sum(dk, lambda shift: lambda x, z, y, k: (x, z + shift, y, k))
-    low, high = [v.reshape(2, 8, HALF, 128).transpose(0, 2, 1, 3).reshape(128, 8, 128) for v in (low, high)]
-    query_grad = jnp.concatenate((low, high), axis=1)
+    query_grad = dq.reshape(2, 16, HALF, 128).transpose(0, 2, 1, 3).reshape(128, 16, 128)
     return query_grad, dk + token[0:1].astype(f32)
 
 

time: 117 us -> 117 us (level)
  waiting for transfers between devices: 19.3 us -> 23.7 us
  Pallas kernels: 52.4 us -> 48.4 us
    ppermute x28, waiting for transfers between devices: 19.3 us -> 23.7 us  [send(): return lax.ppermute(value, ALL, permutation(move))]
    pallas_call x2 -> x1, Pallas kernels: 10 us -> 6.1 us  [queries(): pl.pallas_call(functools.partial(query_kernel, groups), out_shape=(jax.Sh...]
  transfers between devices with their start and end apart: 28 -> 28, of which waited for: 11 -> 14; matrix products, arithmetic and copies ran while one was open for 4% -> 4% of each run, Pallas kernels for 33% -> 29%
where the time goes in v7:
time: 117 us
  Pallas kernels  48.4 us (41%)
  starting transfers between devices  33 us (28%)
  waiting for transfers between devices  23.7 us (20%)
  local copies, waits for them, and re-layouts  7.39 us (6%)
  other arithmetic  3.47 us (3%)
    ppermute x28, starting transfers between devices, send(): return lax.ppermute(value, ALL, permutation(move))  33 us
    ppermute x28, waiting for transfers between devices, send(): return lax.ppermute(value, ALL, permutation(move))  23.7 us
    pallas_call x3, Pallas kernels, targets(): pl.pallas_call(functools.partial(target_kernel, stage, len(after)), out_s...  23.2 us
    pallas_call x1, Pallas kernels, per_device(): pl.pallas_call(functools.partial(logit_kernel, idx_scale), out_shape=(par...  7.98 us
    pallas_call x1, Pallas kernels, per_device(): pl.pallas_call(key_kernel, out_shape=(shard, shard), in_specs=[smem(), sm...  6.77 us
    pallas_call x1, Pallas kernels, queries(): pl.pallas_call(functools.partial(query_kernel, groups), out_shape=(jax.Sh...  6.1 us
    unnamed x15, local copies, waits for them, and re-layouts  4.37 us
    pallas_call x1, Pallas kernels, per_device(): pl.pallas_call(plan_kernel, out_shape=jax.ShapeDtypeStruct((768,), jnp.in...  2.86 us
  transfers between devices with their start and end apart: 28, of which 14 were waited for; matrix products, arithmetic and copies ran while one was open for 4% of the time, Pallas kernels for 29%

profile of v7, /device:TPU:0, one launch (start us, length us, event | category | flops | bytes accessed | tf_op | source)
XLA Modules:
  0.0 117.1 jit_solution(15894539669901809107)
XLA Ops:
  2.6 2.1 %collective-permute-start = (bf16[64,768]{1,0:T(8,128)(2,1)S(1)}, bf16[64,768]{1,0:T(8,128)(2,1)S(1)}, u32[]{:S(2)}, u32[]{:S(2)}) collective-permute-start(bf16[64,768]{1,0:T(8,128)(2,1)S(1)} %get-tuple-element.66), channel_id=1, source_target_pairs={{0,16},{1,19},{2,18},{3,17},{4,20},{5,23},{6,22},{7,21},{8,24},{9,... | collective-permute-start | bytes 294920 | tf_op jit(solution)/shard_map/ppermute | solution.py:41
  6.2 3.7 %collective-permute-start.4 = (bf16[2,17,64,128]{3,2,1,0:T(8,128)(2,1)S(1)}, bf16[2,17,64,128]{3,2,1,0:T(8,128)(2,1)S(1)}, u32[]{:S(2)}, u32[]{:S(2)}) collective-permute-start(bf16[2,17,64,128]{3,2,1,0:T(8,128)(2,1)S(1)} %get-tuple-element.74.iq_ref), channel_id=1, source_target_pairs={{0,2},{1,3},{2,0},{3,1},{4,6},{5,7},{6,4},{7,5},{8,10},{9,11},{10,... | collective-permute-start | bytes 1671176 | tf_op jit(solution)/shard_map/ppermute | solution.py:41
  11.9 1.7 %collective-permute-start.2 = (bf16[2,64,768]{2,1,0:T(8,128)(2,1)S(1)}, bf16[2,64,768]{2,1,0:T(8,128)(2,1)S(1)}, u32[]{:S(2)}, u32[]{:S(2)}) collective-permute-start(bf16[2,64,768]{2,1,0:T(8,128)(2,1)S(1)} %pad_maximum_fusion._after), channel_id=1, source_target_pairs={{0,12},{1,97},{2,14},{3,99},{4,0},{5,101},{6,2},{7,103},{8,4},{9,1... | collective-permute-start | bytes 589832 | tf_op jit(solution)/shard_map/ppermute | solution.py:41
  13.6 2.0 %collective-permute-start.3 = (bf16[2,64,768]{2,1,0:T(8,128)(2,1)S(1)}, bf16[2,64,768]{2,1,0:T(8,128)(2,1)S(1)}, u32[]{:S(2)}, u32[]{:S(2)}) collective-permute-start(bf16[2,64,768]{2,1,0:T(8,128)(2,1)S(1)} %pad_maximum_fusion._after), channel_id=1, source_target_pairs={{0,8},{1,65},{2,10},{3,67},{4,12},{5,69},{6,14},{7,71},{8,0},{9,73... | collective-permute-start | bytes 589832 | tf_op jit(solution)/shard_map/ppermute | solution.py:41
  15.6 2.9 %plan.1 = s32[768]{0:T(1024)S(1)} custom-call(s32[4]{0:T(128)S(1)} %pad_add_fusion.meta, s32[64]{0:T(128)S(1)} %copy-done.2, s32[64]{0:T(128)S(1)} %get-tuple-element.82.slot, s32[64]{0:T(128)S(1)} %get-tuple-element.81.row, s32[64]{0:T(128)S(1)} %get-tuple-element.62.row_other, bf16[2,64,768]{2,1,0:T(8,128)(2,1)S(1)} %pad_maximum_fusion._after), custom_call_target="tpu_custom_call" | custom-call | flops 1000000 | bytes 1000000 | tf_op jit(solution)/shard_map/plan/pallas_call | solution.py:402
  18.5 2.2 %collective-permute-done.3 = bf16[2,64,768]{2,1,0:T(8,128)(2,1)S(1)} collective-permute-done((bf16[2,64,768]{2,1,0:T(8,128)(2,1)S(1)}, bf16[2,64,768]{2,1,0:T(8,128)(2,1)S(1)}, u32[]{:S(2)}, u32[]{:S(2)}) %collective-permute-start.3) | collective-permute-done | bytes 196640 | tf_op jit(solution)/shard_map/ppermute | solution.py:41
  20.8 2.0 %collective-permute-done.4 = bf16[2,17,64,128]{3,2,1,0:T(8,128)(2,1)S(1)} collective-permute-done((bf16[2,17,64,128]{3,2,1,0:T(8,128)(2,1)S(1)}, bf16[2,17,64,128]{3,2,1,0:T(8,128)(2,1)S(1)}, u32[]{:S(2)}, u32[]{:S(2)}) %collective-permute-start.4) | collective-permute-done | bytes 557088 | tf_op jit(solution)/shard_map/ppermute | solution.py:41
  25.5 1.7 %collective-permute-start.8 = (bf16[8,64,768]{2,1,0:T(8,128)(2,1)S(1)}, bf16[8,64,768]{2,1,0:T(8,128)(2,1)S(1)}, u32[]{:S(2)}, u32[]{:S(2)}) collective-permute-start(bf16[8,64,768]{2,1,0:T(8,128)(2,1)S(1)} %constant_dynamic-update-slice_fusion.refs_0_), channel_id=1, source_target_pairs={{0,96},{1,13},{2,98},{3,15},{4,100},{5,1},{6,102},{7,3},{8,104},{9... | collective-permute-start | bytes 2359304 | tf_op jit(solution)/shard_map/ppermute | solution.py:41
  28.6 2.3 %copy-done = bf16[128,32,576]{0,2,1:T(8,128)(2,1)S(1)} copy-done((bf16[128,32,576]{0,2,1:T(8,128)(2,1)S(1)}, bf16[128,32,576]{0,2,1:T(8,128)(2,1)}, u32[]{:S(2)}) %copy-start) | copy-done | bytes 4718616
  30.9 7.9 %targets_first.1 = (f32[69,64,128]{2,1,0:T(8,128)S(1)}, bf16[4096,128]{1,0:T(8,128)(2,1)S(1)}, s32[8,128]{1,0:T(8,128)S(1)}, bf16[2,640,2048]{2,1,0:T(8,128)(2,1)S(1)}) custom-call(s32[4]{0:T(128)S(1)} %pad_add_fusion.meta, s32[768]{0:T(1024)S(1)} %plan.1, bf16[32,576,128]{2,1,0:T(8,128)(2,1)S(1)} %bitcast.54, ...), custom_call_target="tpu_custom_call" | custom-call | flops 1000000 | bytes 1000000 | tf_op jit(solution)/shard_map/targets_first/pallas_call | solution.py:426
  39.9 2.3 %collective-permute-start.10 = (bf16[4,64,768]{2,1,0:T(8,128)(2,1)S(1)}, bf16[4,64,768]{2,1,0:T(8,128)(2,1)S(1)}, u32[]{:S(2)}, u32[]{:S(2)}) collective-permute-start(bf16[4,64,768]{2,1,0:T(8,128)(2,1)S(1)} %take.3), channel_id=1, source_target_pairs={{0,96},{1,13},{2,98},{3,15},{4,100},{5,1},{6,102},{7,3},{8,104},{9... | collective-permute-start | bytes 1179656 | tf_op jit(solution)/shard_map/ppermute | solution.py:41
  43.2 8.3 %targets_near.1 = (f32[69,64,128]{2,1,0:T(8,128)S(1)}, bf16[4096,128]{1,0:T(8,128)(2,1)S(1)}, s32[8,128]{1,0:T(8,128)S(1)}) custom-call(s32[4]{0:T(128)S(1)} %pad_add_fusion.meta, s32[768]{0:T(1024)S(1)} %plan.1, bf16[2,640,2048]{2,1,0:T(8,128)(2,1)S(1)} %get-tuple-element.34.q_ref, ...), custom_call_target="tpu_custom_call", output_to_operand_aliasing={{0}: (7, {}), {1}: (8, {})} | custom-call | flops 1000000 | bytes 1000000 | tf_op jit(solution)/shard_map/targets_near/pallas_call | solution.py:426
  54.0 7.0 %targets_far.1 = (f32[69,64,128]{2,1,0:T(8,128)S(1)}, bf16[4096,128]{1,0:T(8,128)(2,1)S(1)}, f32[17,32,256]{2,1,0:T(8,128)S(1)}, f32[17,32,256]{2,1,0:T(8,128)S(1)}) custom-call(s32[4]{0:T(128)S(1)} %pad_add_fusion.meta, s32[768]{0:T(1024)S(1)} %plan.1, ...), custom_call_target="tpu_custom_call", output_to_operand_aliasing={{0}: (7, {}), {1}: (8, {})} | custom-call | flops 1000000 | bytes 1000000 | tf_op jit(solution)/shard_map/targets_far/pallas_call | solution.py:426
  61.2 1.8 %collective-permute-done.15.b_ref = f32[17,32,256]{2,1,0:T(8,128)S(1)} collective-permute-done((f32[17,32,256]{2,1,0:T(8,128)S(1)}, f32[17,32,256]{2,1,0:T(8,128)S(1)}, u32[]{:S(2)}, u32[]{:S(2)}) %collective-permute-start.15) | collective-permute-done | bytes 557088 | tf_op jit(solution)/shard_map/ppermute | solution.py:41
  64.3 8.0 %logits.1 = (f32[17,32,256]{2,1,0:T(8,128)S(1)}, f32[2,1024,128]{2,1,0:T(8,128)S(1)}, bf16[2,128,1024]{2,1,0:T(8,128)(2,1)S(1)}) custom-call(s32[4]{0:T(128)S(1)} %pad_add_fusion.meta, bf16[2,2,17,32,128]{4,3,2,1,0:T(8,128)(2,1)S(1)} %get-tuple-element.68.refs_3_.a_ref, bf16[2,2,17,32,128]{4,3,2,1,0:T(8,128)(2,1)S(1)} %collective-permute-done.5.refs_8_.b_ref, ...), custom_call_target="tpu_custom_call" | custom-call | flops 1000000 | bytes 1000000 | tf_op jit(solution)/shard_map/logits/pallas_call | solution.py:471
  76.2 6.8 %keys.1 = (f32[64,32,128]{2,1,0:T(8,128)S(1)}, f32[64,32,128]{2,1,0:T(8,128)S(1)}) custom-call(s32[4]{0:T(128)S(1)} %pad_add_fusion.meta, s32[768]{0:T(1024)S(1)} %plan.1, bf16[17,32,256]{2,1,0:T(8,128)(2,1)S(1)} %gradient.1.g_ref, bf16[17,32,256]{2,1,0:T(8,128)(2,1)S(1)} %collective-permute-done.17.h_ref, ...), custom_call_target="tpu_custom_call" | custom-call | flops 1000000 | bytes 1000000 | tf_op jit(solution)/shard_map/keys/pallas_call | solution.py:499
  83.2 2.5 %collective-permute-done.18 = f32[64,32,128]{2,1,0:T(8,128)S(1)} collective-permute-done((f32[64,32,128]{2,1,0:T(8,128)S(1)}, f32[64,32,128]{2,1,0:T(8,128)S(1)}, u32[]{:S(2)}, u32[]{:S(2)}) %collective-permute-start.18) | collective-permute-done | bytes 1048608 | tf_op jit(solution)/shard_map/ppermute | solution.py:41
  86.0 1.6 %collective-permute-start.19 = (f32[4,4,32,128]{3,2,1,0:T(8,128)S(1)}, f32[4,4,32,128]{3,2,1,0:T(8,128)S(1)}, u32[]{:S(2)}, u32[]{:S(2)}) collective-permute-start(f32[4,4,32,128]{3,2,1,0:T(8,128)S(1)} %bitcast.66), channel_id=1, source_target_pairs={{0,4},{1,33},{2,6},{3,35},{4,8},{5,37},{6,10},{7,39},{8,12},{9,41}... | collective-permute-start | bytes 786440 | tf_op jit(solution)/shard_map/ppermute | solution.py:41
  87.6 2.5 %collective-permute-start.20 = (f32[4,4,32,128]{3,2,1,0:T(8,128)S(1)}, f32[4,4,32,128]{3,2,1,0:T(8,128)S(1)}, u32[]{:S(2)}, u32[]{:S(2)}) collective-permute-start(f32[4,4,32,128]{3,2,1,0:T(8,128)S(1)} %bitcast.65), channel_id=1, source_target_pairs={{0,12},{1,97},{2,14},{3,99},{4,0},{5,101},{6,2},{7,103},{8,4},{9,1... | collective-permute-start | bytes 786440 | tf_op jit(solution)/shard_map/ppermute | solution.py:41
  91.6 6.1 %queries.1 = (f32[2,1024,128]{2,1,0:T(8,128)S(1)}, s32[8,128]{1,0:T(8,128)S(1)}) custom-call(s32[4]{0:T(128)S(1)} %pad_add_fusion.meta, bf16[17,32,256]{2,1,0:T(8,128)(2,1)S(1)} %gradient.1.g_ref, bf16[17,32,256]{2,1,0:T(8,128)(2,1)S(1)} %collective-permute-done.17.h_ref, bf16[2,17,64,128]{3,2,1,0:T(8,128)(2,1)S(1)} %get-tuple-element.74.iq_ref, ...), custom_call_target="tpu_custom_call" | custom-call | flops 1000000 | bytes 1000000 | tf_op jit(solution)/shard_map/queries/pallas_call | solution.py:509
  99.7 2.4 %collective-permute-start.23 = (f32[4,32,128]{2,1,0:T(8,128)S(1)}, f32[4,32,128]{2,1,0:T(8,128)S(1)}, u32[]{:S(2)}, u32[]{:S(2)}) collective-permute-start(f32[4,32,128]{2,1,0:T(8,128)S(1)} %get-tuple-element.77), channel_id=1, source_target_pairs={{0,96},{1,13},{2,98},{3,15},{4,100},{5,1},{6,102},{7,3},{8,104},{9... | collective-permute-start | bytes 196616 | tf_op jit(solution)/shard_map/ppermute | solution.py:41
  104.4 3.5 %collective-permute-done.24 = f32[4,32,128]{2,1,0:T(8,128)S(1)} collective-permute-done((f32[4,32,128]{2,1,0:T(8,128)S(1)}, f32[4,32,128]{2,1,0:T(8,128)S(1)}, u32[]{:S(2)}, u32[]{:S(2)}) %collective-permute-start.24) | collective-permute-done | bytes 65568 | tf_op jit(solution)/shard_map/ppermute | solution.py:41
  108.1 3.1 %collective-permute-start.26 = (f32[32,128]{1,0:T(8,128)S(1)}, f32[32,128]{1,0:T(8,128)S(1)}, u32[]{:S(2)}, u32[]{:S(2)}) collective-permute-start(f32[32,128]{1,0:T(8,128)S(1)} %get-tuple-element.80), channel_id=1, source_target_pairs={{0,18},{1,19},{2,16},{3,17},{4,22},{5,23},{6,20},{7,21},{8,26},{9,... | collective-permute-start | bytes 49160 | tf_op jit(solution)/shard_map/ppermute | solution.py:41
  113.0 3.5 %collective-permute-done.27 = f32[32,128]{1,0:T(8,128)S(1)} collective-permute-done((f32[32,128]{1,0:T(8,128)S(1)}, f32[32,128]{1,0:T(8,128)S(1)}, u32[]{:S(2)}, u32[]{:S(2)}) %collective-permute-start.27) | collective-permute-done | bytes 16416 | tf_op jit(solution)/shard_map/ppermute | solution.py:41
  (80 shorter events, 27.9 us)
Async XLA Ops:
  2.6 7.7 %collective-permute-start = (bf16[64,768]{1,0:T(8,128)(2,1)S(1)}, bf16[64,768]{1,0:T(8,128)(2,1)S(1)}, u32[]{:S(2)}, u32[]{:S(2)}) collective-permute-start(bf16[64,768]{1,0:T(8,128)(2,1)S(1)} %get-tuple-element.66), channel_id=1, source_target_pairs={{0,16},{1,19},{2,18},{3,17},{4,20},{5,23},{6,22},{7,21},{8,24},{9,... | collective-permute-start | bytes 294920 | tf_op jit(solution)/shard_map/ppermute | solution.py:41
  6.2 16.5 %collective-permute-start.4 = (bf16[2,17,64,128]{3,2,1,0:T(8,128)(2,1)S(1)}, bf16[2,17,64,128]{3,2,1,0:T(8,128)(2,1)S(1)}, u32[]{:S(2)}, u32[]{:S(2)}) collective-permute-start(bf16[2,17,64,128]{3,2,1,0:T(8,128)(2,1)S(1)} %get-tuple-element.74.iq_ref), channel_id=1, source_target_pairs={{0,2},{1,3},{2,0},{3,1},{4,6},{5,7},{6,4},{7,5},{8,10},{9,11},{10,... | collective-permute-start | bytes 1671176 | tf_op jit(solution)/shard_map/ppermute | solution.py:41
  10.3 8.2 %collective-permute-start.1 = (bf16[2,64,768]{2,1,0:T(8,128)(2,1)S(1)}, bf16[2,64,768]{2,1,0:T(8,128)(2,1)S(1)}, u32[]{:S(2)}, u32[]{:S(2)}) collective-permute-start(bf16[2,64,768]{2,1,0:T(8,128)(2,1)S(1)} %pad_maximum_fusion._after), channel_id=1, source_target_pairs={{0,4},{1,33},{2,6},{3,35},{4,8},{5,37},{6,10},{7,39},{8,12},{9,41}... | collective-permute-start | bytes 589832 | tf_op jit(solution)/shard_map/ppermute | solution.py:41
  11.9 6.6 %collective-permute-start.2 = (bf16[2,64,768]{2,1,0:T(8,128)(2,1)S(1)}, bf16[2,64,768]{2,1,0:T(8,128)(2,1)S(1)}, u32[]{:S(2)}, u32[]{:S(2)}) collective-permute-start(bf16[2,64,768]{2,1,0:T(8,128)(2,1)S(1)} %pad_maximum_fusion._after), channel_id=1, source_target_pairs={{0,12},{1,97},{2,14},{3,99},{4,0},{5,101},{6,2},{7,103},{8,4},{9,1... | collective-permute-start | bytes 589832 | tf_op jit(solution)/shard_map/ppermute | solution.py:41
  13.6 7.2 %collective-permute-start.3 = (bf16[2,64,768]{2,1,0:T(8,128)(2,1)S(1)}, bf16[2,64,768]{2,1,0:T(8,128)(2,1)S(1)}, u32[]{:S(2)}, u32[]{:S(2)}) collective-permute-start(bf16[2,64,768]{2,1,0:T(8,128)(2,1)S(1)} %pad_maximum_fusion._after), channel_id=1, source_target_pairs={{0,8},{1,65},{2,10},{3,67},{4,12},{5,69},{6,14},{7,71},{8,0},{9,73... | collective-permute-start | bytes 589832 | tf_op jit(solution)/shard_map/ppermute | solution.py:41
  23.6 5.0 %collective-permute-start.6 = (bf16[8,64,768]{2,1,0:T(8,128)(2,1)S(1)}, bf16[8,64,768]{2,1,0:T(8,128)(2,1)}, u32[]{:S(2)}, u32[]{:S(2)}) collective-permute-start(bf16[8,64,768]{2,1,0:T(8,128)(2,1)S(1)} %constant_dynamic-update-slice_fusion.refs_0_), channel_id=1, source_target_pairs={{0,1},{1,0},{2,3},{3,2},{4,5},{5,4},{6,7},{7,6},{8,9},{9,8},{10,11... | collective-permute-start | bytes 2359304 | tf_op jit(solution)/shard_map/ppermute | solution.py:41
  24.0 14.8 %collective-permute-start.7 = (bf16[8,64,768]{2,1,0:T(8,128)(2,1)S(1)}, bf16[8,64,768]{2,1,0:T(8,128)(2,1)S(1)}, u32[]{:S(2)}, u32[]{:S(2)}) collective-permute-start(bf16[8,64,768]{2,1,0:T(8,128)(2,1)S(1)} %constant_dynamic-update-slice_fusion.refs_0_), channel_id=1, source_target_pairs={{0,32},{1,5},{2,34},{3,7},{4,36},{5,9},{6,38},{7,11},{8,40},{9,13}... | collective-permute-start | bytes 2359304 | tf_op jit(solution)/shard_map/ppermute | solution.py:41
  25.5 13.4 %collective-permute-start.8 = (bf16[8,64,768]{2,1,0:T(8,128)(2,1)S(1)}, bf16[8,64,768]{2,1,0:T(8,128)(2,1)S(1)}, u32[]{:S(2)}, u32[]{:S(2)}) collective-permute-start(bf16[8,64,768]{2,1,0:T(8,128)(2,1)S(1)} %constant_dynamic-update-slice_fusion.refs_0_), channel_id=1, source_target_pairs={{0,96},{1,13},{2,98},{3,15},{4,100},{5,1},{6,102},{7,3},{8,104},{9... | collective-permute-start | bytes 2359304 | tf_op jit(solution)/shard_map/ppermute | solution.py:41
  38.9 4.3 %collective-permute-start.11 = (bf16[8,64,768]{2,1,0:T(8,128)(2,1)S(1)}, bf16[8,64,768]{2,1,0:T(8,128)(2,1)S(1)}, u32[]{:S(2)}, u32[]{:S(2)}) collective-permute-start(bf16[8,64,768]{2,1,0:T(8,128)(2,1)S(1)} %collective-permute-done.7.source.refs_0_), channel_id=1, source_target_pairs={{0,1},{1,0},{2,3},{3,2},{4,5},{5,4},{6,7},{7,6},{8,9},{9,8},{10,11... | collective-permute-start | bytes 2359304 | tf_op jit(solution)/shard_map/ppermute | solution.py:41
  39.0 4.2 %collective-permute-start.12 = (bf16[8,64,768]{2,1,0:T(8,128)(2,1)S(1)}, bf16[8,64,768]{2,1,0:T(8,128)(2,1)S(1)}, u32[]{:S(2)}, u32[]{:S(2)}) collective-permute-start(bf16[8,64,768]{2,1,0:T(8,128)(2,1)S(1)} %collective-permute-done.8.source.refs_1_), channel_id=1, source_target_pairs={{0,1},{1,0},{2,3},{3,2},{4,5},{5,4},{6,7},{7,6},{8,9},{9,8},{10,11... | collective-permute-start | bytes 2359304 | tf_op jit(solution)/shard_map/ppermute | solution.py:41
  39.4 3.7 %collective-permute-start.5 = (bf16[2,2,17,32,128]{4,3,2,1,0:T(8,128)(2,1)S(1)}, bf16[2,2,17,32,128]{4,3,2,1,0:T(8,128)(2,1)S(1)}, u32[]{:S(2)}, u32[]{:S(2)}) collective-permute-start(bf16[2,2,17,32,128]{4,3,2,1,0:T(8,128)(2,1)S(1)} %get-tuple-element.67.refs_4_), channel_id=1, source_target_pairs={{0,1},{1,0},{2,3},{3,2},{4,5},{5,4},{6,7},{7,6},{8,9},{9,8},{10,11... | collective-permute-start | bytes 1671176 | tf_op jit(solution)/shard_map/ppermute | solution.py:41
  39.9 11.5 %collective-permute-start.10 = (bf16[4,64,768]{2,1,0:T(8,128)(2,1)S(1)}, bf16[4,64,768]{2,1,0:T(8,128)(2,1)S(1)}, u32[]{:S(2)}, u32[]{:S(2)}) collective-permute-start(bf16[4,64,768]{2,1,0:T(8,128)(2,1)S(1)} %take.3), channel_id=1, source_target_pairs={{0,96},{1,13},{2,98},{3,15},{4,100},{5,1},{6,102},{7,3},{8,104},{9... | collective-permute-start | bytes 1179656 | tf_op jit(solution)/shard_map/ppermute | solution.py:41
  42.3 9.2 %collective-permute-start.9 = (bf16[4,64,768]{2,1,0:T(8,128)(2,1)S(1)}, bf16[4,64,768]{2,1,0:T(8,128)(2,1)S(1)}, u32[]{:S(2)}, u32[]{:S(2)}) collective-permute-start(bf16[4,64,768]{2,1,0:T(8,128)(2,1)S(1)} %take.2), channel_id=1, source_target_pairs={{0,32},{1,5},{2,34},{3,7},{4,36},{5,9},{6,38},{7,11},{8,40},{9,13}... | collective-permute-start | bytes 1179656 | tf_op jit(solution)/shard_map/ppermute | solution.py:41
  63.1 10.3 %collective-permute-start.16 = (bf16[17,32,256]{2,1,0:T(8,128)(2,1)S(1)}, bf16[17,32,256]{2,1,0:T(8,128)(2,1)S(1)}, u32[]{:S(2)}, u32[]{:S(2)}) collective-permute-start(bf16[17,32,256]{2,1,0:T(8,128)(2,1)S(1)} %add_convert_fusion), channel_id=1, source_target_pairs={{0,2},{1,3},{2,0},{3,1},{4,6},{5,7},{6,4},{7,5},{8,10},{9,11},{10,... | collective-permute-start | bytes 835592 | tf_op jit(solution)/shard_map/ppermute | solution.py:41
  83.0 2.7 %collective-permute-start.18 = (f32[64,32,128]{2,1,0:T(8,128)S(1)}, f32[64,32,128]{2,1,0:T(8,128)S(1)}, u32[]{:S(2)}, u32[]{:S(2)}) collective-permute-start(f32[64,32,128]{2,1,0:T(8,128)S(1)} %get-tuple-element.55), channel_id=1, source_target_pairs={{0,1},{1,0},{2,3},{3,2},{4,5},{5,4},{6,7},{7,6},{8,9},{9,8},{10,11... | collective-permute-start | bytes 3145736 | tf_op jit(solution)/shard_map/ppermute | solution.py:41
  86.0 11.7 %collective-permute-start.19 = (f32[4,4,32,128]{3,2,1,0:T(8,128)S(1)}, f32[4,4,32,128]{3,2,1,0:T(8,128)S(1)}, u32[]{:S(2)}, u32[]{:S(2)}) collective-permute-start(f32[4,4,32,128]{3,2,1,0:T(8,128)S(1)} %bitcast.66), channel_id=1, source_target_pairs={{0,4},{1,33},{2,6},{3,35},{4,8},{5,37},{6,10},{7,39},{8,12},{9,41}... | collective-permute-start | bytes 786440 | tf_op jit(solution)/shard_map/ppermute | solution.py:41
  87.6 10.0 %collective-permute-start.20 = (f32[4,4,32,128]{3,2,1,0:T(8,128)S(1)}, f32[4,4,32,128]{3,2,1,0:T(8,128)S(1)}, u32[]{:S(2)}, u32[]{:S(2)}) collective-permute-start(f32[4,4,32,128]{3,2,1,0:T(8,128)S(1)} %bitcast.65), channel_id=1, source_target_pairs={{0,12},{1,97},{2,14},{3,99},{4,0},{5,101},{6,2},{7,103},{8,4},{9,1... | collective-permute-start | bytes 786440 | tf_op jit(solution)/shard_map/ppermute | solution.py:41
  90.2 8.5 %collective-permute-start.21 = (f32[4,4,32,128]{3,2,1,0:T(8,128)S(1)}, f32[4,4,32,128]{3,2,1,0:T(8,128)S(1)}, u32[]{:S(2)}, u32[]{:S(2)}) collective-permute-start(f32[4,4,32,128]{3,2,1,0:T(8,128)S(1)} %bitcast.64), channel_id=1, source_target_pairs={{0,8},{1,65},{2,10},{3,67},{4,12},{5,69},{6,14},{7,71},{8,0},{9,73... | collective-permute-start | bytes 786440 | tf_op jit(solution)/shard_map/ppermute | solution.py:41
  98.8 5.5 %collective-permute-start.22 = (f32[4,32,128]{2,1,0:T(8,128)S(1)}, f32[4,32,128]{2,1,0:T(8,128)S(1)}, u32[]{:S(2)}, u32[]{:S(2)}) collective-permute-start(f32[4,32,128]{2,1,0:T(8,128)S(1)} %get-tuple-element.75), channel_id=1, source_target_pairs={{0,32},{1,5},{2,34},{3,7},{4,36},{5,9},{6,38},{7,11},{8,40},{9,13}... | collective-permute-start | bytes 196616 | tf_op jit(solution)/shard_map/ppermute | solution.py:41
  99.7 4.6 %collective-permute-start.23 = (f32[4,32,128]{2,1,0:T(8,128)S(1)}, f32[4,32,128]{2,1,0:T(8,128)S(1)}, u32[]{:S(2)}, u32[]{:S(2)}) collective-permute-start(f32[4,32,128]{2,1,0:T(8,128)S(1)} %get-tuple-element.77), channel_id=1, source_target_pairs={{0,96},{1,13},{2,98},{3,15},{4,100},{5,1},{6,102},{7,3},{8,104},{9... | collective-permute-start | bytes 196616 | tf_op jit(solution)/shard_map/ppermute | solution.py:41
  102.1 5.8 %collective-permute-start.24 = (f32[4,32,128]{2,1,0:T(8,128)S(1)}, f32[4,32,128]{2,1,0:T(8,128)S(1)}, u32[]{:S(2)}, u32[]{:S(2)}) collective-permute-start(f32[4,32,128]{2,1,0:T(8,128)S(1)} %get-tuple-element.76), channel_id=1, source_target_pairs={{0,64},{1,9},{2,66},{3,11},{4,68},{5,13},{6,70},{7,15},{8,72},{9,1... | collective-permute-start | bytes 196616 | tf_op jit(solution)/shard_map/ppermute | solution.py:41
  107.9 5.0 %collective-permute-start.25 = (f32[32,128]{1,0:T(8,128)S(1)}, f32[32,128]{1,0:T(8,128)S(1)}, u32[]{:S(2)}, u32[]{:S(2)}) collective-permute-start(f32[32,128]{1,0:T(8,128)S(1)} %get-tuple-element.78), channel_id=1, source_target_pairs={{0,16},{1,17},{2,18},{3,19},{4,20},{5,21},{6,22},{7,23},{8,24},{9,... | collective-permute-start | bytes 49160 | tf_op jit(solution)/shard_map/ppermute | solution.py:41
  108.1 4.8 %collective-permute-start.26 = (f32[32,128]{1,0:T(8,128)S(1)}, f32[32,128]{1,0:T(8,128)S(1)}, u32[]{:S(2)}, u32[]{:S(2)}) collective-permute-start(f32[32,128]{1,0:T(8,128)S(1)} %get-tuple-element.80), channel_id=1, source_target_pairs={{0,18},{1,19},{2,16},{3,17},{4,22},{5,23},{6,20},{7,21},{8,26},{9,... | collective-permute-start | bytes 49160 | tf_op jit(solution)/shard_map/ppermute | solution.py:41
  111.2 5.2 %collective-permute-start.27 = (f32[32,128]{1,0:T(8,128)S(1)}, f32[32,128]{1,0:T(8,128)S(1)}, u32[]{:S(2)}, u32[]{:S(2)}) collective-permute-start(f32[32,128]{1,0:T(8,128)S(1)} %get-tuple-element.79), channel_id=1, source_target_pairs={{0,2},{1,3},{2,0},{3,1},{4,6},{5,7},{6,4},{7,5},{8,10},{9,11},{10,... | collective-permute-start | bytes 49160 | tf_op jit(solution)/shard_map/ppermute | solution.py:41
  (9 other events, 21.5 us)
